TPU v7x, 32 devices: a whole 2x2x4 slice. The times are simulated.
32 devices in a mesh: wide: 8 (over z, x), narrow: 4 (over y, core).
Axes of the slice: x: 2, y: 2, z: 4, core: 2. Of those that a mesh axis runs over, the one named last changes fastest.
Arguments:
- recording: bfloat16 [32768, 512], P(('wide', 'narrow')), may hold values from -6 to 6
- conv_weight: bfloat16 [3, 3, 512, 512], replicated, may hold values from -0.15625 to 0.15625
- conv_bias: float32 [3, 512], replicated, may hold values from -3 to 3
- projection: bfloat16 [512, 64], replicated, may hold values from -0.25 to 0.25
Outputs:
- path_points: bfloat16 [32768, 64], P(('wide', 'narrow'))
- level_one: float32 [8, 64], P('wide')
- level_two: float32 [8, 4096], P('wide')
- level_three: float32 [8, 64, 4096], P('wide', 'narrow')
All inputs are finite; a program needn't handle non-finite values.
Results may differ from a plain program's by a relative error of at most 0.0075.
Values may be sent and summed in bfloat16 or wider, within the bound.
No kernel may reach another device: no remote copies, remote signals or barrier semaphores. Data moves between devices by JAX's collectives and lax.ppermute only.
A program may use at most 64 MiB of HBM per device.

v0:
```python
import jax
import jax.numpy as jnp
from jax import lax
from jax.sharding import PartitionSpec as P

PRECISE = lax.Precision.HIGHEST


def padded_2(array, sides, width):
    for axis, dim in sides:
        size, length = (lax.axis_size(axis), array.shape[dim])
        up = [(i, (i + 1) % size) for i in range(size - 1)]
        down = [(j, i) for i, j in up]
        last = lax.slice_in_dim(array, length - width, length, axis=dim)
        first = lax.slice_in_dim(array, 0, width, axis=dim)
        before = lax.ppermute(last, axis, up)
        after = lax.ppermute(first, axis, down)
        array = jnp.concatenate([before, array, after], axis=dim)
    return array


def from_behind(array, axis, by):
    size = lax.axis_size(axis)
    pairs = [(i, i + by) for i in range(size) if 0 <= i + by < size]
    return lax.ppermute(array, axis, pairs)


def prefix(array, axis, combine, identity):
    size, index = (lax.axis_size(axis), lax.axis_index(axis))
    everything = jax.tree.map(lambda part: lax.all_gather(part, axis), array)
    start = jax.tree.map(
        lambda part, zero: jnp.broadcast_to(jnp.asarray(zero, part.dtype), part.shape),
        array,
        identity,
    )

    def hop(k, before):
        reached = k < index
        new = combine(before, jax.tree.map(lambda part: part[k], everything))
        return jax.tree.map(lambda a, b: jnp.where(reached, a, b), new, before)

    return lax.fori_loop(0, size, hop, start)


def apply_taps(padded, weights, layer_bias, dilation, length):
    totals = layer_bias[None, :]
    for tap_idx in range(3):
        window = padded[tap_idx * dilation : tap_idx * dilation + length]
        totals = totals + jnp.dot(window, weights[tap_idx], preferred_element_type=jnp.float32)
    return totals


def sig_update(signature, increments, row_count):
    first_level, second_level, third_level = signature
    path_width = increments.shape[1]
    step_count = increments.shape[0]
    running = jnp.cumsum(increments, axis=0)
    totals = running[-1]
    before = first_level[None, :] + running - increments
    remaining = totals[None, :] - running
    second_terms = ((before + 0.5 * increments)[:, :, None] * increments[:, None, :]).reshape(
        step_count, row_count * path_width
    )
    third_terms = ((0.5 * before + increments / 6.0)[:, :, None] * increments[:, None, :]).reshape(
        step_count, row_count * path_width
    )
    gained = jnp.einsum("nm,nk->mk", second_terms, remaining, precision=PRECISE)
    gained = gained + jnp.einsum("nm,nk->mk", third_terms, increments, precision=PRECISE)
    second_rows = second_level
    carried = (second_rows[:, :, None] * totals[None, None, :]).reshape(
        row_count, path_width * path_width
    )
    third_level = third_level + carried + gained.reshape(row_count, path_width * path_width)
    second_level = second_level + jnp.einsum("ni,nj->ij", before, increments, precision=PRECISE)
    second_level = second_level + 0.5 * jnp.einsum(
        "ni,nj->ij", increments, increments, precision=PRECISE
    )
    first_level = first_level + totals
    return (first_level, second_level, third_level)


def chen(earlier, later, row_start, row_count):
    first_a, second_a, third_a = earlier
    first_b, second_b, third_b = later
    first_level = first_a + first_b
    second_level = second_a + second_b + first_a[:, None] * first_b[None, :]
    first_rows = lax.dynamic_slice_in_dim(first_a, row_start, row_count, 0)
    second_rows = lax.dynamic_slice_in_dim(second_a, row_start, row_count, 0)
    mixed = first_rows[:, None] * second_b.reshape(1, -1)
    mixed = mixed + (second_rows[:, :, None] * first_b[None, None, :]).reshape(row_count, -1)
    return (first_level, second_level, third_a + third_b + mixed)


def per_device(recording, conv_weight, conv_bias, projection):
    shard_len = recording.shape[0]
    layers = conv_weight.shape[0]
    path_width = projection.shape[1]
    narrow_size = lax.axis_size("narrow")
    total_steps = shard_len * lax.axis_size("wide") * narrow_size
    hidden = recording
    for layer_idx in range(layers):
        dilation = 2**layer_idx
        padded = padded_2(hidden, ((("wide", "narrow"), 0),), dilation)
        totals = apply_taps(
            padded, conv_weight[layer_idx], conv_bias[layer_idx], dilation, shard_len
        )
        hidden = (hidden.astype(jnp.float32) + jax.nn.silu(totals)).astype(jnp.bfloat16)
    path_points = jnp.dot(hidden, projection, preferred_element_type=jnp.float32).astype(
        jnp.bfloat16
    )
    step_scale = total_steps ** (-0.2)
    row_count = path_width // narrow_size
    row_start = lax.axis_index("narrow") * row_count
    empty_state = (
        jnp.zeros((path_width,), jnp.float32),
        jnp.zeros((path_width, path_width), jnp.float32),
        jnp.zeros((row_count, path_width * path_width), jnp.float32),
    )

    def combine(earlier, later):
        return chen(earlier, later, row_start, row_count)

    previous = from_behind(path_points[-1:], ("wide", "narrow"), 1)
    own_points = jnp.concatenate([previous, path_points], axis=0).astype(jnp.float32)
    own_steps = (own_points[1:] - own_points[:-1]) * step_scale
    quarters = own_steps.reshape(4, shard_len // 4, path_width)
    whole_empty = (
        empty_state[0],
        empty_state[1],
        jnp.zeros((path_width, path_width * path_width), jnp.float32),
    )

    def whole_step(signature, piece):
        return (sig_update(signature, piece, path_width), None)

    partial_sig, unused = lax.scan(whole_step, whole_empty, quarters)
    third_parts = lax.all_to_all(
        partial_sig[2].reshape(1, path_width, path_width * path_width).astype(jnp.bfloat16),
        "narrow",
        split_axis=1,
        concat_axis=0,
        tiled=True,
    ).astype(jnp.float32)
    first_parts, second_parts = (
        lax.all_gather(partial_sig[0][None], "narrow", axis=0, tiled=True),
        lax.all_gather(partial_sig[1][None], "narrow", axis=0, tiled=True),
    )

    def fold_step(signature, element):
        return (combine(signature, element), None)

    signature, unused = lax.scan(fold_step, empty_state, (first_parts, second_parts, third_parts))
    preceding = prefix(signature, "wide", combine, empty_state)
    result = combine(preceding, signature)
    return (
        path_points,
        result[0][None],
        result[1].reshape(1, path_width * path_width),
        result[2][None],
    )


def solution(mesh):
    return jax.shard_map(
        per_device,
        mesh=mesh,
        in_specs=(P(("wide", "narrow"), None), P(), P(), P()),
        out_specs=(
            P(("wide", "narrow"), None),
            P("wide", None),
            P("wide", None),
            P("wide", "narrow", None),
        ),
        check_vma=False,
    )
```

profile of v0, /device:TPU:0, one launch (start us, length us, event | category | flops | bytes accessed | tf_op | source)
XLA Modules:
  0.0 238.4 jit_solution(4955220168358620782)
XLA Ops:
  8.0 2.3 collective-permute-start
  10.4 1.3 collective-permute-start.1
  11.7 2.1 fusion.38
  13.8 1.9 fusion.24
  15.8 2.4 %add_convert_fusion.2 = bf16[1024,512]{1,0:T(8,128)(2,1)S(1)} fusion(f32[1024,512]{1,0:T(8,128)S(1)} %fusion.38, f32[1024,512]{1,0:T(8,128)S(1)} %fusion.24, bf16[1024,512]{1,0:T(8,128)(2,1)S(1)} %copy-done.3, bf16[1,512]{1,0:T(2,128)(2,1)S(1)} %collective-permute-done.1, f32[512]{0:T(512)S(1)} %bitcast.203, bf16[3,3,512,512]{3,2,1,0:T(8,128)(2,1)} %param.11), kind=kOutput, calls=%fused_computation.50 | convolution fusion | flops 544210944 | bytes 7868416 | tf_op jit(solution)/shard_map/dot_general | solution.py:49
  18.2 5.2 %collective-permute-start.2 = (bf16[2,512]{1,0:T(2,128)(2,1)S(1)}, bf16[2,512]{1,0:T(2,128)(2,1)S(1)}, u32[]{:S(2)}, u32[]{:S(2)}) collective-permute-start(bf16[2,512]{1,0:T(2,128)(2,1)S(1)} %get-tuple-element.523), channel_id=1, source_target_pairs={{0,1},{1,2},{2,3},{3,4},{4,5},{5,6},{6,7},{7,8},{8,9},{9,10},{10,1... | collective-permute-start | bytes 6152 | tf_op jit(solution)/shard_map/ppermute | solution.py:16
  24.1 1.3 collective-permute-start.3
  26.1 2.3 collective-permute-done.3
  28.4 1.3 add_convert_fusion.1
  29.7 4.3 %collective-permute-start.4 = (bf16[4,512]{1,0:T(4,128)(2,1)S(1)}, bf16[4,512]{1,0:T(4,128)(2,1)S(1)}, u32[]{:S(2)}, u32[]{:S(2)}) collective-permute-start(bf16[4,512]{1,0:T(4,128)(2,1)S(1)} %get-tuple-element.521), channel_id=1, source_target_pairs={{0,1},{1,2},{2,3},{3,4},{4,5},{5,6},{6,7},{7,8},{8,9},{9,10},{10,1... | collective-permute-start | bytes 12296 | tf_op jit(solution)/shard_map/ppermute | solution.py:16
  34.7 1.3 collective-permute-start.5
  36.0 2.0 fusion.18
  38.0 3.2 %fusion.15 = bf16[1024,64]{0,1:T(8,128)(2,1)S(1)} fusion(bf16[512,64]{0,1:T(8,128)(2,1)S(1)} %copy-done, f32[1024,512]{1,0:T(8,128)S(1)} %fusion.30, f32[1024,512]{1,0:T(8,128)} %fusion.18, bf16[1024,512]{1,0:T(8,128)(2,1)S(1)} %add_convert_fusion.1, bf16[4,512]{1,0:T(4,128)(2,1)S(1)} %collective-permute-done.5, f32[512]{0:T(512)S(1)} %bitcast.201, ...), kind=kOutput, calls=%fused_computation.52 | convolution fusion | flops 611385344 | bytes 7018496 | tf_op jit(solution)/shard_map/dot_general | solution.py:108
  41.3 5.3 %collective-permute-start.6 = (bf16[1,64]{0,1:T(8,128)(2,1)S(1)}, bf16[1,64]{0,1:T(8,128)(2,1)S(1)}, u32[]{:S(2)}, u32[]{:S(2)}) collective-permute-start(bf16[1,64]{0,1:T(8,128)(2,1)S(1)} %slice.153), channel_id=1, source_target_pairs={{0,1},{1,2},{2,3},{3,4},{4,5},{5,6},{6,7},{7,8},{8,9},{9,10},{10,1... | collective-permute-start | bytes 392 | tf_op jit(solution)/shard_map/ppermute | solution.py:25
  48.3 74.6 %while.52 = (s32[]{:T(128)}, f32[64]{0:T(128)S(1)}, f32[64,64]{1,0:T(8,128)S(1)}, f32[64,4096]{1,0:T(8,128)}, f32[4,256,64]{1,0,2:T(4,128)}, /*index=5*/s32[]{:T(128)}, f32[]{:T(128)}, s32[]{:T(128)}) while((s32[]{:T(128)}, f32[64]{0:T(128)S(1)}, f32[64,64]{1,0:T(8,128)S(1)}, f32[64,4096]{1,0:T(8,128)}, f32[4,256,64]{1,0,2:T(4,128)}, ...), condition=%wide.region_3.4_spmd.clone, body=%wide.region_0.3_spmd.clone.sunk | while | flops 1641513216 | bytes 33087340 | solution.py:136
  50.6 1.2 broadcast_multiply_fusion.3
  51.8 4.2 %fusion.91 = f32[4096,64]{0,1:T(8,128)S(1)} fusion(f32[256,4096]{0,1:T(8,128)S(1)} %bitcast.189, f32[64]{0:T(128)S(1)} %slice_reduce_fusion.5, f32[64,2,128]{2,0,1:T(8,128)S(1)} %reduce-window.14, f32[64,2]{0,1:T(2,128)S(1)} %slice.213), kind=kOutput, calls=%fused_computation.35.clone.1 | convolution fusion | flops 805339136 | bytes 5309184 | tf_op jit(solution)/shard_map/while/body/eval_jaxpr/nm,nk->mk/dot_general | solution.py:67
  56.0 4.2 %convolution_add_fusion.5 = f32[4096,64]{0,1:T(8,128)S(1)} fusion(f32[4096,64]{0,1:T(8,128)S(1)} %fusion.91, f32[256,4096]{0,1:T(8,128)S(1)} %bitcast.188, f32[1,256,64]{1,0,2:T(1,128)S(1)} %constant_dynamic-slice_fusion.13), kind=kOutput, calls=%fused_computation.23.clone.1 | convolution fusion | flops 805568512 | bytes 6356992 | tf_op jit(solution)/shard_map/while/body/eval_jaxpr/nm,nk->mk/dot_general | solution.py:68
  62.2 1.6 mul.471
  63.8 2.4 fusion.92
  68.9 1.2 broadcast_multiply_fusion.3
  70.2 4.2 %fusion.91 = f32[4096,64]{0,1:T(8,128)S(1)} fusion(f32[256,4096]{0,1:T(8,128)S(1)} %bitcast.189, f32[64]{0:T(128)S(1)} %slice_reduce_fusion.5, f32[64,2,128]{2,0,1:T(8,128)S(1)} %reduce-window.14, f32[64,2]{0,1:T(2,128)S(1)} %slice.213), kind=kOutput, calls=%fused_computation.35.clone.1 | convolution fusion | flops 805339136 | bytes 5309184 | tf_op jit(solution)/shard_map/while/body/eval_jaxpr/nm,nk->mk/dot_general | solution.py:67
  74.4 4.2 %convolution_add_fusion.5 = f32[4096,64]{0,1:T(8,128)S(1)} fusion(f32[4096,64]{0,1:T(8,128)S(1)} %fusion.91, f32[256,4096]{0,1:T(8,128)S(1)} %bitcast.188, f32[1,256,64]{1,0,2:T(1,128)S(1)} %constant_dynamic-slice_fusion.13), kind=kOutput, calls=%fused_computation.23.clone.1 | convolution fusion | flops 805568512 | bytes 6356992 | tf_op jit(solution)/shard_map/while/body/eval_jaxpr/nm,nk->mk/dot_general | solution.py:68
  80.5 1.6 mul.471
  82.2 2.7 %fusion.92 = f32[64,4096]{1,0:T(8,128)} fusion(f32[64,4096]{1,0:T(8,128)S(1)} %reshape.148, f32[64,4096]{1,0:T(8,128)} %get-tuple-element.713, f32[64,4096]{1,0:T(8,128)} %mul.471, f32[4096]{0:T(1024)S(1)} %mul.473, pred[]{:T(512)S(6)} %compare.9), kind=kLoop, calls=%fused_computation.30.clone.1 | loop fusion | flops 1048576 | bytes 4210689 | tf_op jit(solution)/shard_map/while/body/eval_jaxpr/add | solution.py:73
  87.6 1.2 broadcast_multiply_fusion.3
  88.8 4.2 %fusion.91 = f32[4096,64]{0,1:T(8,128)S(1)} fusion(f32[256,4096]{0,1:T(8,128)S(1)} %bitcast.189, f32[64]{0:T(128)S(1)} %slice_reduce_fusion.5, f32[64,2,128]{2,0,1:T(8,128)S(1)} %reduce-window.14, f32[64,2]{0,1:T(2,128)S(1)} %slice.213), kind=kOutput, calls=%fused_computation.35.clone.1 | convolution fusion | flops 805339136 | bytes 5309184 | tf_op jit(solution)/shard_map/while/body/eval_jaxpr/nm,nk->mk/dot_general | solution.py:67
  93.0 4.2 %convolution_add_fusion.5 = f32[4096,64]{0,1:T(8,128)S(1)} fusion(f32[4096,64]{0,1:T(8,128)S(1)} %fusion.91, f32[256,4096]{0,1:T(8,128)S(1)} %bitcast.188, f32[1,256,64]{1,0,2:T(1,128)S(1)} %constant_dynamic-slice_fusion.13), kind=kOutput, calls=%fused_computation.23.clone.1 | convolution fusion | flops 805568512 | bytes 6356992 | tf_op jit(solution)/shard_map/while/body/eval_jaxpr/nm,nk->mk/dot_general | solution.py:68
  99.2 1.6 mul.471
  100.8 2.7 %fusion.92 = f32[64,4096]{1,0:T(8,128)} fusion(f32[64,4096]{1,0:T(8,128)S(1)} %reshape.148, f32[64,4096]{1,0:T(8,128)} %get-tuple-element.713, f32[64,4096]{1,0:T(8,128)} %mul.471, f32[4096]{0:T(1024)S(1)} %mul.473, pred[]{:T(512)S(6)} %compare.9), kind=kLoop, calls=%fused_computation.30.clone.1 | loop fusion | flops 1048576 | bytes 4210689 | tf_op jit(solution)/shard_map/while/body/eval_jaxpr/add | solution.py:73
  106.3 1.2 broadcast_multiply_fusion.3
  107.5 4.2 %fusion.91 = f32[4096,64]{0,1:T(8,128)S(1)} fusion(f32[256,4096]{0,1:T(8,128)S(1)} %bitcast.189, f32[64]{0:T(128)S(1)} %slice_reduce_fusion.5, f32[64,2,128]{2,0,1:T(8,128)S(1)} %reduce-window.14, f32[64,2]{0,1:T(2,128)S(1)} %slice.213), kind=kOutput, calls=%fused_computation.35.clone.1 | convolution fusion | flops 805339136 | bytes 5309184 | tf_op jit(solution)/shard_map/while/body/eval_jaxpr/nm,nk->mk/dot_general | solution.py:67
  111.7 4.2 %convolution_add_fusion.5 = f32[4096,64]{0,1:T(8,128)S(1)} fusion(f32[4096,64]{0,1:T(8,128)S(1)} %fusion.91, f32[256,4096]{0,1:T(8,128)S(1)} %bitcast.188, f32[1,256,64]{1,0,2:T(1,128)S(1)} %constant_dynamic-slice_fusion.13), kind=kOutput, calls=%fused_computation.23.clone.1 | convolution fusion | flops 805568512 | bytes 6356992 | tf_op jit(solution)/shard_map/while/body/eval_jaxpr/nm,nk->mk/dot_general | solution.py:68
  117.9 1.6 mul.471
  119.5 2.7 %fusion.92 = f32[64,4096]{1,0:T(8,128)} fusion(f32[64,4096]{1,0:T(8,128)S(1)} %reshape.148, f32[64,4096]{1,0:T(8,128)} %get-tuple-element.713, f32[64,4096]{1,0:T(8,128)} %mul.471, f32[4096]{0:T(1024)S(1)} %mul.473, pred[]{:T(512)S(6)} %compare.9), kind=kLoop, calls=%fused_computation.30.clone.1 | loop fusion | flops 1048576 | bytes 4210689 | tf_op jit(solution)/shard_map/while/body/eval_jaxpr/add | solution.py:73
  122.9 1.3 convert_bitcast_fusion
  124.2 1.2 copy.57
  125.9 3.8 %reduce.4 = bf16[64,4096]{1,0:T(8,128)(2,1)S(1)} reduce(bf16[64,1,4096]{2,1,0:T(2,128)(2,1)S(1)} %bitcast.194, bf16[]{:T(256)} %broadcast.154), dimensions={1}, to_apply=%bitcast.133.reduce_sub_computation | reduce | bytes 1048578
  129.7 1.2 reshape.145
  130.8 4.3 %all-to-all-start = ((bf16[4,2,32768]{2,1,0:T(2,128)(2,1)}), bf16[4,2,32768]{2,1,0:T(2,128)(2,1)S(1)}, u32[]{:S(2)}, u32[]{:S(2)}) async-start(bf16[4,2,32768]{2,1,0:T(2,128)(2,1)} %reshape.145), calls=%async_computation | async-start | bytes 1048576 | tf_op jit(solution)/shard_map/all_to_all | solution.py:137
  136.7 8.8 %all-reduce = f32[256]{0:T(256)S(1)} all-reduce(f32[256]{0:T(256)S(1)} %dynamic-update-slice), channel_id=2, replica_groups=mesh['wide'=8,'narrow'=4] {'narrow'}, use_global_device_ids=true, to_apply=%add | all-reduce | flops 256 | bytes 2048
  145.5 5.6 %all-gather.1 = f32[256,64]{1,0:T(8,128)S(1)} all-gather(f32[64,64]{1,0:T(8,128)S(1)} %get-tuple-element.348), channel_id=3, replica_groups=mesh['wide'=8,'narrow'=4] {'narrow'}, dimensions={0}, use_global_device_ids=true | all-gather | bytes 81920 | tf_op jit(solution)/shard_map/all_gather | solution.py:146
  152.2 3.4 %while.53 = (s32[]{:T(128)}, f32[64]{0:T(128)S(1)}, f32[64,64]{1,0:T(8,128)S(1)}, f32[16,4096]{1,0:T(8,128)S(1)}, f32[4,64]{1,0:T(4,128)S(1)}, /*index=5*/f32[4,...) while((s32[]{:T(128)}, f32[64]{0:T(128)S(1)}, ...), condition=%wide.region_5.6_spmd.clone, body=%wide.region_4.5_spmd.clone.sunk | while | flops 409731 | bytes 2046277 | solution.py:152
  157.9 24.3 %all-reduce.1 = f32[512]{0:T(512)S(1)} all-reduce(f32[512]{0:T(512)S(1)} %dynamic-update-slice.1), channel_id=4, replica_groups=mesh['wide'=8,'narrow'=4] {'wide'}, use_global_device_ids=true, to_apply=%add.1 | all-reduce | flops 512 | bytes 4096
  182.4 31.8 %all-gather.3 = f32[512,64]{1,0:T(8,128)S(1)} all-gather(f32[64,64]{1,0:T(8,128)S(1)} %get-tuple-element.351), channel_id=5, replica_groups=mesh['wide'=8,'narrow'=4] {'wide'}, dimensions={0}, use_global_device_ids=true | all-gather | bytes 147456 | tf_op jit(solution)/shard_map/all_gather | solution.py:30
  214.5 14.4 %while.54 = (s32[]{:T(128)}, f32[64]{0:T(128)S(1)}, f32[64,64]{1,0:T(8,128)S(1)}, f32[16,4096]{1,0:T(8,128)S(1)}, s32[]{:T(128)}, /*index=5*/f32[8,64]{1,0:T(8,1...) while((s32[]{:T(128)}, f32[64]{0:T(128)S(1)}, ...), condition=%wide.region_7.8_spmd.clone, body=%wide.region_6.7_spmd.clone.sunk | while | flops 479428 | bytes 2046297 | solution.py:42
  215.2 1.1 fusion.97
  217.0 1.1 fusion.97
  (267 shorter events, 45.8 us)
Async XLA Ops:
  7.2 30.9 %copy-start = (bf16[512,64]{0,1:T(8,128)(2,1)S(1)}, bf16[512,64]{0,1:T(8,128)(2,1)}, u32[]{:S(2)}) copy-start(bf16[512,64]{0,1:T(8,128)(2,1)} %param.13) | copy-start | bytes 196612
  7.2 6.6 %copy-start.3 = (bf16[1024,512]{1,0:T(8,128)(2,1)S(1)}, bf16[1024,512]{1,0:T(8,128)(2,1)}, u32[]{:S(2)}) copy-start(bf16[1024,512]{1,0:T(8,128)(2,1)} %param.10) | copy-start | bytes 3145732
  7.2 6.5 %copy-start.5 = (f32[3,512]{1,0:T(4,128)S(1)}, f32[3,512]{1,0:T(4,128)}, u32[]{:S(2)}) copy-start(f32[3,512]{1,0:T(4,128)} %param.12) | copy-start | bytes 18436
  8.0 5.8 %collective-permute-start = (bf16[1,512]{1,0:T(2,128)(2,1)S(1)}, bf16[1,512]{1,0:T(2,128)(2,1)S(1)}, u32[]{:S(2)}, u32[]{:S(2)}) collective-permute-start(bf16[1,512]{1,0:T(2,128)(2,1)S(1)} %get-tuple-element.525), channel_id=1, source_target_pairs={{0,1},{1,2},{2,3},{3,4},{4,5},{5,6},{6,7},{7,8},{8,9},{9,10},{10,1... | collective-permute-start | bytes 3080 | tf_op jit(solution)/shard_map/ppermute | solution.py:16
  10.4 5.4 %collective-permute-start.1 = (bf16[1,512]{1,0:T(2,128)(2,1)S(1)}, bf16[1,512]{1,0:T(2,128)(2,1)S(1)}, u32[]{:S(2)}, u32[]{:S(2)}) collective-permute-start(bf16[1,512]{1,0:T(2,128)(2,1)S(1)} %get-tuple-element.524), channel_id=1, source_target_pairs={{1,0},{2,1},{3,2},{4,3},{5,4},{6,5},{7,6},{8,7},{9,8},{10,9},{11,1... | collective-permute-start | bytes 3080 | tf_op jit(solution)/shard_map/ppermute | solution.py:17
  13.8 9.5 %slice-start = ((s8[4718592]{0:T(1024)(128)(4,1)}), s8[4194304]{0:T(1024)(128)(4,1)S(1)}, s32[]{:S(2)}) async-start(s8[4718592]{0:T(1024)(128)(4,1)} %bitcast.199), calls=%async_computation.2 | async-start | bytes 8388608
  15.7 7.6 %slice-start.1 = ((s8[4718592]{0:T(1024)(128)(4,1)}), s8[524288]{0:T(1024)(128)(4,1)S(1)}, s32[]{:S(2)}) async-start(s8[4718592]{0:T(1024)(128)(4,1)} %bitcast.199), calls=%async_computation.3 | async-start | bytes 1048576
  18.2 7.2 %collective-permute-start.2 = (bf16[2,512]{1,0:T(2,128)(2,1)S(1)}, bf16[2,512]{1,0:T(2,128)(2,1)S(1)}, u32[]{:S(2)}, u32[]{:S(2)}) collective-permute-start(bf16[2,512]{1,0:T(2,128)(2,1)S(1)} %get-tuple-element.523), channel_id=1, source_target_pairs={{0,1},{1,2},{2,3},{3,4},{4,5},{5,6},{6,7},{7,8},{8,9},{9,10},{10,1... | collective-permute-start | bytes 6152 | tf_op jit(solution)/shard_map/ppermute | solution.py:16
  24.1 4.3 %collective-permute-start.3 = (bf16[2,512]{1,0:T(2,128)(2,1)S(1)}, bf16[2,512]{1,0:T(2,128)(2,1)S(1)}, u32[]{:S(2)}, u32[]{:S(2)}) collective-permute-start(bf16[2,512]{1,0:T(2,128)(2,1)S(1)} %get-tuple-element.522), channel_id=1, source_target_pairs={{1,0},{2,1},{3,2},{4,3},{5,4},{6,5},{7,6},{8,7},{9,8},{10,9},{11,1... | collective-permute-start | bytes 6152 | tf_op jit(solution)/shard_map/ppermute | solution.py:17
  29.7 6.3 %collective-permute-start.4 = (bf16[4,512]{1,0:T(4,128)(2,1)S(1)}, bf16[4,512]{1,0:T(4,128)(2,1)S(1)}, u32[]{:S(2)}, u32[]{:S(2)}) collective-permute-start(bf16[4,512]{1,0:T(4,128)(2,1)S(1)} %get-tuple-element.521), channel_id=1, source_target_pairs={{0,1},{1,2},{2,3},{3,4},{4,5},{5,6},{6,7},{7,8},{8,9},{9,10},{10,1... | collective-permute-start | bytes 12296 | tf_op jit(solution)/shard_map/ppermute | solution.py:16
  34.7 3.4 %collective-permute-start.5 = (bf16[4,512]{1,0:T(4,128)(2,1)S(1)}, bf16[4,512]{1,0:T(4,128)(2,1)S(1)}, u32[]{:S(2)}, u32[]{:S(2)}) collective-permute-start(bf16[4,512]{1,0:T(4,128)(2,1)S(1)} %get-tuple-element.520), channel_id=1, source_target_pairs={{1,0},{2,1},{3,2},{4,3},{5,4},{6,5},{7,6},{8,7},{9,8},{10,9},{11,1... | collective-permute-start | bytes 12296 | tf_op jit(solution)/shard_map/ppermute | solution.py:17
  41.3 7.1 %copy-start.4 = (bf16[1024,64]{0,1:T(8,128)(2,1)}, bf16[1024,64]{0,1:T(8,128)(2,1)S(1)}, u32[]{:S(2)}) copy-start(bf16[1024,64]{0,1:T(8,128)(2,1)S(1)} %fusion.15) | copy-start | bytes 393220
  41.3 5.9 %collective-permute-start.6 = (bf16[1,64]{0,1:T(8,128)(2,1)S(1)}, bf16[1,64]{0,1:T(8,128)(2,1)S(1)}, u32[]{:S(2)}, u32[]{:S(2)}) collective-permute-start(bf16[1,64]{0,1:T(8,128)(2,1)S(1)} %slice.153), channel_id=1, source_target_pairs={{0,1},{1,2},{2,3},{3,4},{4,5},{5,6},{6,7},{7,8},{8,9},{9,10},{10,1... | collective-permute-start | bytes 392 | tf_op jit(solution)/shard_map/ppermute | solution.py:25
  125.3 9.8 %copy-start.7 = (u32[32]{0:T(128)S(1)}, u32[32]{0:T(128)}, u32[]{:S(2)}) copy-start(u32[32]{0:T(128)} %constant.107) | copy-start | bytes 388
  130.8 20.2 %all-to-all-start = ((bf16[4,2,32768]{2,1,0:T(2,128)(2,1)}), bf16[4,2,32768]{2,1,0:T(2,128)(2,1)S(1)}, u32[]{:S(2)}, u32[]{:S(2)}) async-start(bf16[4,2,32768]{2,1,0:T(2,128)(2,1)} %reshape.145), calls=%async_computation | async-start | bytes 1048576 | tf_op jit(solution)/shard_map/all_to_all | solution.py:137
  135.2 79.4 %all-gather.7.cloned.1.call-start = ((), (), s32[]{:S(2)}) async-start(), calls=%async_computation.1 | async-start | bytes 2359296 | tf_op jit(solution)/shard_map/all_gather | solution.py:30
  152.2 4.1 %copy-start.6 = (u32[32]{0:T(128)S(1)}, u32[32]{0:T(128)}, u32[]{:S(2)}) copy-start(u32[32]{0:T(128)} %constant.112) | copy-start | bytes 388
  155.6 0.7 copy-start.1
  214.5 16.2 %copy-start.2 = (f32[16,4096]{1,0:T(8,128)S(1)}, f32[16,4096]{1,0:T(8,128)}, u32[]{:S(2)}) copy-start(f32[16,4096]{1,0:T(8,128)} %copy-done.1) | copy-start | bytes 786436
Sparse Core Ops, SparseCore 0:
  156.5 58.0 all-gather.6
where the time goes:
time: 239 us; the launch traced here: 238 us
  blocking collectives  70.3 us (29%)
  matrix products  50.5 us (21%)
  local copies, waits for them, and re-layouts  36.6 us (15%)
  other arithmetic  35.5 us (15%)
  starting transfers between devices  25.2 us (11%)
  between operations  15.8 us (7%)
  waiting for transfers between devices  3.3 us (1%)
    unnamed x2, blocking collectives  33 us
    all_gather x1, blocking collectives, prefix(): everything = jax.tree.map(lambda part: lax.all_gather(part, axis), array)  31.8 us
    dot_general x4, matrix products, sig_update(): jnp.einsum('nm,nk->mk', third_terms, increments, precision=PRECISE)  16.9 us
    dot_general x4, matrix products, sig_update(): gained = jnp.einsum('nm,nk->mk', second_terms, remaining, precision=PRECISE)  16.7 us
    dot_general x8, matrix products, apply_taps(): jnp.dot(window, weights[tap_idx], preferred_element_type=jnp.float32)  11.8 us
    ppermute x3, starting transfers between devices, padded_2(): before = lax.ppermute(last, axis, up)  11.8 us
    add x4, other arithmetic, sig_update(): third_level + carried + gained.reshape(row_count, path_width * path_width)  10.4 us
    mul x16, local copies, waits for them, and re-layouts, sig_update(): second_rows[:, :, None] * totals[None, None, :]  9.29 us
  transfers between devices with their start and end apart: 9, of which 3 were waited for; matrix products, arithmetic and copies ran while one was open for 4% of the time, Pallas kernels for 0%

commit v1 on v0

v1 whole, which is shorter than its diff:
```python
import functools

import jax
import jax.numpy as jnp
from jax import lax
from jax.experimental import pallas as pl
from jax.experimental.pallas import tpu as pltpu
from jax.sharding import PartitionSpec as P

HALO = 16
LANES = 128
F32 = jnp.float32
BF16 = jnp.bfloat16
NT = (((1,), (1,)), ((), ()))
WHOLE = ("wide", "narrow")


def shifted(array, axis, by):
    size = lax.axis_size(axis)
    pairs = [(i, i + by) for i in range(size) if 0 <= i + by < size]
    return lax.ppermute(array, axis, pairs)


def exchanged(array, axis, distance):
    size = lax.axis_size(axis)
    return lax.ppermute(array, axis, [(i, i ^ distance) for i in range(size)])


def conv_kernel(chunk, rec, left, right, weights, bias, proj, points, piece, even, odd):
    layers = weights.shape[0]
    length = rec.shape[0]
    rows = length + 2 * HALO
    place = lax.axis_index("wide") * lax.axis_size("narrow") + lax.axis_index("narrow")
    last = lax.axis_size("wide") * lax.axis_size("narrow") - 1
    lower = jnp.where(place == 0, HALO, 0)
    upper = jnp.where(place == last, HALO + length, rows)
    even[8 : 8 + HALO, :] = left[...].astype(F32)
    even[8 + HALO : 8 + HALO + length, :] = rec[...].astype(F32)
    even[8 + HALO + length : 8 + rows, :] = right[...].astype(F32)
    source, target = even, odd
    for layer in range(layers):
        reach = 2**layer
        for start in range(0, rows, chunk):
            windows = [
                source[8 + start + k * reach : 8 + start + k * reach + chunk, :] for k in (-1, 0, 1)
            ]
            stacked = jnp.concatenate([window.astype(BF16) for window in windows], axis=1)
            conv = jnp.dot(stacked, weights[layer], preferred_element_type=F32)
            half = 0.5 * (conv + bias[layer : layer + 1, :])
            hidden = windows[1] + (half + half * jnp.tanh(half))
            hidden = hidden.astype(BF16).astype(F32)
            step = start + lax.broadcasted_iota(jnp.int32, (chunk, 1), 0)
            inside = jnp.logical_and(step >= lower, step < upper)
            target[8 + start : 8 + start + chunk, :] = jnp.where(inside, hidden, 0.0)
        source, target = target, source
    final = source[8 : 8 + rows, :].astype(BF16)
    path = lax.dot_general(proj[...], final, NT, preferred_element_type=F32)
    path = path.astype(BF16).astype(F32)
    width = piece.shape[1]
    path = jnp.concatenate([path, jnp.zeros((path.shape[0], width - rows), F32)], axis=1)
    points[...] = pltpu.roll(path, width - HALO, 1)[:, :length].astype(BF16)
    piece[...] = pltpu.roll(path, width - HALO + 1, 1).astype(BF16)


def sig_kernel(masks, row_count, *refs):
    pieces, (third, second, sent, ends), (diff, lead, rest, lhs) = (
        refs[: len(masks)],
        refs[len(masks) : len(masks) + 4],
        refs[len(masks) + 4 :],
    )
    width, padded = pieces[0].shape
    length = padded - LANES
    me = lax.axis_index("narrow")
    first_row = pl.multiple_of(me * row_count, row_count)
    group = max(1, 16 // row_count)
    half_rows = width // 2 * row_count
    sums = [jnp.zeros((half_rows, width), F32) for _ in range(2)]
    crossed = jnp.zeros((width, width), F32)
    lane = lax.broadcasted_iota(jnp.int32, (width, LANES), 1)
    end_points = jnp.zeros((width, LANES), F32)
    for mask, piece in zip(masks, pieces):
        wide_x = piece[...].astype(F32)
        after = pltpu.roll(wide_x, padded - 1, 1)[:, :length]
        before = pltpu.roll(wide_x, 1, 1)[:, :length]
        here = wide_x[:, :length]
        middle = 0.5 * (after + before)
        diff[...] = after - before
        lead[...] = 2.0 * here + middle
        rest[...] = middle - here
        here = piece[:, :length]
        crossed += lax.dot_general(after.astype(BF16), here, NT, preferred_element_type=F32)
        own_lead = lead[pl.ds(first_row, row_count), :]
        own_diff = diff[pl.ds(first_row, row_count), :]
        for h in range(2):
            for at in range(0, width // 2, group):
                terms = []
                for g in range(group):
                    j = 2 * (at + g) + h
                    terms.append(diff[j : j + 1, :] * own_lead + rest[j : j + 1, :] * own_diff)
                term = terms[0] if group == 1 else jnp.concatenate(terms, axis=0)
                lhs[h, at * row_count : (at + group) * row_count, :] = term.astype(BF16)
            sums[h] += lax.dot_general(lhs[h], here, NT, preferred_element_type=F32)
        is_last = jnp.bitwise_xor(me, mask) == lax.axis_size("narrow") - 1
        final = jnp.broadcast_to(wide_x[:, length : length + 1], (width, LANES))
        previous = jnp.broadcast_to(wide_x[:, length - 1 : length], (width, LANES))
        end_points = jnp.where(is_last, jnp.where(lane == 0, final, previous), end_points)
    total = jnp.concatenate(sums, axis=1)
    doubled = jnp.concatenate([crossed, crossed], axis=1)
    third[...] = total
    second[...] = doubled
    ends[...] = end_points
    pack(sent, total, doubled)


def pack(sent, total, doubled):
    count = total.shape[0]
    high = doubled.astype(BF16).astype(F32)
    lane = lax.broadcasted_iota(jnp.int32, doubled.shape, 1)
    sent[:count, :] = total.astype(BF16)
    sent[count:, :] = jnp.where(lane < LANES // 2, high, doubled - high).astype(BF16)


def unpack(received, count):
    coded = received[count:, :].astype(F32)
    return received[:count, :].astype(F32), coded + pltpu.roll(coded, LANES // 2, 1)


def add_kernel(third, second, received, new_third, new_second, sent):
    more_third, more_second = unpack(received, third.shape[0])
    total = third[...] + more_third
    doubled = second[...] + more_second
    new_third[...] = total
    new_second[...] = doubled
    pack(sent, total, doubled)


def final_kernel(scale, row_count, third, second, received, ends, level_one, level_two, level_three, held):
    width = second.shape[0]
    more_third, more_second = unpack(received, third.shape[0])
    crossed = (second[...] + more_second)[:, :width]
    end_cols = ends[...]
    end_rows = end_cols.T
    x_col, a_col = end_cols[:, 0:1], end_cols[:, 1:2]
    x_row, a_row = end_rows[0:1, :], end_rows[1:2, :]
    xx = x_col * x_row
    pairs = 0.5 * xx + 0.5 * (crossed.T - crossed)
    edge = a_col * x_row - a_col * a_row - 2.0 * x_col * a_row
    factor = pairs - edge / 6.0 - xx / 3.0
    level_one[...] = scale * x_row
    held[:, :width] = scale**2 * pairs
    level_two[:, :width] = held[pl.ds(0, width // 2, stride=2), :width]
    level_two[:, width:] = held[pl.ds(1, width // 2, stride=2), :width]
    held[:, :width] = scale**3 * factor
    first_row = pl.multiple_of(lax.axis_index("narrow") * row_count, row_count)
    own = held[pl.ds(first_row, row_count), :width]
    lane = lax.broadcasted_iota(jnp.int32, (row_count, LANES), 1)
    x_twice = jnp.concatenate([x_row, x_row], axis=1)
    total = (third[...] + more_third) * (scale**3 / 6.0)
    for at in range(width // 2):
        low = jnp.broadcast_to(own[:, 2 * at : 2 * at + 1], (row_count, LANES))
        high = jnp.broadcast_to(own[:, 2 * at + 1 : 2 * at + 2], (row_count, LANES))
        level_three[:, at * LANES : (at + 1) * LANES] = (
            jnp.where(lane < width, low, high) * x_twice
            - total[at * row_count : (at + 1) * row_count, :]
        )


def vmem(count):
    return [pl.BlockSpec(memory_space=pltpu.VMEM)] * count


def params():
    return pltpu.CompilerParams(vmem_limit_bytes=48 * 2**20)


def per_device(recording, conv_weight, conv_bias, projection):
    length, channels = recording.shape
    layers, taps = conv_weight.shape[:2]
    width = projection.shape[1]
    wide_size, narrow_size = lax.axis_size("wide"), lax.axis_size("narrow")
    scale = float(length * wide_size * narrow_size) ** -0.2
    row_count = width // narrow_size
    third_rows = width // 2 * row_count
    shape = jax.ShapeDtypeStruct

    left = shifted(recording[length - HALO :], WHOLE, 1)
    right = shifted(recording[:HALO], WHOLE, -1)
    rows = length + 2 * HALO
    points, piece = pl.pallas_call(
        functools.partial(conv_kernel, rows // 3),
        out_shape=(shape((width, length), BF16), shape((width, length + LANES), BF16)),
        in_specs=vmem(6),
        out_specs=tuple(vmem(2)),
        scratch_shapes=[pltpu.VMEM((rows + 16, channels), F32)] * 2,
        compiler_params=params(),
        name="conv",
    )(
        recording,
        left,
        right,
        conv_weight.reshape(layers, taps * channels, channels),
        conv_bias,
        projection.T,
    )

    masks, pieces = [0], [piece]
    distance = narrow_size // 2
    while distance:
        pieces = pieces + [exchanged(held, "narrow", distance) for held in pieces]
        masks = masks + [mask ^ distance for mask in masks]
        distance //= 2
    sums_shape = (
        shape((third_rows, LANES), F32),
        shape((width, LANES), F32),
        shape((third_rows + width, LANES), BF16),
    )
    third, second, sent, ends = pl.pallas_call(
        functools.partial(sig_kernel, masks, row_count),
        out_shape=sums_shape + (shape((width, LANES), F32),),
        in_specs=vmem(len(pieces)),
        out_specs=tuple(vmem(4)),
        scratch_shapes=[pltpu.VMEM((width, length), F32)] * 3 + [pltpu.VMEM((2, third_rows, length), BF16)],
        compiler_params=params(),
        name="block_sums",
    )(*pieces)

    distance = 1
    received = shifted(sent, "wide", distance)
    while 2 * distance < wide_size:
        distance *= 2
        third, second, sent = pl.pallas_call(
            add_kernel,
            out_shape=sums_shape,
            in_specs=vmem(3),
            out_specs=tuple(vmem(3)),
            compiler_params=params(),
            name="add",
        )(third, second, received)
        received = shifted(sent, "wide", distance)

    level_one, level_two, level_three = pl.pallas_call(
        functools.partial(final_kernel, scale, row_count),
        out_shape=(
            shape((1, width), F32),
            shape((width // 2, LANES), F32),
            shape((row_count, width * width), F32),
        ),
        in_specs=vmem(4),
        out_specs=tuple(vmem(3)),
        scratch_shapes=[pltpu.VMEM((width, LANES), F32)],
        compiler_params=params(),
        name="finish",
    )(third, second, received, ends)
    return points.T, level_one, level_two.reshape(1, width * width), level_three[None]


def solution(mesh):
    return jax.shard_map(
        per_device,
        mesh=mesh,
        in_specs=(P(WHOLE, None), P(), P(), P()),
        out_specs=(P(WHOLE, None), P("wide", None), P("wide", None), P("wide", "narrow", None)),
        check_vma=False,
    )
```

time: 239 us -> 61.9 us (0.26)
  the two profiles are of different devices: /device:TPU:0 before, /device:TPU:24 now
where the time goes in v1:
time: 61.9 us; the launch traced here: 61.4 us
  waiting for transfers between devices  32.4 us (52%)
  Pallas kernels  12.4 us (20%)
  starting transfers between devices  10.1 us (16%)
  local copies, waits for them, and re-layouts  5.84 us (9%)
  between operations  0.69 us (1%)
    ppermute x5, waiting for transfers between devices, shifted(): return lax.ppermute(array, axis, pairs)  25.9 us
    ppermute x5, starting transfers between devices, shifted(): return lax.ppermute(array, axis, pairs)  10.1 us
    pallas_call x1, Pallas kernels, per_device(): pl.pallas_call(functools.partial(conv_kernel, rows // 3), out_shape=(shap...  7.6 us
    ppermute x3, waiting for transfers between devices, exchanged(): return lax.ppermute(array, axis, [(i, i ^ distance) for i in range(size)])  6.5 us
    unnamed x8, local copies, waits for them, and re-layouts  5.1 us
    pallas_call x1, Pallas kernels, per_device(): pl.pallas_call(functools.partial(sig_kernel, masks, row_count), out_shape...  3.42 us
  transfers between devices with their start and end apart: 8, of which 6 were waited for; matrix products, arithmetic and copies ran while one was open for 0% of the time, Pallas kernels for 0%

profile of v1, /device:TPU:24, one launch (start us, length us, event | category | flops | bytes accessed | tf_op | source)
XLA Modules:
  0.0 61.4 jit_solution(14920198756025185827)
XLA Ops:
  0.6 0.7 %fusion = (bf16[16,512]{1,0:T(8,128)(2,1)S(1)}, bf16[16,512]{1,0:T(8,128)(2,1)S(1)}) fusion(bf16[1024,512]{1,0:T(8,128)(2,1)} %rec.1), kind=kLoop, calls=%fused_computation | loop fusion | bytes 65536 | tf_op jit(solution)/shard_map/slice | solution.py:187
  1.4 3.7 %collective-permute-start.1 = (bf16[16,512]{1,0:T(8,128)(2,1)S(1)}, bf16[16,512]{1,0:T(8,128)(2,1)S(1)}, u32[]{:S(2)}, u32[]{:S(2)}) collective-permute-start(bf16[16,512]{1,0:T(8,128)(2,1)S(1)} %get-tuple-element.34), channel_id=1, source_target_pairs={{1,0},{2,1},{3,2},{4,3},{5,4},{6,5},{7,6},{8,7},{9,8},{10,9},{11,1... | collective-permute-start | bytes 49160 | tf_op jit(solution)/shard_map/ppermute | solution.py:21
  5.0 1.9 %collective-permute-start = (bf16[16,512]{1,0:T(8,128)(2,1)S(1)}, bf16[16,512]{1,0:T(8,128)(2,1)S(1)}, u32[]{:S(2)}, u32[]{:S(2)}) collective-permute-start(bf16[16,512]{1,0:T(8,128)(2,1)S(1)} %get-tuple-element.35), channel_id=1, source_target_pairs={{0,1},{1,2},{2,3},{3,4},{4,5},{5,6},{6,7},{7,8},{8,9},{9,10},{10,1... | collective-permute-start | bytes 49160 | tf_op jit(solution)/shard_map/ppermute | solution.py:21
  7.0 0.0 collective-permute-done.1.right
  7.0 4.9 %collective-permute-done.left = bf16[16,512]{1,0:T(8,128)(2,1)S(1)} collective-permute-done((bf16[16,512]{1,0:T(8,128)(2,1)S(1)}, bf16[16,512]{1,0:T(8,128)(2,1)S(1)}, u32[]{:S(2)}, u32[]{:S(2)}) %collective-permute-start) | collective-permute-done | bytes 16416 | tf_op jit(solution)/shard_map/ppermute | solution.py:21
  11.9 0.0 copy-start
  11.9 2.3 %copy-done = bf16[3,3,512,512]{3,2,1,0:T(8,128)(2,1)S(1)} copy-done((bf16[3,3,512,512]{3,2,1,0:T(8,128)(2,1)S(1)}, bf16[3,3,512,512]{3,2,1,0:T(8,128)(2,1)}, u32[]{:S(2)}) %copy-start) | copy-done | bytes 4718616
  14.2 0.0 copy-start.1
  14.2 1.2 %copy-done.1 = bf16[1024,512]{1,0:T(8,128)(2,1)S(1)} copy-done((bf16[1024,512]{1,0:T(8,128)(2,1)S(1)}, bf16[1024,512]{1,0:T(8,128)(2,1)}, u32[]{:S(2)}) %copy-start.1) | copy-done | bytes 1048600
  15.5 0.0 copy-start.2
  15.5 0.8 %copy-done.2 = bf16[512,64]{0,1:T(8,128)(2,1)S(1)} copy-done((bf16[512,64]{0,1:T(8,128)(2,1)S(1)}, bf16[512,64]{0,1:T(8,128)(2,1)}, u32[]{:S(2)}) %copy-start.2) | copy-done | bytes 65560
  16.3 0.0 copy-start.3
  16.3 0.7 %copy-done.3 = f32[3,512]{1,0:T(4,128)S(1)} copy-done((f32[3,512]{1,0:T(4,128)S(1)}, f32[3,512]{1,0:T(4,128)}, u32[]{:S(2)}) %copy-start.3) | copy-done | bytes 6168
  17.0 7.6 %conv.1 = (bf16[64,1024]{1,0:T(8,128)(2,1)}, bf16[64,1152]{1,0:T(8,128)(2,1)S(1)}) custom-call(bf16[1024,512]{1,0:T(8,128)(2,1)S(1)} %copy-done.1, bf16[16,512]{1,0:T(8,128)(2,1)S(1)} %collective-permute-done.left, bf16[16,512]{1,0:T(8,128)(2,1)S(1)} %collective-permute-done.1.right, bf16[3,1536,512]{2,1,0:T(8,128)(2,1)S(1)} %bitcast.5, ...), custom_call_target="tpu_custom_call" | custom-call | tf_op jit(solution)/shard_map/conv/pallas_call | solution.py:189
  24.6 0.0 collective-permute-start.2
  24.6 0.0 collective-permute-start.3
  24.6 5.1 %collective-permute-done.2.refs_1_ = bf16[64,1152]{1,0:T(8,128)(2,1)S(1)} collective-permute-done((bf16[64,1152]{1,0:T(8,128)(2,1)S(1)}, bf16[64,1152]{1,0:T(8,128)(2,1)S(1)}, u32[]{:S(2)}, u32[]{:S(2)}) %collective-permute-start.2) | collective-permute-done | bytes 147488 | tf_op jit(solution)/shard_map/ppermute | solution.py:26
  29.7 0.0 collective-permute-start.4
  29.7 0.0 collective-permute-done.3.refs_2_
  29.8 1.4 %collective-permute-done.4.refs_3_ = bf16[64,1152]{1,0:T(8,128)(2,1)S(1)} collective-permute-done((bf16[64,1152]{1,0:T(8,128)(2,1)S(1)}, bf16[64,1152]{1,0:T(8,128)(2,1)S(1)}, u32[]{:S(2)}, u32[]{:S(2)}) %collective-permute-start.4) | collective-permute-done | bytes 147488 | tf_op jit(solution)/shard_map/ppermute | solution.py:26
  31.1 3.4 %block_sums.1 = (f32[512,128]{1,0:T(8,128)S(1)}, f32[64,128]{1,0:T(8,128)S(1)}, bf16[576,128]{1,0:T(8,128)(2,1)S(1)}, f32[64,128]{1,0:T(8,128)S(1)}) custom-call(bf16[64,1152]{1,0:T(8,128)(2,1)S(1)} %get-tuple-element.20.refs_0_, bf16[64,1152]{1,0:T(8,128)(2,1)S(1)} %collective-permute-done.2.refs_1_, bf16[64,1152]{1,0:T(8,128)(2,1)S(1)} %collective-permute-done.3.refs_2_, ...), custom_call_target="tpu_custom_call" | custom-call | tf_op jit(solution)/shard_map/block_sums/pallas_call | solution.py:217
  34.5 1.9 %collective-permute-start.5 = (bf16[576,128]{1,0:T(8,128)(2,1)S(1)}, bf16[576,128]{1,0:T(8,128)(2,1)S(1)}, u32[]{:S(2)}, u32[]{:S(2)}) collective-permute-start(bf16[576,128]{1,0:T(8,128)(2,1)S(1)} %get-tuple-element.23), channel_id=1, source_target_pairs={{0,4},{4,8},{8,12},{12,16},{16,20},{20,24},{24,28},{1,5},{5,9},{9,... | collective-permute-start | bytes 442376 | tf_op jit(solution)/shard_map/ppermute | solution.py:21
  36.5 6.8 %collective-permute-done.5.received = bf16[576,128]{1,0:T(8,128)(2,1)S(1)} collective-permute-done((bf16[576,128]{1,0:T(8,128)(2,1)S(1)}, bf16[576,128]{1,0:T(8,128)(2,1)S(1)}, u32[]{:S(2)}, u32[]{:S(2)}) %collective-permute-start.5) | collective-permute-done | bytes 147488 | tf_op jit(solution)/shard_map/ppermute | solution.py:21
  43.2 0.1 add.2
  43.3 1.3 %collective-permute-start.6 = (bf16[576,128]{1,0:T(8,128)(2,1)S(1)}, bf16[576,128]{1,0:T(8,128)(2,1)S(1)}, u32[]{:S(2)}, u32[]{:S(2)}) collective-permute-start(bf16[576,128]{1,0:T(8,128)(2,1)S(1)} %get-tuple-element.26), channel_id=1, source_target_pairs={{0,8},{4,12},{8,16},{12,20},{16,24},{20,28},{1,9},{5,13},{9,17},{1... | collective-permute-start | bytes 442376 | tf_op jit(solution)/shard_map/ppermute | solution.py:21
  44.6 5.7 %collective-permute-done.6.received = bf16[576,128]{1,0:T(8,128)(2,1)S(1)} collective-permute-done((bf16[576,128]{1,0:T(8,128)(2,1)S(1)}, bf16[576,128]{1,0:T(8,128)(2,1)S(1)}, u32[]{:S(2)}, u32[]{:S(2)}) %collective-permute-start.6) | collective-permute-done | bytes 147488 | tf_op jit(solution)/shard_map/ppermute | solution.py:21
  50.4 0.1 add.3
  50.5 1.3 %collective-permute-start.7 = (bf16[576,128]{1,0:T(8,128)(2,1)S(1)}, bf16[576,128]{1,0:T(8,128)(2,1)S(1)}, u32[]{:S(2)}, u32[]{:S(2)}) collective-permute-start(bf16[576,128]{1,0:T(8,128)(2,1)S(1)} %get-tuple-element.29), channel_id=1, source_target_pairs={{0,16},{4,20},{8,24},{12,28},{1,17},{5,21},{9,25},{13,29},{2,18},{... | collective-permute-start | bytes 442376 | tf_op jit(solution)/shard_map/ppermute | solution.py:21
  51.8 8.5 %collective-permute-done.7.received = bf16[576,128]{1,0:T(8,128)(2,1)S(1)} collective-permute-done((bf16[576,128]{1,0:T(8,128)(2,1)S(1)}, bf16[576,128]{1,0:T(8,128)(2,1)S(1)}, u32[]{:S(2)}, u32[]{:S(2)}) %collective-permute-start.7) | collective-permute-done | bytes 147488 | tf_op jit(solution)/shard_map/ppermute | solution.py:21
  60.2 1.2 %finish.1 = (f32[1,64]{1,0:T(1,128)}, f32[32,128]{1,0:T(8,128)}, f32[16,4096]{1,0:T(8,128)}) custom-call(f32[512,128]{1,0:T(8,128)S(1)} %get-tuple-element.27.third, f32[64,128]{1,0:T(8,128)S(1)} %get-tuple-element.28.second, bf16[576,128]{1,0:T(8,128)(2,1)S(1)} %collective-permute-done.7.received, f32[64,128]{1,0:T(8,128)S(1)} %get-tuple-element.30.ends), custom_call_target="tpu_custom_call" | custom-call | tf_op jit(solution)/shard_map/finish/pallas_call | solution.py:241
Async XLA Ops:
  1.4 5.6 %collective-permute-start.1 = (bf16[16,512]{1,0:T(8,128)(2,1)S(1)}, bf16[16,512]{1,0:T(8,128)(2,1)S(1)}, u32[]{:S(2)}, u32[]{:S(2)}) collective-permute-start(bf16[16,512]{1,0:T(8,128)(2,1)S(1)} %get-tuple-element.34), channel_id=1, source_target_pairs={{1,0},{2,1},{3,2},{4,3},{5,4},{6,5},{7,6},{8,7},{9,8},{10,9},{11,1... | collective-permute-start | bytes 49160 | tf_op jit(solution)/shard_map/ppermute | solution.py:21
  5.0 6.9 %collective-permute-start = (bf16[16,512]{1,0:T(8,128)(2,1)S(1)}, bf16[16,512]{1,0:T(8,128)(2,1)S(1)}, u32[]{:S(2)}, u32[]{:S(2)}) collective-permute-start(bf16[16,512]{1,0:T(8,128)(2,1)S(1)} %get-tuple-element.35), channel_id=1, source_target_pairs={{0,1},{1,2},{2,3},{3,4},{4,5},{5,6},{6,7},{7,8},{8,9},{9,10},{10,1... | collective-permute-start | bytes 49160 | tf_op jit(solution)/shard_map/ppermute | solution.py:21
  11.9 2.3 %copy-start = (bf16[3,3,512,512]{3,2,1,0:T(8,128)(2,1)S(1)}, bf16[3,3,512,512]{3,2,1,0:T(8,128)(2,1)}, u32[]{:S(2)}) copy-start(bf16[3,3,512,512]{3,2,1,0:T(8,128)(2,1)} %param.5) | copy-start | bytes 14155780
  14.2 1.2 %copy-start.1 = (bf16[1024,512]{1,0:T(8,128)(2,1)S(1)}, bf16[1024,512]{1,0:T(8,128)(2,1)}, u32[]{:S(2)}) copy-start(bf16[1024,512]{1,0:T(8,128)(2,1)} %rec.1) | copy-start | bytes 3145732
  15.5 0.8 %copy-start.2 = (bf16[512,64]{0,1:T(8,128)(2,1)S(1)}, bf16[512,64]{0,1:T(8,128)(2,1)}, u32[]{:S(2)}) copy-start(bf16[512,64]{0,1:T(8,128)(2,1)} %param.7) | copy-start | bytes 196612
  16.3 0.7 %copy-start.3 = (f32[3,512]{1,0:T(4,128)S(1)}, f32[3,512]{1,0:T(4,128)}, u32[]{:S(2)}) copy-start(f32[3,512]{1,0:T(4,128)} %bias.1) | copy-start | bytes 18436
  24.6 5.1 %collective-permute-start.2 = (bf16[64,1152]{1,0:T(8,128)(2,1)S(1)}, bf16[64,1152]{1,0:T(8,128)(2,1)S(1)}, u32[]{:S(2)}, u32[]{:S(2)}) collective-permute-start(bf16[64,1152]{1,0:T(8,128)(2,1)S(1)} %get-tuple-element.20.refs_0_), channel_id=1, source_target_pairs={{0,2},{1,3},{2,0},{3,1},{4,6},{5,7},{6,4},{7,5},{8,10},{9,11},{10,... | collective-permute-start | bytes 442376 | tf_op jit(solution)/shard_map/ppermute | solution.py:26
  24.6 5.1 %collective-permute-start.3 = (bf16[64,1152]{1,0:T(8,128)(2,1)S(1)}, bf16[64,1152]{1,0:T(8,128)(2,1)S(1)}, u32[]{:S(2)}, u32[]{:S(2)}) collective-permute-start(bf16[64,1152]{1,0:T(8,128)(2,1)S(1)} %get-tuple-element.20.refs_0_), channel_id=1, source_target_pairs={{0,1},{1,0},{2,3},{3,2},{4,5},{5,4},{6,7},{7,6},{8,9},{9,8},{10,11... | collective-permute-start | bytes 442376 | tf_op jit(solution)/shard_map/ppermute | solution.py:26
  29.7 1.4 %collective-permute-start.4 = (bf16[64,1152]{1,0:T(8,128)(2,1)S(1)}, bf16[64,1152]{1,0:T(8,128)(2,1)S(1)}, u32[]{:S(2)}, u32[]{:S(2)}) collective-permute-start(bf16[64,1152]{1,0:T(8,128)(2,1)S(1)} %collective-permute-done.2.refs_1_), channel_id=1, source_target_pairs={{0,1},{1,0},{2,3},{3,2},{4,5},{5,4},{6,7},{7,6},{8,9},{9,8},{10,11... | collective-permute-start | bytes 442376 | tf_op jit(solution)/shard_map/ppermute | solution.py:26
  34.5 8.7 %collective-permute-start.5 = (bf16[576,128]{1,0:T(8,128)(2,1)S(1)}, bf16[576,128]{1,0:T(8,128)(2,1)S(1)}, u32[]{:S(2)}, u32[]{:S(2)}) collective-permute-start(bf16[576,128]{1,0:T(8,128)(2,1)S(1)} %get-tuple-element.23), channel_id=1, source_target_pairs={{0,4},{4,8},{8,12},{12,16},{16,20},{20,24},{24,28},{1,5},{5,9},{9,... | collective-permute-start | bytes 442376 | tf_op jit(solution)/shard_map/ppermute | solution.py:21
  43.3 7.0 %collective-permute-start.6 = (bf16[576,128]{1,0:T(8,128)(2,1)S(1)}, bf16[576,128]{1,0:T(8,128)(2,1)S(1)}, u32[]{:S(2)}, u32[]{:S(2)}) collective-permute-start(bf16[576,128]{1,0:T(8,128)(2,1)S(1)} %get-tuple-element.26), channel_id=1, source_target_pairs={{0,8},{4,12},{8,16},{12,20},{16,24},{20,28},{1,9},{5,13},{9,17},{1... | collective-permute-start | bytes 442376 | tf_op jit(solution)/shard_map/ppermute | solution.py:21
  50.5 9.8 %collective-permute-start.7 = (bf16[576,128]{1,0:T(8,128)(2,1)S(1)}, bf16[576,128]{1,0:T(8,128)(2,1)S(1)}, u32[]{:S(2)}, u32[]{:S(2)}) collective-permute-start(bf16[576,128]{1,0:T(8,128)(2,1)S(1)} %get-tuple-element.29), channel_id=1, source_target_pairs={{0,16},{4,20},{8,24},{12,28},{1,17},{5,21},{9,25},{13,29},{2,18},{... | collective-permute-start | bytes 442376 | tf_op jit(solution)/shard_map/ppermute | solution.py:21

commit v2 on v1

v2 whole, which is shorter than its diff:
```python
import functools

import jax
import jax.numpy as jnp
from jax import lax
from jax.experimental import pallas as pl
from jax.experimental.pallas import tpu as pltpu
from jax.sharding import PartitionSpec as P

HALO = 16
LANES = 128
F32 = jnp.float32
BF16 = jnp.bfloat16
NT = (((1,), (1,)), ((), ()))
WHOLE = ("wide", "narrow")


def exchanged(array, axis, distance):
    size = lax.axis_size(axis)
    return lax.ppermute(array, axis, [(i, i ^ distance) for i in range(size)])


def edges_exchanged(recording):
    length = recording.shape[0]
    is_odd = lax.axis_index("narrow") % 2
    outer = lax.dynamic_slice_in_dim(recording, is_odd * (length - HALO), HALO, 0)
    inner = lax.dynamic_slice_in_dim(recording, (1 - is_odd) * (length - HALO), HALO, 0)
    size = lax.axis_size("wide") * lax.axis_size("narrow")
    across = [(i, min(max(i - 1 + 2 * (i % 2), 0), size - 1)) for i in range(size)]
    outer = lax.ppermute(outer, WHOLE, across)
    inner = exchanged(inner, "narrow", 1)
    return outer, inner


def conv_kernel(chunk, rec_hbm, outer, inner, weights_hbm, bias, proj, points, piece, even, odd, rec, weights, sems):
    layers = weights.shape[0]
    length = rec.shape[0]
    rows = length + 2 * HALO
    copies = [pltpu.make_async_copy(rec_hbm, rec, sems.at[layers])]
    copies += [pltpu.make_async_copy(weights_hbm.at[i], weights.at[i], sems.at[i]) for i in range(layers)]
    for copy in copies:
        copy.start()
    narrow = lax.axis_index("narrow")
    place = lax.axis_index("wide") * lax.axis_size("narrow") + narrow
    last = lax.axis_size("wide") * lax.axis_size("narrow") - 1
    is_odd = lax.rem(narrow, 2)
    lower = jnp.where(place == 0, HALO, 0)
    upper = jnp.where(place == last, HALO + length, rows)
    far = HALO + length
    at_end = jnp.logical_or(place == 0, place == last)
    even[pl.ds(pl.multiple_of(8 + is_odd * far, 8), HALO), :] = jnp.where(at_end, 0.0, outer[...].astype(F32))
    even[pl.ds(pl.multiple_of(8 + (1 - is_odd) * far, 8), HALO), :] = inner[...].astype(F32)
    copies[0].wait()
    even[8 + HALO : 8 + HALO + length, :] = rec[...].astype(F32)
    source, target = even, odd
    for layer in range(layers):
        copies[1 + layer].wait()
        reach = 2**layer
        for start in range(0, rows, chunk):
            windows = [
                source[8 + start + k * reach : 8 + start + k * reach + chunk, :] for k in (-1, 0, 1)
            ]
            stacked = jnp.concatenate([window.astype(BF16) for window in windows], axis=1)
            conv = jnp.dot(stacked, weights[layer], preferred_element_type=F32)
            half = 0.5 * (conv + bias[layer : layer + 1, :])
            hidden = windows[1] + (half + half * jnp.tanh(half))
            hidden = hidden.astype(BF16).astype(F32)
            step = start + lax.broadcasted_iota(jnp.int32, (chunk, 1), 0)
            inside = jnp.logical_and(step >= lower, step < upper)
            target[8 + start : 8 + start + chunk, :] = jnp.where(inside, hidden, 0.0)
        source, target = target, source
    final = source[8 : 8 + rows, :].astype(BF16)
    path = lax.dot_general(proj[...], final, NT, preferred_element_type=F32)
    path = path.astype(BF16).astype(F32)
    width = piece.shape[1]
    path = jnp.concatenate([path, jnp.zeros((path.shape[0], width - rows), F32)], axis=1)
    points[...] = pltpu.roll(path, width - HALO, 1)[:, :length].astype(BF16)
    piece[...] = pltpu.roll(path, width - HALO + 1, 1).astype(BF16)


def coefficients(piece, diff, lead, rest):
    padded = piece.shape[1]
    length = padded - LANES
    points = piece[...].astype(F32)
    after = pltpu.roll(points, padded - 1, 1)[:, :length]
    before = pltpu.roll(points, 1, 1)[:, :length]
    here = points[:, :length]
    middle = 0.5 * (after + before)
    diff[...] = after - before
    lead[...] = 2.0 * here + middle
    rest[...] = middle - here
    return points, after


def half_sum(half, piece, diff, lead, rest, lhs):
    width, padded = piece.shape
    length = padded - LANES
    row_count = 4 * lhs.shape[1] // width
    first_row = pl.multiple_of(lax.axis_index("narrow") * row_count, row_count)
    group = max(1, 16 // row_count)
    own_lead = lead[pl.ds(first_row, row_count), :]
    own_diff = diff[pl.ds(first_row, row_count), :]
    sums = []
    for h in range(2):
        for at in range(0, width // 4, group):
            terms = []
            for g in range(group):
                row = pl.ds(half * (width // 2) + 2 * (at + g) + h, 1)
                terms.append(diff[row, :] * own_lead + rest[row, :] * own_diff)
            term = terms[0] if group == 1 else jnp.concatenate(terms, axis=0)
            lhs[h, at * row_count : (at + group) * row_count, :] = term.astype(BF16)
        sums.append(lax.dot_general(lhs[h], piece[:, :length], NT, preferred_element_type=F32))
    return jnp.concatenate(sums, axis=1)


def parity():
    return lax.rem(lax.axis_index("wide"), 2)


def sums_kernel(masks, started, *refs):
    before, refs = refs[: 4 * started], refs[4 * started :]
    pieces, (kept, given, second, ends, diff, lead, rest, lhs) = refs[: len(masks)], refs[len(masks) :]
    values = [ref[...] for ref in before]
    for mask, piece in zip(masks, pieces):
        width, padded = piece.shape
        length = padded - LANES
        points, after = coefficients(piece, diff, lead, rest)
        crossed = lax.dot_general(after.astype(BF16), piece[:, :length], NT, preferred_element_type=F32)
        crossed = jnp.concatenate([crossed, crossed], axis=1)
        is_last = jnp.bitwise_xor(lax.axis_index("narrow"), mask) == lax.axis_size("narrow") - 1
        final = jnp.broadcast_to(points[:, length : length + 1], (width, LANES))
        previous = jnp.broadcast_to(points[:, length - 1 : length], (width, LANES))
        lane = lax.broadcasted_iota(jnp.int32, (width, LANES), 1)
        end_points = jnp.where(is_last, jnp.where(lane == 0, final, previous), 0.0)
        given_sum = half_sum(1 - parity(), piece, diff, lead, rest, lhs)
        kept_sum = half_sum(parity(), piece, diff, lead, rest, lhs)
        more = [kept_sum, given_sum, crossed, end_points]
        values = [value + extra for value, extra in zip(values, more)] if values else more
    for target, value in zip((kept, given, second, ends), values):
        target[...] = value


def pack(sent, total, doubled):
    count = total.shape[0]
    high = doubled.astype(BF16).astype(F32)
    lane = lax.broadcasted_iota(jnp.int32, doubled.shape, 1)
    sent[:count, :] = total.astype(BF16)
    sent[count:, :] = jnp.where(lane < LANES // 2, high, doubled - high).astype(BF16)


def unpack(received, count):
    coded = received[count:, :].astype(F32)
    return received[:count, :].astype(F32), coded + pltpu.roll(coded, LANES // 2, 1)


def give_kernel(given, second, sent):
    pack(sent, given[...], second[...])


def pair_kernel(kept, second, received, pair_third, pair_second, sent):
    more_third, more_second = unpack(received, kept.shape[0])
    total = kept[...] + more_third
    doubled = second[...] + more_second
    pair_third[...] = total
    pair_second[...] = doubled
    pack(sent, total, doubled)


def is_later(distance):
    return jnp.bitwise_and(lax.axis_index("wide"), distance) != 0


def scan_kernel(distance, started, *refs):
    before, (group_third, group_second, received, third, second, new_third, new_second, sent) = (
        refs[: 2 * started],
        refs[2 * started :],
    )
    more_third, more_second = unpack(received, group_third.shape[0])
    earlier_third = jnp.where(is_later(distance), more_third, 0.0)
    earlier_second = jnp.where(is_later(distance), more_second, 0.0)
    if started:
        earlier_third, earlier_second = earlier_third + before[0][...], earlier_second + before[1][...]
    third[...] = earlier_third
    second[...] = earlier_second
    total, doubled = group_third[...] + more_third, group_second[...] + more_second
    new_third[...] = total
    new_second[...] = doubled
    pack(sent, total, doubled)


def return_kernel(distance, third, received, kept, earlier, sent):
    count = third.shape[0]
    total = third[...] + jnp.where(is_later(distance), received[:count, :].astype(F32), 0.0)
    earlier[...] = total
    sent[...] = jnp.where(parity() == 0, total + kept[...], total).astype(BF16)


def products(result, half, factor, x_twice, total):
    row_count, width = factor.shape
    lane = lax.broadcasted_iota(jnp.int32, (row_count, LANES), 1)
    factor = jnp.where(half == 0, factor[:, : width // 2], factor[:, width // 2 :])
    for at in range(width // 4):
        low = jnp.broadcast_to(factor[:, 2 * at : 2 * at + 1], (row_count, LANES))
        high = jnp.broadcast_to(factor[:, 2 * at + 1 : 2 * at + 2], (row_count, LANES))
        result[:, at * LANES : (at + 1) * LANES] = (
            jnp.where(lane < width, low, high) * x_twice - total[at * row_count : (at + 1) * row_count, :]
        )


def levels_kernel(
    scale, row_count, distance, second, received, own_second, pair_second, ends, earlier, kept, pair_third,
    level_one, level_two, own_factor, x_twice, own_half, held,
):
    width = second.shape[0]
    count = received.shape[0] - width
    is_first = parity() == 0
    coded = jnp.where(is_later(distance), received[count:, :].astype(F32), 0.0)
    crossed = second[...] + coded + pltpu.roll(coded, LANES // 2, 1)
    crossed = (crossed + jnp.where(is_first, own_second[...], pair_second[...]))[:, :width]
    end_cols = ends[...]
    end_rows = end_cols.T
    x_col, a_col = end_cols[:, 0:1], end_cols[:, 1:2]
    x_row, a_row = end_rows[0:1, :], end_rows[1:2, :]
    xx = x_col * x_row
    pairs = 0.5 * xx + 0.5 * (crossed.T - crossed)
    edge = a_col * x_row - a_col * a_row - 2.0 * x_col * a_row
    factor = pairs - edge / 6.0 - xx / 3.0
    level_one[...] = scale * x_row
    held[:, :width] = scale**2 * pairs
    level_two[:, :width] = held[pl.ds(0, width // 2, stride=2), :width]
    level_two[:, width:] = held[pl.ds(1, width // 2, stride=2), :width]
    held[:, :width] = scale**3 * factor
    first_row = pl.multiple_of(lax.axis_index("narrow") * row_count, row_count)
    own = held[pl.ds(first_row, row_count), :]
    own_factor[...] = own
    twice = jnp.concatenate([x_row, x_row], axis=1)
    x_twice[...] = twice
    total = (earlier[...] + jnp.where(is_first, kept[...], pair_third[...])) * (scale**3 / 6.0)
    products(own_half, parity(), own[:, :width], twice, total)


def finish_kernel(scale, received, given, own_factor, x_twice, own_half, level_three, other_half):
    width = own_factor.shape[1] // 2
    total = (received[...].astype(F32) + given[...]) * (scale**3 / 6.0)
    products(other_half, 1 - parity(), own_factor[:, :width], x_twice[...], total)
    size = own_half.shape[1]
    at = pl.multiple_of(parity() * size, size)
    level_three[:, pl.ds(at, size)] = own_half[...]
    level_three[:, pl.ds(size - at, size)] = other_half[...]


def call(kernel, name, out_shape, scratch=(), in_specs=None, flops=0, moved=0, limit=32 * 2**20):
    shapes = [jax.ShapeDtypeStruct(dims, dtype) for dims, dtype in out_shape]
    vmem = pl.BlockSpec(memory_space=pltpu.VMEM)

    def run(*operands):
        return pl.pallas_call(
            kernel,
            out_shape=tuple(shapes),
            in_specs=in_specs or [vmem] * len(operands),
            out_specs=(vmem,) * len(shapes),
            scratch_shapes=list(scratch),
            compiler_params=pltpu.CompilerParams(vmem_limit_bytes=limit),
            cost_estimate=pl.CostEstimate(flops=flops, bytes_accessed=moved, transcendentals=0),
            name=name,
        )(*operands)

    return run


def path_of(recording, conv_weight, conv_bias, projection):
    length, channels = recording.shape
    layers, taps = conv_weight.shape[:2]
    width = projection.shape[1]
    rows = length + 2 * HALO
    outer, inner = edges_exchanged(recording)
    vmem, hbm = pl.BlockSpec(memory_space=pltpu.VMEM), pl.BlockSpec(memory_space=pltpu.HBM)
    weights = conv_weight.reshape(layers, taps * channels, channels)
    return call(
        functools.partial(conv_kernel, rows // 3),
        "conv",
        [((width, length), BF16), ((width, length + LANES), BF16)],
        scratch=[pltpu.VMEM((rows + 16, channels), F32)] * 2
        + [pltpu.VMEM(recording.shape, BF16), pltpu.VMEM(weights.shape, BF16), pltpu.SemaphoreType.DMA((layers + 1,))],
        in_specs=[hbm, vmem, vmem, hbm, vmem, vmem],
        flops=2 * layers * taps * length * channels**2,
        moved=2 * weights.size,
        limit=60 * 2**20,
    )(recording, outer, inner, weights, conv_bias, projection.T)


def per_device(recording, conv_weight, conv_bias, projection):
    length = recording.shape[0]
    width = projection.shape[1]
    wide_size, narrow_size = lax.axis_size("wide"), lax.axis_size("narrow")
    scale = float(length * wide_size * narrow_size) ** -0.2
    row_count = width // narrow_size
    count = width // 4 * row_count
    points, piece = path_of(recording, conv_weight, conv_bias, projection)

    half, square = ((count, LANES), F32), ((width, LANES), F32)
    message = ((count + width, LANES), BF16)

    order = [0]
    distance = narrow_size // 2
    held = {0: piece}
    while distance:
        for mask in list(order):
            held[mask ^ distance] = exchanged(held[mask], "narrow", distance)
            order.append(mask ^ distance)
        distance //= 2
    sums = ()
    order = sorted(order)
    for masks in (order[:2], order[2:]):
        sums = call(
            functools.partial(sums_kernel, masks, len(sums) > 0),
            "block_sums",
            [half, half, square, square],
            scratch=[pltpu.VMEM((width, length), F32)] * 3 + [pltpu.VMEM((2, count, length), BF16)],
            flops=2 * 10**9,
        )(*sums, *[held[mask] for mask in masks])
    kept, given, second, ends = sums
    (sent,) = call(give_kernel, "give", [message])(given, second)
    received = exchanged(sent, "wide", 1)
    pair_third, pair_second, sent = call(pair_kernel, "pair", [half, square, message])(kept, second, received)
    distance = 2
    received = exchanged(sent, "wide", distance)
    earlier, group_third, group_second = (), pair_third, pair_second
    while 2 * distance < wide_size:
        *earlier, group_third, group_second, sent = call(
            functools.partial(scan_kernel, distance, len(earlier) > 0),
            "scan",
            [half, square, half, square, message],
        )(*earlier, group_third, group_second, received)
        distance *= 2
        received = exchanged(sent, "wide", distance)
    if not earlier:
        earlier = [jnp.zeros(dims, dtype) for dims, dtype in (half, square)]
    total, sent = call(functools.partial(return_kernel, distance), "back", [half, ((count, LANES), BF16)])(
        earlier[0], received, kept
    )
    returned = exchanged(sent, "wide", 1)
    own_size = width * width // 2
    level_one, level_two, own_factor, x_twice, own_half = call(
        functools.partial(levels_kernel, scale, row_count, distance),
        "levels",
        [
            ((1, width), F32),
            ((width // 2, LANES), F32),
            ((row_count, LANES), F32),
            ((1, LANES), F32),
            ((row_count, own_size), F32),
        ],
        scratch=[pltpu.VMEM((width, LANES), F32)],
        flops=10**9,
    )(earlier[1], received, second, pair_second, ends, total, kept, pair_third)
    (level_three,) = call(
        functools.partial(finish_kernel, scale),
        "finish",
        [((row_count, 2 * own_size), F32)],
        scratch=[pltpu.VMEM((row_count, own_size), F32)],
    )(returned, given, own_factor, x_twice, own_half)
    return points.T, level_one, level_two.reshape(1, width * width), level_three[None]


def solution(mesh):
    return jax.shard_map(
        per_device,
        mesh=mesh,
        in_specs=(P(WHOLE, None), P(), P(), P()),
        out_specs=(P(WHOLE, None), P("wide", None), P("wide", None), P("wide", "narrow", None)),
        check_vma=False,
    )
```

time: 61.9 us -> 53 us (0.86)
  the two profiles are of different devices: /device:TPU:24 before, /device:TPU:0 now
where the time goes in v2:
time: 53 us; the launch traced here: 52.5 us
  starting transfers between devices  18.5 us (35%)
  Pallas kernels  17.4 us (33%)
  waiting for transfers between devices  13.6 us (26%)
  local copies, waits for them, and re-layouts  2.26 us (4%)
  between operations  0.71 us (1%)
    ppermute x8, starting transfers between devices, exchanged(): return lax.ppermute(array, axis, [(i, i ^ distance) for i in range(size)])  17.9 us
    pallas_call x9, Pallas kernels, run(): pl.pallas_call(kernel, out_shape=tuple(shapes), in_specs=in_specs or [vme...  17.4 us
    ppermute x8, waiting for transfers between devices, exchanged(): return lax.ppermute(array, axis, [(i, i ^ distance) for i in range(size)])  13.6 us
    unnamed x6, local copies, waits for them, and re-layouts  1.52 us
  transfers between devices with their start and end apart: 9, of which 6 were waited for; matrix products, arithmetic and copies ran while one was open for 0% of the time, Pallas kernels for 5%

profile of v2, /device:TPU:0, one launch (start us, length us, event | category | flops | bytes accessed | tf_op | source)
XLA Modules:
  0.0 52.5 jit_solution(16475694865767951637)
XLA Ops:
  0.7 0.7 %constant_dynamic-slice_fusion = (bf16[16,512]{1,0:T(8,128)(2,1)S(1)}, bf16[16,512]{1,0:T(8,128)(2,1)S(1)}) fusion(bf16[1024,512]{1,0:T(8,128)(2,1)} %rec_hbm.1, s32[]{:T(128)S(6)} %select_n.15, s32[]{:T(128)S(6)} %select_n.14), kind=kLoop, calls=%fused_computation | loop fusion | bytes 65544 | tf_op jit(solution)/shard_map/dynamic_slice | solution.py:27
  1.4 0.5 collective-permute-start.1
  1.8 0.7 %collective-permute-start = (bf16[16,512]{1,0:T(8,128)(2,1)S(1)}, bf16[16,512]{1,0:T(8,128)(2,1)S(1)}, u32[]{:S(2)}, u32[]{:S(2)}) collective-permute-start(bf16[16,512]{1,0:T(8,128)(2,1)S(1)} %get-tuple-element.51), channel_id=1, source_target_pairs={{0,0},{1,2},{2,1},{3,4},{4,3},{5,6},{6,5},{7,8},{8,7},{9,10},{10,9... | collective-permute-start | bytes 49160 | tf_op jit(solution)/shard_map/ppermute | solution.py:30
  2.5 0.2 collective-permute-done.1.inner
  2.7 0.0 copy-start.1
  2.7 0.0 collective-permute-done.outer
  2.7 0.0 copy-start.2
  2.7 0.6 %copy-done.1 = bf16[16,512]{1,0:T(8,128)(2,1)} copy-done((bf16[16,512]{1,0:T(8,128)(2,1)}, bf16[16,512]{1,0:T(8,128)(2,1)S(1)}, u32[]{:S(2)}) %copy-start.1) | copy-done | bytes 16408
  3.3 0.0 copy-done.2
  3.3 10.9 %conv.1 = (bf16[64,1024]{1,0:T(8,128)(2,1)}, bf16[64,1152]{1,0:T(8,128)(2,1)}) custom-call(bf16[1024,512]{1,0:T(8,128)(2,1)} %rec_hbm.1, bf16[16,512]{1,0:T(8,128)(2,1)} %copy-done.2, bf16[16,512]{1,0:T(8,128)(2,1)} %copy-done.1, bf16[3,1536,512]{2,1,0:T(8,128)(2,1)} %bitcast.6, f32[3,512]{1,0:T(4,128)} %bias.1, bf16[64,512]{1,0:T(8,128)(2,1)} %bitcast.7), custom_call_target="tpu_custom_call" | custom-call | flops 4831838208 | bytes 4718592 | tf_op jit(solution)/shard_map/conv/pallas_call | solution.py:257
  14.2 6.8 %collective-permute-start.3 = (bf16[64,1152]{1,0:T(8,128)(2,1)}, bf16[64,1152]{1,0:T(8,128)(2,1)S(1)}, u32[]{:S(2)}, u32[]{:S(2)}) collective-permute-start(bf16[64,1152]{1,0:T(8,128)(2,1)} %get-tuple-element.28.refs_0_), channel_id=1, source_target_pairs={{0,2},{1,3},{2,0},{3,1},{4,6},{5,7},{6,4},{7,5},{8,10},{9,11},{10,... | collective-permute-start | bytes 442376 | tf_op jit(solution)/shard_map/ppermute | solution.py:20
  21.0 1.1 %collective-permute-start.2 = (bf16[64,1152]{1,0:T(8,128)(2,1)}, bf16[64,1152]{1,0:T(8,128)(2,1)S(1)}, u32[]{:S(2)}, u32[]{:S(2)}) collective-permute-start(bf16[64,1152]{1,0:T(8,128)(2,1)} %get-tuple-element.28.refs_0_), channel_id=1, source_target_pairs={{0,1},{1,0},{2,3},{3,2},{4,5},{5,4},{6,7},{7,6},{8,9},{9,8},{10,11... | collective-permute-start | bytes 442376 | tf_op jit(solution)/shard_map/ppermute | solution.py:20
  22.1 3.2 %collective-permute-done.3.refs_4_ = bf16[64,1152]{1,0:T(8,128)(2,1)S(1)} collective-permute-done((bf16[64,1152]{1,0:T(8,128)(2,1)}, bf16[64,1152]{1,0:T(8,128)(2,1)S(1)}, u32[]{:S(2)}, u32[]{:S(2)}) %collective-permute-start.3) | collective-permute-done | bytes 147488 | tf_op jit(solution)/shard_map/ppermute | solution.py:20
  25.3 0.5 collective-permute-start.4
  25.8 0.0 collective-permute-done.2.refs_1_
  25.8 0.0 copy-start
  25.8 0.9 %copy-done = bf16[64,1152]{1,0:T(8,128)(2,1)S(1)} copy-done((bf16[64,1152]{1,0:T(8,128)(2,1)S(1)}, bf16[64,1152]{1,0:T(8,128)(2,1)}, u32[]{:S(2)}) %copy-start) | copy-done | bytes 147480
  26.7 1.9 %block_sums.2 = (f32[256,128]{1,0:T(8,128)S(1)}, f32[256,128]{1,0:T(8,128)S(1)}, f32[64,128]{1,0:T(8,128)S(1)}, f32[64,128]{1,0:T(8,128)S(1)}) custom-call(bf16[64,1152]{1,0:T(8,128)(2,1)S(1)} %copy-done, bf16[64,1152]{1,0:T(8,128)(2,1)S(1)} %collective-permute-done.2.refs_1_), custom_call_target="tpu_custom_call" | custom-call | flops 2000000000 | tf_op jit(solution)/shard_map/block_sums/pallas_call | solution.py:257
  28.6 0.0 collective-permute-done.4.refs_5_
  28.6 1.9 %block_sums.3 = (f32[256,128]{1,0:T(8,128)S(1)}, f32[256,128]{1,0:T(8,128)S(1)}, f32[64,128]{1,0:T(8,128)S(1)}, f32[64,128]{1,0:T(8,128)S(1)}) custom-call(f32[256,128]{1,0:T(8,128)S(1)} %get-tuple-element.29.refs_0_, f32[256,128]{1,0:T(8,128)S(1)} %get-tuple-element.30.refs_1_, f32[64,128]{1,0:T(8,128)S(1)} %get-tuple-element.31.refs_2_, ...), custom_call_target="tpu_custom_call" | custom-call | flops 2000000000 | tf_op jit(solution)/shard_map/block_sums/pallas_call | solution.py:257
  30.5 3.1 %collective-permute-start.5 = (bf16[320,128]{1,0:T(8,128)(2,1)S(1)}, bf16[320,128]{1,0:T(8,128)(2,1)S(1)}, u32[]{:S(2)}, u32[]{:S(2)}) collective-permute-start(bf16[320,128]{1,0:T(8,128)(2,1)S(1)} %give.1), channel_id=1, source_target_pairs={{0,4},{4,0},{8,12},{12,8},{16,20},{20,16},{24,28},{28,24},{1,5},{5... | collective-permute-start | bytes 245768 | tf_op jit(solution)/shard_map/ppermute | solution.py:20
  33.6 3.0 %collective-permute-done.5.received = bf16[320,128]{1,0:T(8,128)(2,1)S(1)} collective-permute-done((bf16[320,128]{1,0:T(8,128)(2,1)S(1)}, bf16[320,128]{1,0:T(8,128)(2,1)S(1)}, u32[]{:S(2)}, u32[]{:S(2)}) %collective-permute-start.5) | collective-permute-done | bytes 81952 | tf_op jit(solution)/shard_map/ppermute | solution.py:20
  36.6 0.1 pair.1
  36.7 1.6 %collective-permute-start.6 = (bf16[320,128]{1,0:T(8,128)(2,1)S(1)}, bf16[320,128]{1,0:T(8,128)(2,1)S(1)}, u32[]{:S(2)}, u32[]{:S(2)}) collective-permute-start(bf16[320,128]{1,0:T(8,128)(2,1)S(1)} %get-tuple-element.38), channel_id=1, source_target_pairs={{0,8},{4,12},{8,0},{12,4},{16,24},{20,28},{24,16},{28,20},{1,9},{5... | collective-permute-start | bytes 245768 | tf_op jit(solution)/shard_map/ppermute | solution.py:20
  38.3 2.9 %collective-permute-done.6.refs_2_ = bf16[320,128]{1,0:T(8,128)(2,1)S(1)} collective-permute-done((bf16[320,128]{1,0:T(8,128)(2,1)S(1)}, bf16[320,128]{1,0:T(8,128)(2,1)S(1)}, u32[]{:S(2)}, u32[]{:S(2)}) %collective-permute-start.6) | collective-permute-done | bytes 81952 | tf_op jit(solution)/shard_map/ppermute | solution.py:20
  41.2 0.7 %scan.1 = (f32[256,128]{1,0:T(8,128)S(1)}, f32[64,128]{1,0:T(8,128)S(1)}, f32[256,128]{1,0:T(8,128)}, f32[64,128]{1,0:T(8,128)}, bf16[320,128]{1,0:T(8,128)(2,1)S(1)}) custom-call(f32[256,128]{1,0:T(8,128)S(1)} %get-tuple-element.36.refs_0_.pair_third, f32[64,128]{1,0:T(8,128)S(1)} %get-tuple-element.37.refs_1_.pair_second, ...), custom_call_target="tpu_custom_call" | custom-call | tf_op jit(solution)/shard_map/scan/pallas_call | solution.py:257
  41.9 2.5 %collective-permute-start.7 = (bf16[320,128]{1,0:T(8,128)(2,1)S(1)}, bf16[320,128]{1,0:T(8,128)(2,1)S(1)}, u32[]{:S(2)}, u32[]{:S(2)}) collective-permute-start(bf16[320,128]{1,0:T(8,128)(2,1)S(1)} %get-tuple-element.40), channel_id=1, source_target_pairs={{0,16},{4,20},{8,24},{12,28},{16,0},{20,4},{24,8},{28,12},{1,17},{... | collective-permute-start | bytes 245768 | tf_op jit(solution)/shard_map/ppermute | solution.py:20
  44.4 2.8 %collective-permute-done.7.received = bf16[320,128]{1,0:T(8,128)(2,1)S(1)} collective-permute-done((bf16[320,128]{1,0:T(8,128)(2,1)S(1)}, bf16[320,128]{1,0:T(8,128)(2,1)S(1)}, u32[]{:S(2)}, u32[]{:S(2)}) %collective-permute-start.7) | collective-permute-done | bytes 81952 | tf_op jit(solution)/shard_map/ppermute | solution.py:20
  47.2 1.8 %collective-permute-start.8 = (bf16[256,128]{1,0:T(8,128)(2,1)S(1)}, bf16[256,128]{1,0:T(8,128)(2,1)S(1)}, u32[]{:S(2)}, u32[]{:S(2)}) collective-permute-start(bf16[256,128]{1,0:T(8,128)(2,1)S(1)} %get-tuple-element.46), channel_id=1, source_target_pairs={{0,4},{4,0},{8,12},{12,8},{16,20},{20,16},{24,28},{28,24},{1,5},{5... | collective-permute-start | bytes 196616 | tf_op jit(solution)/shard_map/ppermute | solution.py:20
  49.1 0.9 %levels.1 = (f32[1,64]{1,0:T(1,128)}, f32[32,128]{1,0:T(8,128)}, f32[16,128]{1,0:T(8,128)S(1)}, f32[1,128]{1,0:T(1,128)S(1)}, f32[16,2048]{1,0:T(8,128)S(1)}) custom-call(f32[64,128]{1,0:T(8,128)S(1)} %get-tuple-element.39.second, bf16[320,128]{1,0:T(8,128)(2,1)S(1)} %collective-permute-done.7.received, f32[64,128]{1,0:T(8,128)S(1)} %get-tuple-element.34.second.own_second, ...), custom_call_target="tpu_custom_call" | custom-call | flops 1000000000 | tf_op jit(solution)/shard_map/levels/pallas_call | solution.py:257
  49.9 1.6 %collective-permute-done.8.received = bf16[256,128]{1,0:T(8,128)(2,1)S(1)} collective-permute-done((bf16[256,128]{1,0:T(8,128)(2,1)S(1)}, bf16[256,128]{1,0:T(8,128)(2,1)S(1)}, u32[]{:S(2)}, u32[]{:S(2)}) %collective-permute-start.8) | collective-permute-done | bytes 65568 | tf_op jit(solution)/shard_map/ppermute | solution.py:20
  51.6 0.9 %finish.1 = f32[16,4096]{1,0:T(8,128)} custom-call(bf16[256,128]{1,0:T(8,128)(2,1)S(1)} %collective-permute-done.8.received, f32[256,128]{1,0:T(8,128)S(1)} %get-tuple-element.35.given, f32[16,128]{1,0:T(8,128)S(1)} %get-tuple-element.47.own_factor, f32[1,128]{1,0:T(1,128)S(1)} %get-tuple-element.48.x_twice, f32[16,2048]{1,0:T(8,128)S(1)} %get-tuple-element.49.own_half), custom_call_target="tpu_custom_call" | custom-call | tf_op jit(solution)/shard_map/finish/pallas_call | solution.py:257
  (2 shorter events, 0.0 us)
Async XLA Ops:
  1.4 1.3 %collective-permute-start.1 = (bf16[16,512]{1,0:T(8,128)(2,1)S(1)}, bf16[16,512]{1,0:T(8,128)(2,1)S(1)}, u32[]{:S(2)}, u32[]{:S(2)}) collective-permute-start(bf16[16,512]{1,0:T(8,128)(2,1)S(1)} %get-tuple-element.50), channel_id=1, source_target_pairs={{0,1},{1,0},{2,3},{3,2},{4,5},{5,4},{6,7},{7,6},{8,9},{9,8},{10,11... | collective-permute-start | bytes 49160 | tf_op jit(solution)/shard_map/ppermute | solution.py:20
  1.8 0.8 %collective-permute-start = (bf16[16,512]{1,0:T(8,128)(2,1)S(1)}, bf16[16,512]{1,0:T(8,128)(2,1)S(1)}, u32[]{:S(2)}, u32[]{:S(2)}) collective-permute-start(bf16[16,512]{1,0:T(8,128)(2,1)S(1)} %get-tuple-element.51), channel_id=1, source_target_pairs={{0,0},{1,2},{2,1},{3,4},{4,3},{5,6},{6,5},{7,8},{8,7},{9,10},{10,9... | collective-permute-start | bytes 49160 | tf_op jit(solution)/shard_map/ppermute | solution.py:30
  2.7 0.6 %copy-start.1 = (bf16[16,512]{1,0:T(8,128)(2,1)}, bf16[16,512]{1,0:T(8,128)(2,1)S(1)}, u32[]{:S(2)}) copy-start(bf16[16,512]{1,0:T(8,128)(2,1)S(1)} %collective-permute-done.1.inner) | copy-start | bytes 49156
  2.7 0.6 %copy-start.2 = (bf16[16,512]{1,0:T(8,128)(2,1)}, bf16[16,512]{1,0:T(8,128)(2,1)S(1)}, u32[]{:S(2)}) copy-start(bf16[16,512]{1,0:T(8,128)(2,1)S(1)} %collective-permute-done.outer) | copy-start | bytes 49156
  14.2 11.1 %collective-permute-start.3 = (bf16[64,1152]{1,0:T(8,128)(2,1)}, bf16[64,1152]{1,0:T(8,128)(2,1)S(1)}, u32[]{:S(2)}, u32[]{:S(2)}) collective-permute-start(bf16[64,1152]{1,0:T(8,128)(2,1)} %get-tuple-element.28.refs_0_), channel_id=1, source_target_pairs={{0,2},{1,3},{2,0},{3,1},{4,6},{5,7},{6,4},{7,5},{8,10},{9,11},{10,... | collective-permute-start | bytes 442376 | tf_op jit(solution)/shard_map/ppermute | solution.py:20
  21.0 4.7 %collective-permute-start.2 = (bf16[64,1152]{1,0:T(8,128)(2,1)}, bf16[64,1152]{1,0:T(8,128)(2,1)S(1)}, u32[]{:S(2)}, u32[]{:S(2)}) collective-permute-start(bf16[64,1152]{1,0:T(8,128)(2,1)} %get-tuple-element.28.refs_0_), channel_id=1, source_target_pairs={{0,1},{1,0},{2,3},{3,2},{4,5},{5,4},{6,7},{7,6},{8,9},{9,8},{10,11... | collective-permute-start | bytes 442376 | tf_op jit(solution)/shard_map/ppermute | solution.py:20
  25.3 3.3 %collective-permute-start.4 = (bf16[64,1152]{1,0:T(8,128)(2,1)S(1)}, bf16[64,1152]{1,0:T(8,128)(2,1)S(1)}, u32[]{:S(2)}, u32[]{:S(2)}) collective-permute-start(bf16[64,1152]{1,0:T(8,128)(2,1)S(1)} %collective-permute-done.3.refs_4_), channel_id=1, source_target_pairs={{0,1},{1,0},{2,3},{3,2},{4,5},{5,4},{6,7},{7,6},{8,9},{9,8},{10,11... | collective-permute-start | bytes 442376 | tf_op jit(solution)/shard_map/ppermute | solution.py:20
  25.8 0.9 %copy-start = (bf16[64,1152]{1,0:T(8,128)(2,1)S(1)}, bf16[64,1152]{1,0:T(8,128)(2,1)}, u32[]{:S(2)}) copy-start(bf16[64,1152]{1,0:T(8,128)(2,1)} %get-tuple-element.28.refs_0_) | copy-start | bytes 442372
  30.5 6.0 %collective-permute-start.5 = (bf16[320,128]{1,0:T(8,128)(2,1)S(1)}, bf16[320,128]{1,0:T(8,128)(2,1)S(1)}, u32[]{:S(2)}, u32[]{:S(2)}) collective-permute-start(bf16[320,128]{1,0:T(8,128)(2,1)S(1)} %give.1), channel_id=1, source_target_pairs={{0,4},{4,0},{8,12},{12,8},{16,20},{20,16},{24,28},{28,24},{1,5},{5... | collective-permute-start | bytes 245768 | tf_op jit(solution)/shard_map/ppermute | solution.py:20
  36.7 4.5 %collective-permute-start.6 = (bf16[320,128]{1,0:T(8,128)(2,1)S(1)}, bf16[320,128]{1,0:T(8,128)(2,1)S(1)}, u32[]{:S(2)}, u32[]{:S(2)}) collective-permute-start(bf16[320,128]{1,0:T(8,128)(2,1)S(1)} %get-tuple-element.38), channel_id=1, source_target_pairs={{0,8},{4,12},{8,0},{12,4},{16,24},{20,28},{24,16},{28,20},{1,9},{5... | collective-permute-start | bytes 245768 | tf_op jit(solution)/shard_map/ppermute | solution.py:20
  41.9 5.3 %collective-permute-start.7 = (bf16[320,128]{1,0:T(8,128)(2,1)S(1)}, bf16[320,128]{1,0:T(8,128)(2,1)S(1)}, u32[]{:S(2)}, u32[]{:S(2)}) collective-permute-start(bf16[320,128]{1,0:T(8,128)(2,1)S(1)} %get-tuple-element.40), channel_id=1, source_target_pairs={{0,16},{4,20},{8,24},{12,28},{16,0},{20,4},{24,8},{28,12},{1,17},{... | collective-permute-start | bytes 245768 | tf_op jit(solution)/shard_map/ppermute | solution.py:20
  47.2 4.3 %collective-permute-start.8 = (bf16[256,128]{1,0:T(8,128)(2,1)S(1)}, bf16[256,128]{1,0:T(8,128)(2,1)S(1)}, u32[]{:S(2)}, u32[]{:S(2)}) collective-permute-start(bf16[256,128]{1,0:T(8,128)(2,1)S(1)} %get-tuple-element.46), channel_id=1, source_target_pairs={{0,4},{4,0},{8,12},{12,8},{16,20},{20,16},{24,28},{28,24},{1,5},{5... | collective-permute-start | bytes 196616 | tf_op jit(solution)/shard_map/ppermute | solution.py:20

commit v3 on v2

--- a/solution.py
+++ b/solution.py
@@ -32,50 +32,63 @@
     return outer, inner
 
 
-def conv_kernel(chunk, rec_hbm, outer, inner, weights_hbm, bias, proj, points, piece, even, odd, rec, weights, sems):
-    layers = weights.shape[0]
+def load_kernel(rec_hbm, weights_hbm, bias_hbm, proj_hbm, rec, first, bias, proj, sems):
+    pairs = ((rec_hbm, rec), (weights_hbm.at[0], first), (bias_hbm, bias), (proj_hbm, proj))
+    copies = [pltpu.make_async_copy(*pair, sems.at[i]) for i, pair in enumerate(pairs)]
+    for copy in copies:
+        copy.start()
+    for copy in copies:
+        copy.wait()
+
+
+def conv_kernel(chunk, rec, outer, inner, first, weights_hbm, bias, proj, points, piece, even, odd, rest, path, sems):
+    layers = 1 + rest.shape[0]
     length = rec.shape[0]
     rows = length + 2 * HALO
-    copies = [pltpu.make_async_copy(rec_hbm, rec, sems.at[layers])]
-    copies += [pltpu.make_async_copy(weights_hbm.at[i], weights.at[i], sems.at[i]) for i in range(layers)]
-    for copy in copies:
-        copy.start()
+    far = HALO + length
+    copies = [pltpu.make_async_copy(weights_hbm.at[i + 1], rest.at[i], sems.at[i]) for i in range(layers - 1)]
+    copies[0].start()
     narrow = lax.axis_index("narrow")
     place = lax.axis_index("wide") * lax.axis_size("narrow") + narrow
-    last = lax.axis_size("wide") * lax.axis_size("narrow") - 1
+    is_first = place == 0
+    is_last = place == lax.axis_size("wide") * lax.axis_size("narrow") - 1
     is_odd = lax.rem(narrow, 2)
-    lower = jnp.where(place == 0, HALO, 0)
-    upper = jnp.where(place == last, HALO + length, rows)
-    far = HALO + length
-    at_end = jnp.logical_or(place == 0, place == last)
+    at_end = jnp.logical_or(is_first, is_last)
     even[pl.ds(pl.multiple_of(8 + is_odd * far, 8), HALO), :] = jnp.where(at_end, 0.0, outer[...].astype(F32))
     even[pl.ds(pl.multiple_of(8 + (1 - is_odd) * far, 8), HALO), :] = inner[...].astype(F32)
-    copies[0].wait()
-    even[8 + HALO : 8 + HALO + length, :] = rec[...].astype(F32)
+    even[8 + HALO : 8 + far, :] = rec[...].astype(F32)
+    width, padded = path.shape
+    path[:, padded - LANES :] = jnp.zeros((width, LANES), F32)
     source, target = even, odd
     for layer in range(layers):
-        copies[1 + layer].wait()
+        if layer:
+            copies[layer - 1].wait()
+            if layer < layers - 1:
+                copies[layer].start()
+        weights = rest[layer - 1] if layer else first[...]
         reach = 2**layer
         for start in range(0, rows, chunk):
+            size = min(chunk, rows - start)
             windows = [
-                source[8 + start + k * reach : 8 + start + k * reach + chunk, :] for k in (-1, 0, 1)
+                source[8 + start + k * reach : 8 + start + k * reach + size, :] for k in (-1, 0, 1)
             ]
             stacked = jnp.concatenate([window.astype(BF16) for window in windows], axis=1)
-            conv = jnp.dot(stacked, weights[layer], preferred_element_type=F32)
+            conv = jnp.dot(stacked, weights, preferred_element_type=F32)
             half = 0.5 * (conv + bias[layer : layer + 1, :])
-            hidden = windows[1] + (half + half * jnp.tanh(half))
-            hidden = hidden.astype(BF16).astype(F32)
-            step = start + lax.broadcasted_iota(jnp.int32, (chunk, 1), 0)
-            inside = jnp.logical_and(step >= lower, step < upper)
-            target[8 + start : 8 + start + chunk, :] = jnp.where(inside, hidden, 0.0)
+            hidden = (windows[1] + (half + half * jnp.tanh(half))).astype(BF16)
+            if layer < layers - 1:
+                target[8 + start : 8 + start + size, :] = hidden.astype(F32)
+            else:
+                part = lax.dot_general(hidden, proj[...], NT, preferred_element_type=F32)
+                path[:, start : start + size] = part.astype(BF16).astype(F32).T
+        if layer < layers - 1:
+            target[8 : 8 + HALO, :] = jnp.where(is_first, 0.0, target[8 : 8 + HALO, :])
+            target[8 + far : 8 + rows, :] = jnp.where(is_last, 0.0, target[8 + far : 8 + rows, :])
         source, target = target, source
-    final = source[8 : 8 + rows, :].astype(BF16)
-    path = lax.dot_general(proj[...], final, NT, preferred_element_type=F32)
-    path = path.astype(BF16).astype(F32)
-    width = piece.shape[1]
-    path = jnp.concatenate([path, jnp.zeros((path.shape[0], width - rows), F32)], axis=1)
-    points[...] = pltpu.roll(path, width - HALO, 1)[:, :length].astype(BF16)
-    piece[...] = pltpu.roll(path, width - HALO + 1, 1).astype(BF16)
+    lane = lax.broadcasted_iota(jnp.int32, (width, LANES), 1)
+    path[:, :LANES] = jnp.where(jnp.logical_and(is_first, lane < HALO), 0.0, path[:, :LANES])
+    points[...] = pltpu.roll(path[...], padded - HALO, 1)[:, :length].astype(BF16)
+    piece[...] = pltpu.roll(path[...], padded - HALO + 1, 1).astype(BF16)
 
 
 def coefficients(piece, diff, lead, rest):
@@ -98,17 +111,19 @@
     row_count = 4 * lhs.shape[1] // width
     first_row = pl.multiple_of(lax.axis_index("narrow") * row_count, row_count)
     group = max(1, 16 // row_count)
-    own_lead = lead[pl.ds(first_row, row_count), :]
-    own_diff = diff[pl.ds(first_row, row_count), :]
+    span = 2 * LANES
     sums = []
     for h in range(2):
-        for at in range(0, width // 4, group):
-            terms = []
-            for g in range(group):
-                row = pl.ds(half * (width // 2) + 2 * (at + g) + h, 1)
-                terms.append(diff[row, :] * own_lead + rest[row, :] * own_diff)
-            term = terms[0] if group == 1 else jnp.concatenate(terms, axis=0)
-            lhs[h, at * row_count : (at + group) * row_count, :] = term.astype(BF16)
+        for lanes in [slice(at, at + span) for at in range(0, length, span)]:
+            own_lead = lead[pl.ds(first_row, row_count), lanes]
+            own_diff = diff[pl.ds(first_row, row_count), lanes]
+            for at in range(0, width // 4, group):
+                terms = []
+                for g in range(group):
+                    row = pl.ds(half * (width // 2) + 2 * (at + g) + h, 1)
+                    terms.append(diff[row, lanes] * own_lead + rest[row, lanes] * own_diff)
+                term = terms[0] if group == 1 else jnp.concatenate(terms, axis=0)
+                lhs[h, at * row_count : (at + group) * row_count, lanes] = term.astype(BF16)
         sums.append(lax.dot_general(lhs[h], piece[:, :length], NT, preferred_element_type=F32))
     return jnp.concatenate(sums, axis=1)
 
@@ -117,9 +132,9 @@
     return lax.rem(lax.axis_index("wide"), 2)
 
 
-def sums_kernel(masks, started, *refs):
-    before, refs = refs[: 4 * started], refs[4 * started :]
-    pieces, (kept, given, second, ends, diff, lead, rest, lhs) = refs[: len(masks)], refs[len(masks) :]
+def given_kernel(masks, started, *refs):
+    before, refs = refs[: 3 * started], refs[3 * started :]
+    pieces, (given, second, ends, sent, diff, lead, rest, lhs) = refs[: len(masks)], refs[len(masks) :]
     values = [ref[...] for ref in before]
     for mask, piece in zip(masks, pieces):
         width, padded = piece.shape
@@ -132,12 +147,21 @@
         previous = jnp.broadcast_to(points[:, length - 1 : length], (width, LANES))
         lane = lax.broadcasted_iota(jnp.int32, (width, LANES), 1)
         end_points = jnp.where(is_last, jnp.where(lane == 0, final, previous), 0.0)
-        given_sum = half_sum(1 - parity(), piece, diff, lead, rest, lhs)
-        kept_sum = half_sum(parity(), piece, diff, lead, rest, lhs)
-        more = [kept_sum, given_sum, crossed, end_points]
+        more = [half_sum(1 - parity(), piece, diff, lead, rest, lhs), crossed, end_points]
         values = [value + extra for value, extra in zip(values, more)] if values else more
-    for target, value in zip((kept, given, second, ends), values):
+    for target, value in zip((given, second, ends), values):
         target[...] = value
+    pack(sent, values[0], values[1])
+
+
+def kept_kernel(*refs):
+    pieces, (kept, diff, lead, rest, lhs) = refs[:-5], refs[-5:]
+    total = None
+    for piece in pieces:
+        coefficients(piece, diff, lead, rest)
+        more = half_sum(parity(), piece, diff, lead, rest, lhs)
+        total = more if total is None else total + more
+    kept[...] = total
 
 
 def pack(sent, total, doubled):
@@ -151,10 +175,6 @@
 def unpack(received, count):
     coded = received[count:, :].astype(F32)
     return received[:count, :].astype(F32), coded + pltpu.roll(coded, LANES // 2, 1)
-
-
-def give_kernel(given, second, sent):
-    pack(sent, given[...], second[...])
 
 
 def pair_kernel(kept, second, received, pair_third, pair_second, sent):
@@ -276,17 +296,30 @@
     outer, inner = edges_exchanged(recording)
     vmem, hbm = pl.BlockSpec(memory_space=pltpu.VMEM), pl.BlockSpec(memory_space=pltpu.HBM)
     weights = conv_weight.reshape(layers, taps * channels, channels)
+    far = [pltpu.with_memory_space_constraint(held, pltpu.HBM) for held in (recording, weights, conv_bias, projection.T)]
+    near = call(
+        load_kernel,
+        "load",
+        [(recording.shape, BF16), (weights.shape[1:], BF16), (conv_bias.shape, F32), ((width, channels), BF16)],
+        scratch=[pltpu.SemaphoreType.DMA((4,))],
+        in_specs=[hbm] * 4,
+        flops=10**9,
+        moved=2 * (recording.size + weights.size // layers),
+    )(*far)
     return call(
-        functools.partial(conv_kernel, rows // 3),
+        functools.partial(conv_kernel, 3 * LANES),
         "conv",
         [((width, length), BF16), ((width, length + LANES), BF16)],
         scratch=[pltpu.VMEM((rows + 16, channels), F32)] * 2
-        + [pltpu.VMEM(recording.shape, BF16), pltpu.VMEM(weights.shape, BF16), pltpu.SemaphoreType.DMA((layers + 1,))],
-        in_specs=[hbm, vmem, vmem, hbm, vmem, vmem],
+        + [
+            pltpu.VMEM((layers - 1,) + weights.shape[1:], BF16),
+            pltpu.VMEM((width, length + LANES), F32),
+            pltpu.SemaphoreType.DMA((layers - 1,)),
+        ],
+        in_specs=[vmem] * 4 + [hbm] + [vmem] * 2,
         flops=2 * layers * taps * length * channels**2,
         moved=2 * weights.size,
-        limit=60 * 2**20,
-    )(recording, outer, inner, weights, conv_bias, projection.T)
+    )(near[0], outer, inner, near[1], far[1], near[2], near[3])
 
 
 def per_device(recording, conv_weight, conv_bias, projection):
@@ -301,27 +334,38 @@
     half, square = ((count, LANES), F32), ((width, LANES), F32)
     message = ((count + width, LANES), BF16)
 
-    order = [0]
+    scratch = [pltpu.VMEM((width, length), F32)] * 3 + [pltpu.VMEM((2, count, length), BF16)]
+    share = 10**9 // 2
+    pieces = {0: piece, 1: exchanged(piece, "narrow", 1)}
     distance = narrow_size // 2
-    held = {0: piece}
-    while distance:
-        for mask in list(order):
-            held[mask ^ distance] = exchanged(held[mask], "narrow", distance)
-            order.append(mask ^ distance)
+    arrived = {}
+    while distance > 1:
+        for mask, held in [(0, piece)] + sorted(arrived.items()):
+            arrived[mask ^ distance] = exchanged(held, "narrow", distance)
         distance //= 2
-    sums = ()
-    order = sorted(order)
-    for masks in (order[:2], order[2:]):
-        sums = call(
-            functools.partial(sums_kernel, masks, len(sums) > 0),
-            "block_sums",
-            [half, half, square, square],
-            scratch=[pltpu.VMEM((width, length), F32)] * 3 + [pltpu.VMEM((2, count, length), BF16)],
-            flops=2 * 10**9,
-        )(*sums, *[held[mask] for mask in masks])
-    kept, given, second, ends = sums
-    (sent,) = call(give_kernel, "give", [message])(given, second)
+    sums = call(
+        functools.partial(given_kernel, (0, 1), False),
+        "given",
+        [half, square, square, message],
+        scratch=scratch,
+        flops=2 * share,
+    )(piece, pieces[1])[:3]
+    sums, arrived = lax.optimization_barrier((sums, arrived))
+    masks = []
+    for mask, held in sorted(arrived.items()):
+        pieces[mask], pieces[mask ^ 1] = held, exchanged(held, "narrow", 1)
+        masks += [mask, mask ^ 1]
+    given, second, ends, sent = call(
+        functools.partial(given_kernel, masks, True),
+        "given",
+        [half, square, square, message],
+        scratch=scratch,
+        flops=share * len(masks),
+    )(*sums, *[pieces[mask] for mask in masks])
     received = exchanged(sent, "wide", 1)
+    (kept,) = call(kept_kernel, "kept", [half], scratch=scratch, flops=share * len(pieces))(
+        *[pieces[mask] for mask in sorted(pieces)]
+    )
     pair_third, pair_second, sent = call(pair_kernel, "pair", [half, square, message])(kept, second, received)
     distance = 2
     received = exchanged(sent, "wide", distance)

time: 53 us -> 47 us (0.89)
  waiting for transfers between devices: 13.6 us -> 10.6 us
  starting transfers between devices: 18.5 us -> 16.9 us
  local copies, waits for them, and re-layouts: 2.26 us -> 0.74 us
    ppermute x8, waiting for transfers between devices: 13.6 us -> 10.6 us  [exchanged(): return lax.ppermute(array, axis, [(i, i ^ distance) for i in range(size)])]
    ppermute x8, starting transfers between devices: 17.9 us -> 16.3 us  [exchanged(): return lax.ppermute(array, axis, [(i, i ^ distance) for i in range(size)])]
    unnamed x6 -> x0, local copies, waits for them, and re-layouts: 1.52 us -> none
    pallas_call x9 -> x10, Pallas kernels: 17.4 us -> 17.6 us  [run(): pl.pallas_call(kernel, out_shape=tuple(shapes), in_specs=in_specs or [vme...]
  transfers between devices with their start and end apart: 9 -> 9, of which waited for: 6 -> 6; matrix products, arithmetic and copies ran while one was open for 0% -> 0% of each run, Pallas kernels for 5% -> 15%
where the time goes in v3:
time: 47 us; the launch traced here: 46.6 us
  Pallas kernels  17.6 us (37%)
  starting transfers between devices  16.9 us (36%)
  waiting for transfers between devices  10.6 us (23%)
  local copies, waits for them, and re-layouts  0.74 us (2%)
  between operations  0.72 us (2%)
    pallas_call x10, Pallas kernels, run(): pl.pallas_call(kernel, out_shape=tuple(shapes), in_specs=in_specs or [vme...  17.6 us
    ppermute x8, starting transfers between devices, exchanged(): return lax.ppermute(array, axis, [(i, i ^ distance) for i in range(size)])  16.3 us
    ppermute x8, waiting for transfers between devices, exchanged(): return lax.ppermute(array, axis, [(i, i ^ distance) for i in range(size)])  10.6 us
  transfers between devices with their start and end apart: 9, of which 6 were waited for; matrix products, arithmetic and copies ran while one was open for 0% of the time, Pallas kernels for 15%

profile of v3, /device:TPU:0, one launch (start us, length us, event | category | flops | bytes accessed | tf_op | source)
XLA Modules:
  0.0 46.6 jit_solution(7135771656256823693)
XLA Ops:
  0.7 0.7 %constant_dynamic-slice_fusion = (bf16[16,512]{1,0:T(8,128)(2,1)S(1)}, bf16[16,512]{1,0:T(8,128)(2,1)S(1)}) fusion(bf16[1024,512]{1,0:T(8,128)(2,1)} %rec_hbm.1, s32[]{:T(128)S(6)} %select_n.15, s32[]{:T(128)S(6)} %select_n.14), kind=kLoop, calls=%fused_computation | loop fusion | bytes 65544 | tf_op jit(solution)/shard_map/dynamic_slice | solution.py:27
  1.4 0.5 collective-permute-start.1
  1.8 0.7 %collective-permute-start = (bf16[16,512]{1,0:T(8,128)(2,1)S(1)}, bf16[16,512]{1,0:T(8,128)(2,1)S(1)}, u32[]{:S(2)}, u32[]{:S(2)}) collective-permute-start(bf16[16,512]{1,0:T(8,128)(2,1)S(1)} %get-tuple-element.65), channel_id=1, source_target_pairs={{0,0},{1,2},{2,1},{3,4},{4,3},{5,6},{6,5},{7,8},{8,7},{9,10},{10,9... | collective-permute-start | bytes 49160 | tf_op jit(solution)/shard_map/ppermute | solution.py:30
  2.5 1.8 %load.1 = (bf16[1024,512]{1,0:T(8,128)(2,1)S(1)}, bf16[1536,512]{1,0:T(8,128)(2,1)S(1)}, f32[3,512]{1,0:T(4,128)S(1)}, bf16[64,512]{1,0:T(8,128)(2,1)S(1)}) custom-call(bf16[1024,512]{1,0:T(8,128)(2,1)} %rec_hbm.1, bf16[3,1536,512]{2,1,0:T(8,128)(2,1)} %bitcast.5, f32[3,512]{1,0:T(4,128)} %bias_hbm.1, bf16[64,512]{1,0:T(8,128)(2,1)} %bitcast.8), custom_call_target="tpu_custom_call" | custom-call | flops 1000000000 | bytes 2621440 | tf_op jit(solution)/shard_map/load/pallas_call | solution.py:277
  4.3 0.0 collective-permute-done.1.inner
  4.3 0.0 collective-permute-done.outer
  4.3 7.9 %conv.1 = (bf16[64,1024]{1,0:T(8,128)(2,1)}, bf16[64,1152]{1,0:T(8,128)(2,1)S(1)}) custom-call(bf16[1024,512]{1,0:T(8,128)(2,1)S(1)} %get-tuple-element.34.rec, bf16[16,512]{1,0:T(8,128)(2,1)S(1)} %collective-permute-done.outer, bf16[16,512]{1,0:T(8,128)(2,1)S(1)} %collective-permute-done.1.inner, bf16[1536,512]{1,0:T(8,128)(2,1)S(1)} %get-tuple-element.35.first, ...), custom_call_target="tpu_custom_call" | custom-call | flops 4831838208 | bytes 4718592 | tf_op jit(solution)/shard_map/conv/pallas_call | solution.py:277
  12.2 3.9 %collective-permute-start.2 = (bf16[64,1152]{1,0:T(8,128)(2,1)S(1)}, bf16[64,1152]{1,0:T(8,128)(2,1)S(1)}, u32[]{:S(2)}, u32[]{:S(2)}) collective-permute-start(bf16[64,1152]{1,0:T(8,128)(2,1)S(1)} %get-tuple-element.39.refs_0_), channel_id=1, source_target_pairs={{0,1},{1,0},{2,3},{3,2},{4,5},{5,4},{6,7},{7,6},{8,9},{9,8},{10,11... | collective-permute-start | bytes 442376 | tf_op jit(solution)/shard_map/ppermute | solution.py:20
  16.1 2.6 %collective-permute-start.3 = (bf16[64,1152]{1,0:T(8,128)(2,1)S(1)}, bf16[64,1152]{1,0:T(8,128)(2,1)S(1)}, u32[]{:S(2)}, u32[]{:S(2)}) collective-permute-start(bf16[64,1152]{1,0:T(8,128)(2,1)S(1)} %get-tuple-element.39.refs_0_), channel_id=1, source_target_pairs={{0,2},{1,3},{2,0},{3,1},{4,6},{5,7},{6,4},{7,5},{8,10},{9,11},{10,... | collective-permute-start | bytes 442376 | tf_op jit(solution)/shard_map/ppermute | solution.py:20
  18.8 0.0 collective-permute-done.2.refs_1_
  18.8 1.8 %given.2 = (f32[256,128]{1,0:T(8,128)S(1)}, f32[64,128]{1,0:T(8,128)S(1)}, f32[64,128]{1,0:T(8,128)S(1)}, bf16[320,128]{1,0:T(8,128)(2,1)}) custom-call(bf16[64,1152]{1,0:T(8,128)(2,1)S(1)} %get-tuple-element.39.refs_0_, bf16[64,1152]{1,0:T(8,128)(2,1)S(1)} %collective-permute-done.2.refs_1_), custom_call_target="tpu_custom_call" | custom-call | flops 1000000000 | tf_op jit(solution)/shard_map/given/pallas_call | solution.py:277
  20.6 2.3 %collective-permute-done.3.refs_2_.refs_3_ = bf16[64,1152]{1,0:T(8,128)(2,1)S(1)} collective-permute-done((bf16[64,1152]{1,0:T(8,128)(2,1)S(1)}, bf16[64,1152]{1,0:T(8,128)(2,1)S(1)}, u32[]{:S(2)}, u32[]{:S(2)}) %collective-permute-start.3) | collective-permute-done | bytes 147488 | tf_op jit(solution)/shard_map/ppermute | solution.py:20
  22.9 0.0 collective-permute-start.4
  22.9 1.4 %collective-permute-done.4.refs_3_.refs_4_ = bf16[64,1152]{1,0:T(8,128)(2,1)S(1)} collective-permute-done((bf16[64,1152]{1,0:T(8,128)(2,1)S(1)}, bf16[64,1152]{1,0:T(8,128)(2,1)S(1)}, u32[]{:S(2)}, u32[]{:S(2)}) %collective-permute-start.4) | collective-permute-done | bytes 147488 | tf_op jit(solution)/shard_map/ppermute | solution.py:20
  24.2 1.1 %given.3 = (f32[256,128]{1,0:T(8,128)S(1)}, f32[64,128]{1,0:T(8,128)S(1)}, f32[64,128]{1,0:T(8,128)S(1)}, bf16[320,128]{1,0:T(8,128)(2,1)S(1)}) custom-call(f32[256,128]{1,0:T(8,128)S(1)} %get-tuple-element.44.refs_0_, f32[64,128]{1,0:T(8,128)S(1)} %get-tuple-element.45.refs_1_, f32[64,128]{1,0:T(8,128)S(1)} %get-tuple-element.46.refs_2_, ...), custom_call_target="tpu_custom_call" | custom-call | flops 1000000000 | tf_op jit(solution)/shard_map/given/pallas_call | solution.py:277
  25.4 2.5 %collective-permute-start.5 = (bf16[320,128]{1,0:T(8,128)(2,1)S(1)}, bf16[320,128]{1,0:T(8,128)(2,1)S(1)}, u32[]{:S(2)}, u32[]{:S(2)}) collective-permute-start(bf16[320,128]{1,0:T(8,128)(2,1)S(1)} %get-tuple-element.48), channel_id=1, source_target_pairs={{0,4},{4,0},{8,12},{12,8},{16,20},{20,16},{24,28},{28,24},{1,5},{5... | collective-permute-start | bytes 245768 | tf_op jit(solution)/shard_map/ppermute | solution.py:20
  27.8 2.4 %kept.1 = f32[256,128]{1,0:T(8,128)S(1)} custom-call(bf16[64,1152]{1,0:T(8,128)(2,1)S(1)} %get-tuple-element.39.refs_0_, bf16[64,1152]{1,0:T(8,128)(2,1)S(1)} %collective-permute-done.2.refs_1_, bf16[64,1152]{1,0:T(8,128)(2,1)S(1)} %collective-permute-done.3.refs_2_.refs_3_, bf16[64,1152]{1,0:T(8,128)(2,1)S(1)} %collective-permute-done.4.refs_3_.refs_4_), custom_call_target="tpu_custom_call" | custom-call | flops 2000000000 | tf_op jit(solution)/shard_map/kept/pallas_call | solution.py:277
  30.2 0.4 collective-permute-done.5.received
  30.6 0.1 pair.1
  30.7 2.1 %collective-permute-start.6 = (bf16[320,128]{1,0:T(8,128)(2,1)S(1)}, bf16[320,128]{1,0:T(8,128)(2,1)S(1)}, u32[]{:S(2)}, u32[]{:S(2)}) collective-permute-start(bf16[320,128]{1,0:T(8,128)(2,1)S(1)} %get-tuple-element.51), channel_id=1, source_target_pairs={{0,8},{4,12},{8,0},{12,4},{16,24},{20,28},{24,16},{28,20},{1,9},{5... | collective-permute-start | bytes 245768 | tf_op jit(solution)/shard_map/ppermute | solution.py:20
  32.7 2.4 %collective-permute-done.6.refs_2_ = bf16[320,128]{1,0:T(8,128)(2,1)S(1)} collective-permute-done((bf16[320,128]{1,0:T(8,128)(2,1)S(1)}, bf16[320,128]{1,0:T(8,128)(2,1)S(1)}, u32[]{:S(2)}, u32[]{:S(2)}) %collective-permute-start.6) | collective-permute-done | bytes 81952 | tf_op jit(solution)/shard_map/ppermute | solution.py:20
  35.2 0.7 %scan.1 = (f32[256,128]{1,0:T(8,128)S(1)}, f32[64,128]{1,0:T(8,128)S(1)}, f32[256,128]{1,0:T(8,128)}, f32[64,128]{1,0:T(8,128)}, bf16[320,128]{1,0:T(8,128)(2,1)S(1)}) custom-call(f32[256,128]{1,0:T(8,128)S(1)} %get-tuple-element.49.refs_0_.pair_third, f32[64,128]{1,0:T(8,128)S(1)} %get-tuple-element.50.refs_1_.pair_second, ...), custom_call_target="tpu_custom_call" | custom-call | tf_op jit(solution)/shard_map/scan/pallas_call | solution.py:277
  35.9 3.0 %collective-permute-start.7 = (bf16[320,128]{1,0:T(8,128)(2,1)S(1)}, bf16[320,128]{1,0:T(8,128)(2,1)S(1)}, u32[]{:S(2)}, u32[]{:S(2)}) collective-permute-start(bf16[320,128]{1,0:T(8,128)(2,1)S(1)} %get-tuple-element.53), channel_id=1, source_target_pairs={{0,16},{4,20},{8,24},{12,28},{16,0},{20,4},{24,8},{28,12},{1,17},{... | collective-permute-start | bytes 245768 | tf_op jit(solution)/shard_map/ppermute | solution.py:20
  38.9 2.4 %collective-permute-done.7.received = bf16[320,128]{1,0:T(8,128)(2,1)S(1)} collective-permute-done((bf16[320,128]{1,0:T(8,128)(2,1)S(1)}, bf16[320,128]{1,0:T(8,128)(2,1)S(1)}, u32[]{:S(2)}, u32[]{:S(2)}) %collective-permute-start.7) | collective-permute-done | bytes 81952 | tf_op jit(solution)/shard_map/ppermute | solution.py:20
  41.3 1.7 %collective-permute-start.8 = (bf16[256,128]{1,0:T(8,128)(2,1)S(1)}, bf16[256,128]{1,0:T(8,128)(2,1)S(1)}, u32[]{:S(2)}, u32[]{:S(2)}) collective-permute-start(bf16[256,128]{1,0:T(8,128)(2,1)S(1)} %get-tuple-element.59), channel_id=1, source_target_pairs={{0,4},{4,0},{8,12},{12,8},{16,20},{20,16},{24,28},{28,24},{1,5},{5... | collective-permute-start | bytes 196616 | tf_op jit(solution)/shard_map/ppermute | solution.py:20
  43.0 0.9 %levels.1 = (f32[1,64]{1,0:T(1,128)}, f32[32,128]{1,0:T(8,128)}, f32[16,128]{1,0:T(8,128)S(1)}, f32[1,128]{1,0:T(1,128)S(1)}, f32[16,2048]{1,0:T(8,128)S(1)}) custom-call(f32[64,128]{1,0:T(8,128)S(1)} %get-tuple-element.52.second, bf16[320,128]{1,0:T(8,128)(2,1)S(1)} %collective-permute-done.7.received, f32[64,128]{1,0:T(8,128)S(1)} %get-tuple-element.47.second.own_second, ...), custom_call_target="tpu_custom_call" | custom-call | flops 1000000000 | tf_op jit(solution)/shard_map/levels/pallas_call | solution.py:277
  43.9 1.7 %collective-permute-done.8.received = bf16[256,128]{1,0:T(8,128)(2,1)S(1)} collective-permute-done((bf16[256,128]{1,0:T(8,128)(2,1)S(1)}, bf16[256,128]{1,0:T(8,128)(2,1)S(1)}, u32[]{:S(2)}, u32[]{:S(2)}) %collective-permute-start.8) | collective-permute-done | bytes 65568 | tf_op jit(solution)/shard_map/ppermute | solution.py:20
  45.6 0.9 %finish.1 = f32[16,4096]{1,0:T(8,128)} custom-call(bf16[256,128]{1,0:T(8,128)(2,1)S(1)} %collective-permute-done.8.received, f32[256,128]{1,0:T(8,128)S(1)} %get-tuple-element.60.given, f32[16,128]{1,0:T(8,128)S(1)} %get-tuple-element.61.own_factor, f32[1,128]{1,0:T(1,128)S(1)} %get-tuple-element.62.x_twice, f32[16,2048]{1,0:T(8,128)S(1)} %get-tuple-element.63.own_half), custom_call_target="tpu_custom_call" | custom-call | tf_op jit(solution)/shard_map/finish/pallas_call | solution.py:277
  (1 shorter events, 0.0 us)
Async XLA Ops:
  1.4 2.9 %collective-permute-start.1 = (bf16[16,512]{1,0:T(8,128)(2,1)S(1)}, bf16[16,512]{1,0:T(8,128)(2,1)S(1)}, u32[]{:S(2)}, u32[]{:S(2)}) collective-permute-start(bf16[16,512]{1,0:T(8,128)(2,1)S(1)} %get-tuple-element.64), channel_id=1, source_target_pairs={{0,1},{1,0},{2,3},{3,2},{4,5},{5,4},{6,7},{7,6},{8,9},{9,8},{10,11... | collective-permute-start | bytes 49160 | tf_op jit(solution)/shard_map/ppermute | solution.py:20
  1.8 2.5 %collective-permute-start = (bf16[16,512]{1,0:T(8,128)(2,1)S(1)}, bf16[16,512]{1,0:T(8,128)(2,1)S(1)}, u32[]{:S(2)}, u32[]{:S(2)}) collective-permute-start(bf16[16,512]{1,0:T(8,128)(2,1)S(1)} %get-tuple-element.65), channel_id=1, source_target_pairs={{0,0},{1,2},{2,1},{3,4},{4,3},{5,6},{6,5},{7,8},{8,7},{9,10},{10,9... | collective-permute-start | bytes 49160 | tf_op jit(solution)/shard_map/ppermute | solution.py:30
  12.2 6.6 %collective-permute-start.2 = (bf16[64,1152]{1,0:T(8,128)(2,1)S(1)}, bf16[64,1152]{1,0:T(8,128)(2,1)S(1)}, u32[]{:S(2)}, u32[]{:S(2)}) collective-permute-start(bf16[64,1152]{1,0:T(8,128)(2,1)S(1)} %get-tuple-element.39.refs_0_), channel_id=1, source_target_pairs={{0,1},{1,0},{2,3},{3,2},{4,5},{5,4},{6,7},{7,6},{8,9},{9,8},{10,11... | collective-permute-start | bytes 442376 | tf_op jit(solution)/shard_map/ppermute | solution.py:20
  16.1 6.7 %collective-permute-start.3 = (bf16[64,1152]{1,0:T(8,128)(2,1)S(1)}, bf16[64,1152]{1,0:T(8,128)(2,1)S(1)}, u32[]{:S(2)}, u32[]{:S(2)}) collective-permute-start(bf16[64,1152]{1,0:T(8,128)(2,1)S(1)} %get-tuple-element.39.refs_0_), channel_id=1, source_target_pairs={{0,2},{1,3},{2,0},{3,1},{4,6},{5,7},{6,4},{7,5},{8,10},{9,11},{10,... | collective-permute-start | bytes 442376 | tf_op jit(solution)/shard_map/ppermute | solution.py:20
  22.9 1.4 %collective-permute-start.4 = (bf16[64,1152]{1,0:T(8,128)(2,1)S(1)}, bf16[64,1152]{1,0:T(8,128)(2,1)S(1)}, u32[]{:S(2)}, u32[]{:S(2)}) collective-permute-start(bf16[64,1152]{1,0:T(8,128)(2,1)S(1)} %collective-permute-done.3.refs_2_.refs_3_), channel_id=1, source_target_pairs={{0,1},{1,0},{2,3},{3,2},{4,5},{5,4},{6,7},{7,6},{8,9},{9,8},{10,11... | collective-permute-start | bytes 442376 | tf_op jit(solution)/shard_map/ppermute | solution.py:20
  25.4 5.2 %collective-permute-start.5 = (bf16[320,128]{1,0:T(8,128)(2,1)S(1)}, bf16[320,128]{1,0:T(8,128)(2,1)S(1)}, u32[]{:S(2)}, u32[]{:S(2)}) collective-permute-start(bf16[320,128]{1,0:T(8,128)(2,1)S(1)} %get-tuple-element.48), channel_id=1, source_target_pairs={{0,4},{4,0},{8,12},{12,8},{16,20},{20,16},{24,28},{28,24},{1,5},{5... | collective-permute-start | bytes 245768 | tf_op jit(solution)/shard_map/ppermute | solution.py:20
  30.7 4.5 %collective-permute-start.6 = (bf16[320,128]{1,0:T(8,128)(2,1)S(1)}, bf16[320,128]{1,0:T(8,128)(2,1)S(1)}, u32[]{:S(2)}, u32[]{:S(2)}) collective-permute-start(bf16[320,128]{1,0:T(8,128)(2,1)S(1)} %get-tuple-element.51), channel_id=1, source_target_pairs={{0,8},{4,12},{8,0},{12,4},{16,24},{20,28},{24,16},{28,20},{1,9},{5... | collective-permute-start | bytes 245768 | tf_op jit(solution)/shard_map/ppermute | solution.py:20
  35.9 5.4 %collective-permute-start.7 = (bf16[320,128]{1,0:T(8,128)(2,1)S(1)}, bf16[320,128]{1,0:T(8,128)(2,1)S(1)}, u32[]{:S(2)}, u32[]{:S(2)}) collective-permute-start(bf16[320,128]{1,0:T(8,128)(2,1)S(1)} %get-tuple-element.53), channel_id=1, source_target_pairs={{0,16},{4,20},{8,24},{12,28},{16,0},{20,4},{24,8},{28,12},{1,17},{... | collective-permute-start | bytes 245768 | tf_op jit(solution)/shard_map/ppermute | solution.py:20
  41.3 4.3 %collective-permute-start.8 = (bf16[256,128]{1,0:T(8,128)(2,1)S(1)}, bf16[256,128]{1,0:T(8,128)(2,1)S(1)}, u32[]{:S(2)}, u32[]{:S(2)}) collective-permute-start(bf16[256,128]{1,0:T(8,128)(2,1)S(1)} %get-tuple-element.59), channel_id=1, source_target_pairs={{0,4},{4,0},{8,12},{12,8},{16,20},{20,16},{24,28},{28,24},{1,5},{5... | collective-permute-start | bytes 196616 | tf_op jit(solution)/shard_map/ppermute | solution.py:20

commit v4 on v3

v4 whole, which is shorter than its diff:
```python
import functools

import jax
import jax.numpy as jnp
from jax import lax
from jax.experimental import pallas as pl
from jax.experimental.pallas import tpu as pltpu
from jax.sharding import PartitionSpec as P

HALO = 16
LANES = 128
F32 = jnp.float32
BF16 = jnp.bfloat16
NT = (((1,), (1,)), ((), ()))
WHOLE = ("wide", "narrow")


def exchanged(array, axis, distance):
    size = lax.axis_size(axis)
    return lax.ppermute(array, axis, [(i, i ^ distance) for i in range(size)])


def edges_exchanged(recording):
    length = recording.shape[0]
    is_odd = lax.axis_index("narrow") % 2
    outer = lax.dynamic_slice_in_dim(recording, is_odd * (length - HALO), HALO, 0)
    inner = lax.dynamic_slice_in_dim(recording, (1 - is_odd) * (length - HALO), HALO, 0)
    wide_size, narrow_size = lax.axis_size("wide"), lax.axis_size("narrow")
    size = wide_size * narrow_size
    inside = {i: (i - 1 + 2 * (i % 2)) % narrow_size for i in range(narrow_size)}
    over = {i: (i - 1 + 2 * (i % 2)) % size for i in range(size)}
    if narrow_size > 2:
        end = size - 1
        over.update({0: 1, 1: 2, 2: 0, end: end - 1, end - 1: end - 2, end - 2: end})
    inner = exchanged(inner, "narrow", 1)
    inside = lax.ppermute(outer, "narrow", list(inside.items()))
    over = lax.ppermute(outer, WHOLE, list(over.items()))
    return over, inside, inner


def load_kernel(rec_hbm, weights_hbm, bias_hbm, proj_hbm, padded, weights, bias, proj, rec, sems):
    early = weights.shape[0]
    pairs = ((rec_hbm, rec), (weights_hbm.at[:early], weights), (bias_hbm, bias), (proj_hbm, proj))
    copies = [pltpu.make_async_copy(*pair, sems.at[i]) for i, pair in enumerate(pairs)]
    for copy in copies:
        copy.start()
    copies[0].wait()
    padded[: 8 + HALO, :] = jnp.zeros((8 + HALO, rec.shape[1]), F32)
    padded[8 + HALO : 8 + HALO + rec.shape[0], :] = rec[...].astype(F32)
    padded[8 + HALO + rec.shape[0] :, :] = jnp.zeros((8 + HALO, rec.shape[1]), F32)
    for copy in copies[1:]:
        copy.wait()


def conv_kernel(chunk, _, over, inside, inner, weights, weights_hbm, bias, proj, piece, padded, even, last_weights, path, sem):
    layers = 1 + weights.shape[0]
    rows = padded.shape[0] - 16
    length = rows - 2 * HALO
    far = HALO + length
    copy = pltpu.make_async_copy(weights_hbm.at[layers - 1], last_weights, sem)
    copy.start()
    narrow = lax.axis_index("narrow")
    place = lax.axis_index("wide") * lax.axis_size("narrow") + narrow
    is_first = place == 0
    is_last = place == lax.axis_size("wide") * lax.axis_size("narrow") - 1
    is_odd = lax.rem(narrow, 2) == 1
    width, full = path.shape
    path[:, full - LANES :] = jnp.zeros((width, LANES), F32)
    at_end = jnp.logical_or(is_first, is_last)
    at_edge = jnp.logical_or(narrow == 0, narrow == lax.axis_size("narrow") - 1)
    beyond = jnp.where(at_edge, over[...].astype(F32), inside[...].astype(F32))
    beyond = jnp.where(at_end, 0.0, beyond)
    within = inner[...].astype(F32)
    padded[8 : 8 + HALO, :] = jnp.where(is_odd, within, beyond)
    padded[8 + far : 8 + rows, :] = jnp.where(is_odd, beyond, within)
    source, target = padded, even
    for layer in range(layers):
        if layer == layers - 1:
            copy.wait()
        reach = 2**layer
        for start in range(0, rows, chunk):
            size = min(chunk, rows - start)
            windows = [
                source[8 + start + k * reach : 8 + start + k * reach + size, :] for k in (-1, 0, 1)
            ]
            conv = bias[layer : layer + 1, :]
            for tap, window in enumerate(windows):
                tap_weights = last_weights[tap] if layer == layers - 1 else weights[layer, tap]
                conv = conv + jnp.dot(window.astype(BF16), tap_weights, preferred_element_type=F32)
            half = 0.5 * conv
            hidden = (windows[1] + (half + half * jnp.tanh(half))).astype(BF16)
            if layer < layers - 1:
                target[8 + start : 8 + start + size, :] = hidden.astype(F32)
            else:
                part = lax.dot_general(hidden, proj[...], NT, preferred_element_type=F32)
                path[:, start : start + size] = part.astype(BF16).astype(F32).T
        if layer < layers - 1:
            target[8 : 8 + HALO, :] = jnp.where(is_first, 0.0, target[8 : 8 + HALO, :])
            target[8 + far : 8 + rows, :] = jnp.where(is_last, 0.0, target[8 + far : 8 + rows, :])
        source, target = target, source
    lane = lax.broadcasted_iota(jnp.int32, (width, LANES), 1)
    path[:, :LANES] = jnp.where(jnp.logical_and(is_first, lane < HALO), 0.0, path[:, :LANES])
    piece[...] = pltpu.roll(path[...], full - HALO + 1, 1).astype(BF16)


def coefficients(piece, diff, lead, rest):
    padded = piece.shape[1]
    length = padded - LANES
    points = piece[...].astype(F32)
    after = pltpu.roll(points, padded - 1, 1)[:, :length]
    before = pltpu.roll(points, 1, 1)[:, :length]
    here = points[:, :length]
    middle = 0.5 * (after + before)
    diff[...] = after - before
    lead[...] = 2.0 * here + middle
    rest[...] = middle - here
    return points, after


def half_sum(half, piece, diff, lead, rest, lhs):
    width, padded = piece.shape
    length = padded - LANES
    row_count = 4 * lhs.shape[1] // width
    first_row = pl.multiple_of(lax.axis_index("narrow") * row_count, row_count)
    group = max(1, 16 // row_count)
    span = 2 * LANES
    sums = []
    for h in range(2):
        for lanes in [slice(at, at + span) for at in range(0, length, span)]:
            own_lead = lead[pl.ds(first_row, row_count), lanes]
            own_diff = diff[pl.ds(first_row, row_count), lanes]
            for at in range(0, width // 4, group):
                terms = []
                for g in range(group):
                    row = pl.ds(half * (width // 2) + 2 * (at + g) + h, 1)
                    terms.append(diff[row, lanes] * own_lead + rest[row, lanes] * own_diff)
                term = terms[0] if group == 1 else jnp.concatenate(terms, axis=0)
                lhs[h, at * row_count : (at + group) * row_count, lanes] = term.astype(BF16)
        sums.append(lax.dot_general(lhs[h], piece[:, :length], NT, preferred_element_type=F32))
    return jnp.concatenate(sums, axis=1)


def parity():
    return lax.rem(lax.axis_index("wide"), 2)


def given_kernel(masks, started, ended, *refs):
    before, refs = refs[: 3 * started], refs[3 * started :]
    pieces, refs = refs[: len(masks)], refs[len(masks) :]
    (given, second, ends, extra), (diff, lead, rest, lhs) = refs[:4], refs[-4:]
    kept_total = None
    values = [ref[...] for ref in before]
    for mask, piece in zip(masks, pieces):
        width, padded = piece.shape
        length = padded - LANES
        points, after = coefficients(piece, diff, lead, rest)
        if mask == 0:
            extra[...] = after.astype(BF16)
        crossed = lax.dot_general(after.astype(BF16), piece[:, :length], NT, preferred_element_type=F32)
        is_last = jnp.bitwise_xor(lax.axis_index("narrow"), mask) == lax.axis_size("narrow") - 1
        final = jnp.broadcast_to(points[:, length : length + 1], (width, LANES))
        previous = jnp.broadcast_to(points[:, length - 1 : length], (width, LANES))
        lane = lax.broadcasted_iota(jnp.int32, (width, LANES), 1)
        end_points = jnp.where(is_last, jnp.where(lane == 0, final, previous), 0.0)
        more = [half_sum(1 - parity(), piece, diff, lead, rest, lhs), folded(crossed), end_points]
        values = [value + other for value, other in zip(values, more)] if values else more
        if not started:
            kept = half_sum(parity(), piece, diff, lead, rest, lhs)
            kept_total = kept if kept_total is None else kept_total + kept
    if not started:
        refs[4][...] = kept_total
    for target, value in zip((given, second, ends), values):
        target[...] = value
    if ended:
        pack(extra, values[0], values[1])


def folded(crossed):
    width = crossed.shape[0]
    turned = crossed.T - crossed
    row = lax.broadcasted_iota(jnp.int32, (width // 2, width), 0)
    lane = lax.broadcasted_iota(jnp.int32, (width // 2, width), 1)
    corner = jnp.concatenate([turned[width // 2 :, width // 2 :], turned[width // 2 :, : width // 2]], axis=1)
    upper = jnp.where(lane > row, turned[: width // 2, :], jnp.where(lane < row, corner, 0.0))
    return jnp.concatenate([upper, upper], axis=1)


def unfolded(upper):
    size = upper.shape[0]
    row = lax.broadcasted_iota(jnp.int32, (size, size), 0)
    lane = lax.broadcasted_iota(jnp.int32, (size, size), 1)
    near, far = upper[:, :size], upper[:, size : 2 * size]
    above = jnp.where(lane > row, near, 0.0)
    below = jnp.where(lane < row, near, 0.0)
    return jnp.concatenate(
        [
            jnp.concatenate([above - above.T, far], axis=1),
            jnp.concatenate([-far.T, below - below.T], axis=1),
        ],
        axis=0,
    )


def kept_kernel(before, *refs):
    pieces, (kept, diff, lead, rest, lhs) = refs[:-5], refs[-5:]
    total = before[...]
    for piece in pieces:
        coefficients(piece, diff, lead, rest)
        total = total + half_sum(parity(), piece, diff, lead, rest, lhs)
    kept[...] = total


def pack(sent, total, doubled):
    count = total.shape[0]
    high = doubled.astype(BF16).astype(F32)
    lane = lax.broadcasted_iota(jnp.int32, doubled.shape, 1)
    sent[:count, :] = total.astype(BF16)
    sent[count:, :] = jnp.where(lane < LANES // 2, high, doubled - high).astype(BF16)


def unpack(received, count):
    coded = received[count:, :].astype(F32)
    return received[:count, :].astype(F32), coded + pltpu.roll(coded, LANES // 2, 1)


def pair_kernel(kept, second, received, pair_third, pair_second, sent):
    more_third, more_second = unpack(received, kept.shape[0])
    total = kept[...] + more_third
    doubled = second[...] + more_second
    pair_third[...] = total
    pair_second[...] = doubled
    pack(sent, total, doubled)


def is_later(distance):
    return jnp.bitwise_and(lax.axis_index("wide"), distance) != 0


def scan_kernel(distance, started, ended, *refs):
    before, refs = refs[: 2 * started], refs[2 * started :]
    group_third, group_second, received, third, second, sent = refs[:6]
    more_third, more_second = unpack(received, group_third.shape[0])
    total, doubled = group_third[...] + more_third, group_second[...] + more_second
    pack(sent, total, doubled)
    earlier_third = jnp.where(is_later(distance), more_third, 0.0)
    earlier_second = jnp.where(is_later(distance), more_second, 0.0)
    if started:
        earlier_third, earlier_second = earlier_third + before[0][...], earlier_second + before[1][...]
    third[...] = earlier_third
    second[...] = earlier_second
    if not ended:
        refs[6][...] = total
        refs[7][...] = doubled


def return_kernel(distance, third, received, kept, earlier, sent):
    count = third.shape[0]
    total = third[...] + jnp.where(is_later(distance), received[:count, :].astype(F32), 0.0)
    earlier[...] = total
    sent[...] = jnp.where(parity() == 0, total + kept[...], total).astype(BF16)


def products(result, half, factor, x_twice, total):
    row_count, width = factor.shape
    lane = lax.broadcasted_iota(jnp.int32, (row_count, LANES), 1)
    factor = jnp.where(half == 0, factor[:, : width // 2], factor[:, width // 2 :])
    for at in range(width // 4):
        low = jnp.broadcast_to(factor[:, 2 * at : 2 * at + 1], (row_count, LANES))
        high = jnp.broadcast_to(factor[:, 2 * at + 1 : 2 * at + 2], (row_count, LANES))
        result[:, at * LANES : (at + 1) * LANES] = (
            jnp.where(lane < width, low, high) * x_twice - total[at * row_count : (at + 1) * row_count, :]
        )


def levels_kernel(
    scale, row_count, distance, second, received, own_second, pair_second, ends, earlier, kept, pair_third, given,
    level_one, level_two, partly, rest, held, own_half, sem,
):
    width = ends.shape[0]
    count = received.shape[0] - second.shape[0]
    is_first = parity() == 0
    end_cols = ends[...]
    end_rows = end_cols.T
    x_col, a_col = end_cols[:, 0:1], end_cols[:, 1:2]
    x_row, a_row = end_rows[0:1, :], end_rows[1:2, :]
    xx = x_col * x_row
    edge = a_col * x_row - a_col * a_row - 2.0 * x_col * a_row
    coded = jnp.where(is_later(distance), received[count:, :].astype(F32), 0.0)
    upper = second[...] + coded + pltpu.roll(coded, LANES // 2, 1)
    upper = upper + jnp.where(is_first, own_second[...], pair_second[...])
    pairs = 0.5 * xx + 0.5 * unfolded(upper)
    factor = pairs - edge / 6.0 - xx / 3.0
    level_one[...] = scale * x_row
    held[:, :width] = scale**3 * factor
    first_row = pl.multiple_of(lax.axis_index("narrow") * row_count, row_count)
    own = held[pl.ds(first_row, row_count), :width]
    twice = jnp.concatenate([x_row, x_row], axis=1)
    total = (earlier[...] + jnp.where(is_first, kept[...], pair_third[...])) * (scale**3 / 6.0)
    products(own_half, parity(), own, twice, total)
    size = own_half.shape[1]
    at = pl.multiple_of(parity() * size, size)
    copy = pltpu.make_async_copy(own_half, partly.at[:, pl.ds(at, size)], sem)
    copy.start()
    products(rest, 1 - parity(), own, twice, given[...] * (scale**3 / 6.0))
    held[:, :width] = scale**2 * pairs
    level_two[:, :width] = held[pl.ds(0, width // 2, stride=2), :width]
    level_two[:, width:] = held[pl.ds(1, width // 2, stride=2), :width]
    copy.wait()


def finish_kernel(scale, row_count, received, rest, partly, level_three, other_half, sem):
    size = rest.shape[1]
    for at in range(size // LANES):
        lanes = slice(at * LANES, (at + 1) * LANES)
        come = received[at * row_count : (at + 1) * row_count, :].astype(F32)
        other_half[:, lanes] = rest[:, lanes] - come * (scale**3 / 6.0)
    at = pl.multiple_of((1 - parity()) * size, size)
    copy = pltpu.make_async_copy(other_half, level_three.at[:, pl.ds(at, size)], sem)
    copy.start()
    copy.wait()


VMEM = pl.BlockSpec(memory_space=pltpu.VMEM)
HBM = pl.BlockSpec(memory_space=pltpu.HBM)


def call(kernel, name, out_shape, scratch=(), in_specs=None, out_specs=None, aliases=None, flops=0, moved=0):
    shapes = [jax.ShapeDtypeStruct(dims, dtype) for dims, dtype in out_shape]

    def run(*operands):
        return pl.pallas_call(
            kernel,
            out_shape=tuple(shapes),
            in_specs=in_specs or [VMEM] * len(operands),
            out_specs=out_specs or (VMEM,) * len(shapes),
            input_output_aliases=aliases or {},
            scratch_shapes=list(scratch),
            compiler_params=pltpu.CompilerParams(vmem_limit_bytes=32 * 2**20),
            cost_estimate=pl.CostEstimate(flops=flops, bytes_accessed=moved, transcendentals=0),
            name=name,
        )(*operands)

    return run


def path_of(recording, conv_weight, conv_bias, projection):
    length, channels = recording.shape
    layers, taps = conv_weight.shape[:2]
    width = projection.shape[1]
    rows = length + 2 * HALO
    edges = edges_exchanged(recording)
    buffer = ((rows + 16, channels), F32)
    far = (recording, conv_weight, conv_bias, projection.T)
    far = [pltpu.with_memory_space_constraint(held, pltpu.HBM) for held in far]
    padded, *near = call(
        load_kernel,
        "load",
        [buffer, ((layers - 1,) + conv_weight.shape[1:], BF16), (conv_bias.shape, F32), ((width, channels), BF16)],
        scratch=[pltpu.VMEM(recording.shape, BF16), pltpu.SemaphoreType.DMA((4,))],
        in_specs=[HBM] * len(far),
        flops=10**9,
        moved=2 * sum(held.size for held in far),
    )(*far)
    piece, _ = call(
        functools.partial(conv_kernel, 3 * LANES),
        "conv",
        [((width, length + LANES), BF16), buffer],
        scratch=[
            pltpu.VMEM(buffer[0], F32),
            pltpu.VMEM(conv_weight.shape[1:], BF16),
            pltpu.VMEM((width, length + LANES), F32),
            pltpu.SemaphoreType.DMA,
        ],
        in_specs=[VMEM] * 5 + [HBM] + [VMEM] * 2,
        aliases={0: 1},
        flops=2 * layers * taps * length * channels**2,
        moved=2 * conv_weight.size,
    )(padded, *edges, near[0], far[1], near[1], near[2])
    return piece


def per_device(recording, conv_weight, conv_bias, projection):
    length = recording.shape[0]
    width = projection.shape[1]
    wide_size, narrow_size = lax.axis_size("wide"), lax.axis_size("narrow")
    scale = float(length * wide_size * narrow_size) ** -0.2
    row_count = width // narrow_size
    count = width // 4 * row_count
    piece = path_of(recording, conv_weight, conv_bias, projection)

    half, square, folds = ((count, LANES), F32), ((width, LANES), F32), ((width // 2, LANES), F32)
    message = ((count + width // 2, LANES), BF16)

    scratch = [pltpu.VMEM((width, length), F32)] * 3 + [pltpu.VMEM((2, count, length), BF16)]
    share = 10**9 // 2
    pieces = {0: piece, 1: exchanged(piece, "narrow", 1)}
    distance = narrow_size // 2
    arrived = {}
    while distance > 1:
        for mask, held in [(0, piece)] + sorted(arrived.items()):
            arrived[mask ^ distance] = exchanged(held, "narrow", distance)
        distance //= 2
    *sums, points, kept = call(
        functools.partial(given_kernel, (0, 1), False, False),
        "given",
        [half, folds, square, ((width, length), BF16), half],
        scratch=scratch,
        flops=4 * share,
    )(piece, pieces[1])
    sums, arrived = lax.optimization_barrier((sums, arrived))
    for mask, held in sorted(arrived.items()):
        pieces[mask], pieces[mask ^ 1] = held, exchanged(held, "narrow", 1)
    masks = sorted(arrived) + [mask ^ 1 for mask in sorted(arrived)]
    for mask in masks:
        *sums, sent = call(
            functools.partial(given_kernel, (mask,), True, mask == masks[-1]),
            "given",
            [half, folds, square, message],
            scratch=scratch,
            flops=share,
        )(*sums, pieces[mask])
    given, second, ends = sums
    received = exchanged(sent, "wide", 1)
    (kept,) = call(kept_kernel, "kept", [half], scratch=scratch, flops=share * len(masks))(
        kept, *[pieces[mask] for mask in masks]
    )
    pair_third, pair_second, sent = call(pair_kernel, "pair", [half, folds, message])(kept, second, received)
    distance = 2
    received = exchanged(sent, "wide", distance)
    earlier, group_third, group_second = (), pair_third, pair_second
    while 2 * distance < wide_size:
        ended = 4 * distance >= wide_size
        *earlier, sent = call(
            functools.partial(scan_kernel, distance, len(earlier) > 0, ended),
            "scan",
            [half, folds, message] + ([] if ended else [half, folds]),
        )(*earlier, group_third, group_second, received)
        if not ended:
            sent, group_third, group_second = earlier[2], earlier[3], sent
            earlier = earlier[:2]
        distance *= 2
        received = exchanged(sent, "wide", distance)
    if not earlier:
        earlier = [jnp.zeros(dims, dtype) for dims, dtype in (half, folds)]
    total, sent = call(functools.partial(return_kernel, distance), "back", [half, ((count, LANES), BF16)])(
        earlier[0], received, kept
    )
    returned = exchanged(sent, "wide", 1)
    own_size = width * width // 2
    third_shape = ((row_count, 2 * own_size), F32)
    half_buffer = ((row_count, own_size), F32)
    level_one, level_two, partly, rest = call(
        functools.partial(levels_kernel, scale, row_count, distance),
        "levels",
        [((1, width), F32), folds, third_shape, half_buffer],
        scratch=[pltpu.VMEM((width, LANES), F32), pltpu.VMEM(half_buffer[0], F32), pltpu.SemaphoreType.DMA],
        out_specs=(VMEM, VMEM, HBM, VMEM),
        flops=10**9,
    )(earlier[1], received, second, pair_second, ends, total, kept, pair_third, given)
    (level_three,) = call(
        functools.partial(finish_kernel, scale, row_count),
        "finish",
        [third_shape],
        scratch=[pltpu.VMEM(half_buffer[0], F32), pltpu.SemaphoreType.DMA],
        in_specs=[VMEM, VMEM, HBM],
        out_specs=(HBM,),
        aliases={2: 0},
    )(returned, rest, partly)
    return points.T, level_one, level_two.reshape(1, width * width), level_three[None]


def solution(mesh):
    return jax.shard_map(
        per_device,
        mesh=mesh,
        in_specs=(P(WHOLE, None), P(), P(), P()),
        out_specs=(P(WHOLE, None), P("wide", None), P("wide", None), P("wide", "narrow", None)),
        check_vma=False,
    )
```

time: 47 us -> 43.3 us (0.921)
  starting transfers between devices: 16.9 us -> 13.7 us
  Pallas kernels: 17.6 us -> 16.8 us
    ppermute x8, starting transfers between devices: 16.3 us -> 10.6 us  [exchanged(): return lax.ppermute(array, axis, [(i, i ^ distance) for i in range(size)])]
    ppermute x1 -> x2, starting transfers between devices: 0.65 us -> 3.08 us  [the longest x1 2.41 us: edges_exchanged(): inside = lax.ppermute(outer, 'narrow', list(inside.items()))]
    pallas_call x10 -> x11, Pallas kernels: 17.6 us -> 16.8 us  [run(): pl.pallas_call(kernel, out_shape=tuple(shapes), in_specs=in_specs or [VME...]
    ppermute x1 -> x2, waiting for transfers between devices: 0.01 us -> 0.75 us  [the longest x1 0.75 us: edges_exchanged(): over = lax.ppermute(outer, WHOLE, list(over.items()))]
  transfers between devices with their start and end apart: 9 -> 10, of which waited for: 6 -> 7; matrix products, arithmetic and copies ran while one was open for 0% -> 0% of each run, Pallas kernels for 15% -> 20%
where the time goes in v4:
time: 43.3 us; the launch traced here: 42.9 us
  Pallas kernels  16.8 us (39%)
  starting transfers between devices  13.7 us (32%)
  waiting for transfers between devices  11 us (25%)
  local copies, waits for them, and re-layouts  0.74 us (2%)
  between operations  0.72 us (2%)
    pallas_call x11, Pallas kernels, run(): pl.pallas_call(kernel, out_shape=tuple(shapes), in_specs=in_specs or [VME...  16.8 us
    ppermute x8, starting transfers between devices, exchanged(): return lax.ppermute(array, axis, [(i, i ^ distance) for i in range(size)])  10.6 us
    ppermute x8, waiting for transfers between devices, exchanged(): return lax.ppermute(array, axis, [(i, i ^ distance) for i in range(size)])  10.2 us
    ppermute x1, starting transfers between devices, edges_exchanged(): inside = lax.ppermute(outer, 'narrow', list(inside.items()))  2.41 us
  transfers between devices with their start and end apart: 10, of which 7 were waited for; matrix products, arithmetic and copies ran while one was open for 0% of the time, Pallas kernels for 20%

profile of v4, /device:TPU:0, one launch (start us, length us, event | category | flops | bytes accessed | tf_op | source)
XLA Modules:
  0.0 42.9 jit_solution(11166033233465722095)
XLA Ops:
  0.7 0.7 %constant_dynamic-slice_fusion = (bf16[16,512]{1,0:T(8,128)(2,1)S(1)}, bf16[16,512]{1,0:T(8,128)(2,1)S(1)}) fusion(bf16[1024,512]{1,0:T(8,128)(2,1)} %rec_hbm.1, s32[]{:T(128)S(6)} %select_n.15, s32[]{:T(128)S(6)} %select_n.14), kind=kLoop, calls=%fused_computation | loop fusion | bytes 65544 | tf_op jit(solution)/shard_map/dynamic_slice | solution.py:27
  1.4 2.4 %collective-permute-start.1 = (bf16[16,512]{1,0:T(8,128)(2,1)S(1)}, bf16[16,512]{1,0:T(8,128)(2,1)S(1)}, u32[]{:S(2)}, u32[]{:S(2)}) collective-permute-start(bf16[16,512]{1,0:T(8,128)(2,1)S(1)} %get-tuple-element.71), channel_id=1, source_target_pairs={{0,3},{1,2},{2,1},{3,0},{4,7},{5,6},{6,5},{7,4},{8,11},{9,10},{10,... | collective-permute-start | bytes 49160 | tf_op jit(solution)/shard_map/ppermute | solution.py:36
  3.8 0.7 %collective-permute-start = (bf16[16,512]{1,0:T(8,128)(2,1)S(1)}, bf16[16,512]{1,0:T(8,128)(2,1)S(1)}, u32[]{:S(2)}, u32[]{:S(2)}) collective-permute-start(bf16[16,512]{1,0:T(8,128)(2,1)S(1)} %get-tuple-element.71), channel_id=1, source_target_pairs={{0,1},{1,2},{2,0},{3,4},{4,3},{5,6},{6,5},{7,8},{8,7},{9,10},{10,9... | collective-permute-start | bytes 49160 | tf_op jit(solution)/shard_map/ppermute | solution.py:37
  4.5 0.0 collective-permute-start.2
  4.5 2.3 %load.1 = (f32[1072,512]{1,0:T(8,128)S(1)}, bf16[2,3,512,512]{3,2,1,0:T(8,128)(2,1)S(1)}, f32[3,512]{1,0:T(4,128)S(1)}, bf16[64,512]{1,0:T(8,128)(2,1)S(1)}) custom-call(bf16[1024,512]{1,0:T(8,128)(2,1)} %rec_hbm.1, bf16[3,3,512,512]{3,2,1,0:T(8,128)(2,1)} %weights_hbm.3, f32[3,512]{1,0:T(4,128)} %bias_hbm.1, bf16[64,512]{1,0:T(8,128)(2,1)} %bitcast.5), custom_call_target="tpu_custom_call" | custom-call | flops 1000000000 | bytes 5835776 | tf_op jit(solution)/shard_map/load/pallas_call | solution.py:331
  6.8 0.0 collective-permute-done.2.inner
  6.8 0.0 collective-permute-done.1.inside
  6.8 0.7 %collective-permute-done.over = bf16[16,512]{1,0:T(8,128)(2,1)S(1)} collective-permute-done((bf16[16,512]{1,0:T(8,128)(2,1)S(1)}, bf16[16,512]{1,0:T(8,128)(2,1)S(1)}, u32[]{:S(2)}, u32[]{:S(2)}) %collective-permute-start) | collective-permute-done | bytes 16416 | tf_op jit(solution)/shard_map/ppermute | solution.py:37
  7.5 6.6 %conv.1 = (bf16[64,1152]{1,0:T(8,128)(2,1)S(1)}, f32[1072,512]{1,0:T(8,128)S(1)}) custom-call(f32[1072,512]{1,0:T(8,128)S(1)} %get-tuple-element.37._, bf16[16,512]{1,0:T(8,128)(2,1)S(1)} %collective-permute-done.over, bf16[16,512]{1,0:T(8,128)(2,1)S(1)} %collective-permute-done.1.inside, ...), custom_call_target="tpu_custom_call", output_to_operand_aliasing={{1}: (0, {})} | custom-call | flops 4831838208 | bytes 4718592 | tf_op jit(solution)/shard_map/conv/pallas_call | solution.py:331
  14.2 0.1 collective-permute-start.3
  14.3 1.7 %collective-permute-start.4 = (bf16[64,1152]{1,0:T(8,128)(2,1)S(1)}, bf16[64,1152]{1,0:T(8,128)(2,1)S(1)}, u32[]{:S(2)}, u32[]{:S(2)}) collective-permute-start(bf16[64,1152]{1,0:T(8,128)(2,1)S(1)} %get-tuple-element.41.refs_0_), channel_id=1, source_target_pairs={{0,2},{1,3},{2,0},{3,1},{4,6},{5,7},{6,4},{7,5},{8,10},{9,11},{10,... | collective-permute-start | bytes 442376 | tf_op jit(solution)/shard_map/ppermute | solution.py:20
  16.0 0.0 collective-permute-done.3.refs_1_
  16.0 2.2 %given.3 = (f32[256,128]{1,0:T(8,128)S(1)}, f32[32,128]{1,0:T(8,128)S(1)}, f32[64,128]{1,0:T(8,128)S(1)}, bf16[64,1024]{1,0:T(8,128)(2,1)}, f32[256,128]{1,0:T(8,128)S(1)}) custom-call(bf16[64,1152]{1,0:T(8,128)(2,1)S(1)} %get-tuple-element.41.refs_0_, bf16[64,1152]{1,0:T(8,128)(2,1)S(1)} %collective-permute-done.3.refs_1_), custom_call_target="tpu_custom_call" | custom-call | flops 2000000000 | tf_op jit(solution)/shard_map/given/pallas_call | solution.py:331
  18.1 2.4 %collective-permute-done.4.refs_0_.refs_3_ = bf16[64,1152]{1,0:T(8,128)(2,1)S(1)} collective-permute-done((bf16[64,1152]{1,0:T(8,128)(2,1)S(1)}, bf16[64,1152]{1,0:T(8,128)(2,1)S(1)}, u32[]{:S(2)}, u32[]{:S(2)}) %collective-permute-start.4) | collective-permute-done | bytes 147488 | tf_op jit(solution)/shard_map/ppermute | solution.py:20
  20.5 0.0 collective-permute-start.5
  20.5 1.1 %given.4 = (f32[256,128]{1,0:T(8,128)S(1)}, f32[32,128]{1,0:T(8,128)S(1)}, f32[64,128]{1,0:T(8,128)S(1)}, bf16[288,128]{1,0:T(8,128)(2,1)}) custom-call(f32[256,128]{1,0:T(8,128)S(1)} %get-tuple-element.48.refs_0_, f32[32,128]{1,0:T(8,128)S(1)} %get-tuple-element.49.refs_1_, f32[64,128]{1,0:T(8,128)S(1)} %get-tuple-element.50.refs_2_, ...), custom_call_target="tpu_custom_call" | custom-call | flops 500000000 | tf_op jit(solution)/shard_map/given/pallas_call | solution.py:331
  21.7 0.2 collective-permute-done.5.refs_1_.refs_3_
  21.9 0.7 %given.5 = (f32[256,128]{1,0:T(8,128)S(1)}, f32[32,128]{1,0:T(8,128)S(1)}, f32[64,128]{1,0:T(8,128)S(1)}, bf16[288,128]{1,0:T(8,128)(2,1)S(1)}) custom-call(f32[256,128]{1,0:T(8,128)S(1)} %get-tuple-element.51.refs_0_, f32[32,128]{1,0:T(8,128)S(1)} %get-tuple-element.52.refs_1_, f32[64,128]{1,0:T(8,128)S(1)} %get-tuple-element.53.refs_2_, ...), custom_call_target="tpu_custom_call" | custom-call | flops 500000000 | tf_op jit(solution)/shard_map/given/pallas_call | solution.py:331
  22.6 2.0 %collective-permute-start.6 = (bf16[288,128]{1,0:T(8,128)(2,1)S(1)}, bf16[288,128]{1,0:T(8,128)(2,1)S(1)}, u32[]{:S(2)}, u32[]{:S(2)}) collective-permute-start(bf16[288,128]{1,0:T(8,128)(2,1)S(1)} %get-tuple-element.55), channel_id=1, source_target_pairs={{0,4},{4,0},{8,12},{12,8},{16,20},{20,16},{24,28},{28,24},{1,5},{5... | collective-permute-start | bytes 221192 | tf_op jit(solution)/shard_map/ppermute | solution.py:20
  24.6 1.2 %kept.1 = f32[256,128]{1,0:T(8,128)S(1)} custom-call(f32[256,128]{1,0:T(8,128)S(1)} %get-tuple-element.43.before, bf16[64,1152]{1,0:T(8,128)(2,1)S(1)} %collective-permute-done.4.refs_0_.refs_3_, bf16[64,1152]{1,0:T(8,128)(2,1)S(1)} %collective-permute-done.5.refs_1_.refs_3_), custom_call_target="tpu_custom_call" | custom-call | flops 1000000000 | tf_op jit(solution)/shard_map/kept/pallas_call | solution.py:331
  25.8 1.5 %collective-permute-done.6.received = bf16[288,128]{1,0:T(8,128)(2,1)S(1)} collective-permute-done((bf16[288,128]{1,0:T(8,128)(2,1)S(1)}, bf16[288,128]{1,0:T(8,128)(2,1)S(1)}, u32[]{:S(2)}, u32[]{:S(2)}) %collective-permute-start.6) | collective-permute-done | bytes 73760 | tf_op jit(solution)/shard_map/ppermute | solution.py:20
  27.3 0.1 pair.1
  27.4 2.7 %collective-permute-start.7 = (bf16[288,128]{1,0:T(8,128)(2,1)S(1)}, bf16[288,128]{1,0:T(8,128)(2,1)S(1)}, u32[]{:S(2)}, u32[]{:S(2)}) collective-permute-start(bf16[288,128]{1,0:T(8,128)(2,1)S(1)} %get-tuple-element.58), channel_id=1, source_target_pairs={{0,8},{4,12},{8,0},{12,4},{16,24},{20,28},{24,16},{28,20},{1,9},{5... | collective-permute-start | bytes 221192 | tf_op jit(solution)/shard_map/ppermute | solution.py:20
  30.1 2.3 %collective-permute-done.7.refs_2_ = bf16[288,128]{1,0:T(8,128)(2,1)S(1)} collective-permute-done((bf16[288,128]{1,0:T(8,128)(2,1)S(1)}, bf16[288,128]{1,0:T(8,128)(2,1)S(1)}, u32[]{:S(2)}, u32[]{:S(2)}) %collective-permute-start.7) | collective-permute-done | bytes 73760 | tf_op jit(solution)/shard_map/ppermute | solution.py:20
  32.4 0.1 scan.1
  32.5 3.1 %collective-permute-start.8 = (bf16[288,128]{1,0:T(8,128)(2,1)S(1)}, bf16[288,128]{1,0:T(8,128)(2,1)S(1)}, u32[]{:S(2)}, u32[]{:S(2)}) collective-permute-start(bf16[288,128]{1,0:T(8,128)(2,1)S(1)} %get-tuple-element.60), channel_id=1, source_target_pairs={{0,16},{4,20},{8,24},{12,28},{16,0},{20,4},{24,8},{28,12},{1,17},{... | collective-permute-start | bytes 221192 | tf_op jit(solution)/shard_map/ppermute | solution.py:20
  35.6 2.3 %collective-permute-done.8.received = bf16[288,128]{1,0:T(8,128)(2,1)S(1)} collective-permute-done((bf16[288,128]{1,0:T(8,128)(2,1)S(1)}, bf16[288,128]{1,0:T(8,128)(2,1)S(1)}, u32[]{:S(2)}, u32[]{:S(2)}) %collective-permute-start.8) | collective-permute-done | bytes 73760 | tf_op jit(solution)/shard_map/ppermute | solution.py:20
  37.9 1.1 %collective-permute-start.9 = (bf16[256,128]{1,0:T(8,128)(2,1)S(1)}, bf16[256,128]{1,0:T(8,128)(2,1)S(1)}, u32[]{:S(2)}, u32[]{:S(2)}) collective-permute-start(bf16[256,128]{1,0:T(8,128)(2,1)S(1)} %get-tuple-element.67), channel_id=1, source_target_pairs={{0,4},{4,0},{8,12},{12,8},{16,20},{20,16},{24,28},{28,24},{1,5},{5... | collective-permute-start | bytes 196616 | tf_op jit(solution)/shard_map/ppermute | solution.py:20
  39.0 1.9 %levels.1 = (f32[1,64]{1,0:T(1,128)}, f32[32,128]{1,0:T(8,128)}, f32[16,4096]{1,0:T(8,128)}, f32[16,2048]{1,0:T(8,128)S(1)}) custom-call(f32[32,128]{1,0:T(8,128)S(1)} %get-tuple-element.59.second, bf16[288,128]{1,0:T(8,128)(2,1)S(1)} %collective-permute-done.8.received, f32[32,128]{1,0:T(8,128)S(1)} %get-tuple-element.54.second.own_second, ...), custom_call_target="tpu_custom_call" | custom-call | flops 1000000000 | tf_op jit(solution)/shard_map/levels/pallas_call | solution.py:331
  40.9 1.4 %collective-permute-done.9.received = bf16[256,128]{1,0:T(8,128)(2,1)S(1)} collective-permute-done((bf16[256,128]{1,0:T(8,128)(2,1)S(1)}, bf16[256,128]{1,0:T(8,128)(2,1)S(1)}, u32[]{:S(2)}, u32[]{:S(2)}) %collective-permute-start.9) | collective-permute-done | bytes 65568 | tf_op jit(solution)/shard_map/ppermute | solution.py:20
  42.3 0.7 %finish.1 = f32[16,4096]{1,0:T(8,128)} custom-call(bf16[256,128]{1,0:T(8,128)(2,1)S(1)} %collective-permute-done.9.received, f32[16,2048]{1,0:T(8,128)S(1)} %get-tuple-element.68.rest, f32[16,4096]{1,0:T(8,128)} %get-tuple-element.69.partly), custom_call_target="tpu_custom_call", output_to_operand_aliasing={{}: (2, {})} | custom-call | tf_op jit(solution)/shard_map/finish/pallas_call | solution.py:331
  (1 shorter events, 0.0 us)
Async XLA Ops:
  1.4 5.4 %collective-permute-start.1 = (bf16[16,512]{1,0:T(8,128)(2,1)S(1)}, bf16[16,512]{1,0:T(8,128)(2,1)S(1)}, u32[]{:S(2)}, u32[]{:S(2)}) collective-permute-start(bf16[16,512]{1,0:T(8,128)(2,1)S(1)} %get-tuple-element.71), channel_id=1, source_target_pairs={{0,3},{1,2},{2,1},{3,0},{4,7},{5,6},{6,5},{7,4},{8,11},{9,10},{10,... | collective-permute-start | bytes 49160 | tf_op jit(solution)/shard_map/ppermute | solution.py:36
  3.8 3.7 %collective-permute-start = (bf16[16,512]{1,0:T(8,128)(2,1)S(1)}, bf16[16,512]{1,0:T(8,128)(2,1)S(1)}, u32[]{:S(2)}, u32[]{:S(2)}) collective-permute-start(bf16[16,512]{1,0:T(8,128)(2,1)S(1)} %get-tuple-element.71), channel_id=1, source_target_pairs={{0,1},{1,2},{2,0},{3,4},{4,3},{5,6},{6,5},{7,8},{8,7},{9,10},{10,9... | collective-permute-start | bytes 49160 | tf_op jit(solution)/shard_map/ppermute | solution.py:37
  4.5 2.3 %collective-permute-start.2 = (bf16[16,512]{1,0:T(8,128)(2,1)S(1)}, bf16[16,512]{1,0:T(8,128)(2,1)S(1)}, u32[]{:S(2)}, u32[]{:S(2)}) collective-permute-start(bf16[16,512]{1,0:T(8,128)(2,1)S(1)} %get-tuple-element.70), channel_id=1, source_target_pairs={{0,1},{1,0},{2,3},{3,2},{4,5},{5,4},{6,7},{7,6},{8,9},{9,8},{10,11... | collective-permute-start | bytes 49160 | tf_op jit(solution)/shard_map/ppermute | solution.py:20
  14.2 1.8 %collective-permute-start.3 = (bf16[64,1152]{1,0:T(8,128)(2,1)S(1)}, bf16[64,1152]{1,0:T(8,128)(2,1)S(1)}, u32[]{:S(2)}, u32[]{:S(2)}) collective-permute-start(bf16[64,1152]{1,0:T(8,128)(2,1)S(1)} %get-tuple-element.41.refs_0_), channel_id=1, source_target_pairs={{0,1},{1,0},{2,3},{3,2},{4,5},{5,4},{6,7},{7,6},{8,9},{9,8},{10,11... | collective-permute-start | bytes 442376 | tf_op jit(solution)/shard_map/ppermute | solution.py:20
  14.3 6.3 %collective-permute-start.4 = (bf16[64,1152]{1,0:T(8,128)(2,1)S(1)}, bf16[64,1152]{1,0:T(8,128)(2,1)S(1)}, u32[]{:S(2)}, u32[]{:S(2)}) collective-permute-start(bf16[64,1152]{1,0:T(8,128)(2,1)S(1)} %get-tuple-element.41.refs_0_), channel_id=1, source_target_pairs={{0,2},{1,3},{2,0},{3,1},{4,6},{5,7},{6,4},{7,5},{8,10},{9,11},{10,... | collective-permute-start | bytes 442376 | tf_op jit(solution)/shard_map/ppermute | solution.py:20
  20.5 1.4 %collective-permute-start.5 = (bf16[64,1152]{1,0:T(8,128)(2,1)S(1)}, bf16[64,1152]{1,0:T(8,128)(2,1)S(1)}, u32[]{:S(2)}, u32[]{:S(2)}) collective-permute-start(bf16[64,1152]{1,0:T(8,128)(2,1)S(1)} %collective-permute-done.4.refs_0_.refs_3_), channel_id=1, source_target_pairs={{0,1},{1,0},{2,3},{3,2},{4,5},{5,4},{6,7},{7,6},{8,9},{9,8},{10,11... | collective-permute-start | bytes 442376 | tf_op jit(solution)/shard_map/ppermute | solution.py:20
  22.6 4.7 %collective-permute-start.6 = (bf16[288,128]{1,0:T(8,128)(2,1)S(1)}, bf16[288,128]{1,0:T(8,128)(2,1)S(1)}, u32[]{:S(2)}, u32[]{:S(2)}) collective-permute-start(bf16[288,128]{1,0:T(8,128)(2,1)S(1)} %get-tuple-element.55), channel_id=1, source_target_pairs={{0,4},{4,0},{8,12},{12,8},{16,20},{20,16},{24,28},{28,24},{1,5},{5... | collective-permute-start | bytes 221192 | tf_op jit(solution)/shard_map/ppermute | solution.py:20
  27.4 5.0 %collective-permute-start.7 = (bf16[288,128]{1,0:T(8,128)(2,1)S(1)}, bf16[288,128]{1,0:T(8,128)(2,1)S(1)}, u32[]{:S(2)}, u32[]{:S(2)}) collective-permute-start(bf16[288,128]{1,0:T(8,128)(2,1)S(1)} %get-tuple-element.58), channel_id=1, source_target_pairs={{0,8},{4,12},{8,0},{12,4},{16,24},{20,28},{24,16},{28,20},{1,9},{5... | collective-permute-start | bytes 221192 | tf_op jit(solution)/shard_map/ppermute | solution.py:20
  32.5 5.4 %collective-permute-start.8 = (bf16[288,128]{1,0:T(8,128)(2,1)S(1)}, bf16[288,128]{1,0:T(8,128)(2,1)S(1)}, u32[]{:S(2)}, u32[]{:S(2)}) collective-permute-start(bf16[288,128]{1,0:T(8,128)(2,1)S(1)} %get-tuple-element.60), channel_id=1, source_target_pairs={{0,16},{4,20},{8,24},{12,28},{16,0},{20,4},{24,8},{28,12},{1,17},{... | collective-permute-start | bytes 221192 | tf_op jit(solution)/shard_map/ppermute | solution.py:20
  37.9 4.3 %collective-permute-start.9 = (bf16[256,128]{1,0:T(8,128)(2,1)S(1)}, bf16[256,128]{1,0:T(8,128)(2,1)S(1)}, u32[]{:S(2)}, u32[]{:S(2)}) collective-permute-start(bf16[256,128]{1,0:T(8,128)(2,1)S(1)} %get-tuple-element.67), channel_id=1, source_target_pairs={{0,4},{4,0},{8,12},{12,8},{16,20},{20,16},{24,28},{28,24},{1,5},{5... | collective-permute-start | bytes 196616 | tf_op jit(solution)/shard_map/ppermute | solution.py:20

commit v5 on v4

--- a/solution.py
+++ b/solution.py
@@ -8,6 +8,7 @@
 from jax.sharding import PartitionSpec as P
 
 HALO = 16
+ENDS = 16
 LANES = 128
 F32 = jnp.float32
 BF16 = jnp.bfloat16
@@ -117,11 +118,11 @@
     return points, after
 
 
-def half_sum(half, piece, diff, lead, rest, lhs):
+def half_sum(owner, half, piece, diff, lead, rest, lhs):
     width, padded = piece.shape
     length = padded - LANES
     row_count = 4 * lhs.shape[1] // width
-    first_row = pl.multiple_of(lax.axis_index("narrow") * row_count, row_count)
+    first_row = pl.multiple_of(owner * row_count, row_count)
     group = max(1, 16 // row_count)
     span = 2 * LANES
     sums = []
@@ -144,35 +145,51 @@
     return lax.rem(lax.axis_index("wide"), 2)
 
 
-def given_kernel(masks, started, ended, *refs):
-    before, refs = refs[: 3 * started], refs[3 * started :]
-    pieces, refs = refs[: len(masks)], refs[len(masks) :]
-    (given, second, ends, extra), (diff, lead, rest, lhs) = refs[:4], refs[-4:]
-    kept_total = None
-    values = [ref[...] for ref in before]
-    for mask, piece in zip(masks, pieces):
-        width, padded = piece.shape
-        length = padded - LANES
-        points, after = coefficients(piece, diff, lead, rest)
-        if mask == 0:
-            extra[...] = after.astype(BF16)
-        crossed = lax.dot_general(after.astype(BF16), piece[:, :length], NT, preferred_element_type=F32)
-        is_last = jnp.bitwise_xor(lax.axis_index("narrow"), mask) == lax.axis_size("narrow") - 1
-        final = jnp.broadcast_to(points[:, length : length + 1], (width, LANES))
-        previous = jnp.broadcast_to(points[:, length - 1 : length], (width, LANES))
-        lane = lax.broadcasted_iota(jnp.int32, (width, LANES), 1)
-        end_points = jnp.where(is_last, jnp.where(lane == 0, final, previous), 0.0)
-        more = [half_sum(1 - parity(), piece, diff, lead, rest, lhs), folded(crossed), end_points]
-        values = [value + other for value, other in zip(values, more)] if values else more
-        if not started:
-            kept = half_sum(parity(), piece, diff, lead, rest, lhs)
-            kept_total = kept if kept_total is None else kept_total + kept
-    if not started:
-        refs[4][...] = kept_total
-    for target, value in zip((given, second, ends), values):
-        target[...] = value
-    if ended:
-        pack(extra, values[0], values[1])
+def target_sum(target, *refs):
+    across, mask = target
+    owner = jnp.bitwise_xor(lax.axis_index("narrow"), mask)
+    return half_sum(owner, 1 - parity() if across else parity(), *refs)
+
+
+def besides(mask, piece, points, after):
+    width, padded = piece.shape
+    length = padded - LANES
+    crossed = lax.dot_general(after.astype(BF16), piece[:, :length], NT, preferred_element_type=F32)
+    lane = lax.broadcasted_iota(jnp.int32, (width, LANES), 1)
+    final = jnp.broadcast_to(points[:, length : length + 1], (width, LANES))
+    previous = jnp.broadcast_to(points[:, length - 1 : length], (width, LANES))
+    rows = jnp.where(lane == 0, final, previous).T
+    row = jnp.concatenate([rows[0:1, :], rows[1:2, :]], axis=1)
+    is_last = jnp.bitwise_xor(lax.axis_index("narrow"), mask) == lax.axis_size("narrow") - 1
+    first = lax.broadcasted_iota(jnp.int32, (ENDS, LANES), 0) == 0
+    return folded(crossed), jnp.where(jnp.logical_and(is_last, first), row, 0.0)
+
+
+def own_kernel(targets, piece, path, second, ends, *refs):
+    sums, (diff, lead, rest, lhs) = refs[: len(targets)], refs[len(targets) :]
+    points, after = coefficients(piece, diff, lead, rest)
+    path[...] = after.astype(BF16)
+    second[...], ends[...] = besides(0, piece, points, after)
+    for target, total in zip(targets, sums):
+        total[...] = target_sum(target, piece, diff, lead, rest, lhs)
+
+
+def mate_kernel(targets, piece, second, ends, *refs):
+    count = len(targets)
+    sums, (chip_second, chip_ends), messages, scratch = refs[:count], refs[count : count + 2], refs[count + 2 : -4], refs[-4:]
+    diff, lead, rest, lhs = scratch
+    points, after = coefficients(piece, diff, lead, rest)
+    more_second, more_ends = besides(1, piece, points, after)
+    both_second, both_ends = second[...] + more_second, ends[...] + more_ends
+    chip_second[...] = both_second
+    chip_ends[...] = both_ends
+    for target, before, message in zip(targets, sums, messages):
+        pack(message, before[...] + target_sum(target, piece, diff, lead, rest, lhs), both_second, both_ends)
+
+
+def kept_kernel(piece, before, total, diff, lead, rest, lhs):
+    coefficients(piece, diff, lead, rest)
+    total[...] = before[...] + target_sum((0, 0), piece, diff, lead, rest, lhs)
 
 
 def folded(crossed):
@@ -201,35 +218,53 @@
     )
 
 
-def kept_kernel(before, *refs):
-    pieces, (kept, diff, lead, rest, lhs) = refs[:-5], refs[-5:]
-    total = before[...]
-    for piece in pieces:
-        coefficients(piece, diff, lead, rest)
-        total = total + half_sum(parity(), piece, diff, lead, rest, lhs)
-    kept[...] = total
-
-
-def pack(sent, total, doubled):
-    count = total.shape[0]
+def pack(sent, total, doubled, ends=None):
+    count, rows = total.shape[0], doubled.shape[0]
     high = doubled.astype(BF16).astype(F32)
     lane = lax.broadcasted_iota(jnp.int32, doubled.shape, 1)
     sent[:count, :] = total.astype(BF16)
-    sent[count:, :] = jnp.where(lane < LANES // 2, high, doubled - high).astype(BF16)
-
-
-def unpack(received, count):
-    coded = received[count:, :].astype(F32)
+    sent[count : count + rows, :] = jnp.where(lane < LANES // 2, high, doubled - high).astype(BF16)
+    if ends is not None:
+        sent[count + rows :, :] = ends.astype(BF16)
+
+
+def unpack(received, count, rows):
+    coded = received[count : count + rows, :].astype(F32)
     return received[:count, :].astype(F32), coded + pltpu.roll(coded, LANES // 2, 1)
 
 
-def pair_kernel(kept, second, received, pair_third, pair_second, sent):
-    more_third, more_second = unpack(received, kept.shape[0])
-    total = kept[...] + more_third
-    doubled = second[...] + more_second
-    pair_third[...] = total
+def reduce_kernel(targets, kept, chip_second, chip_ends, *refs):
+    parts, refs = refs[: len(targets)], refs[len(targets) :]
+    own, other, own_second, other_second, pair, pair_second, ends, sent = refs
+    count, rows = kept.shape[0], chip_second.shape[0]
+    sums = [[kept[...], chip_second[...]], None]
+    last = chip_ends[...]
+    for (across, _), part in zip(targets, parts):
+        more = unpack(part, count, rows)
+        sums[across] = [a + b for a, b in zip(sums[across], more)] if sums[across] else more
+        if not across:
+            last = last + part[count + rows :, :].astype(F32)
+    own[...], own_second[...] = sums[0]
+    other[...], other_second[...] = sums[1]
+    total, doubled = sums[0][0] + sums[1][0], sums[0][1] + sums[1][1]
+    pair[...] = total
     pair_second[...] = doubled
+    ends[...] = last
     pack(sent, total, doubled)
+
+
+def ends_kernel(scale, ends, level_one, x_twice, pairs, factor):
+    width = pairs.shape[0]
+    x_row, a_row = ends[0:1, :width], ends[0:1, width:]
+    x_across = jnp.broadcast_to(x_row, (width, width))
+    a_across = jnp.broadcast_to(a_row, (width, width))
+    x_down, a_down = x_across.T, a_across.T
+    xx = x_down * x_across
+    edge = a_down * x_across - a_down * a_across - 2.0 * x_down * a_across
+    level_one[...] = scale * x_row
+    x_twice[...] = jnp.concatenate([x_row, x_row], axis=1)
+    pairs[:, :width] = 0.5 * xx
+    factor[:, :width] = 0.5 * xx - edge / 6.0 - xx / 3.0
 
 
 def is_later(distance):
@@ -239,7 +274,7 @@
 def scan_kernel(distance, started, ended, *refs):
     before, refs = refs[: 2 * started], refs[2 * started :]
     group_third, group_second, received, third, second, sent = refs[:6]
-    more_third, more_second = unpack(received, group_third.shape[0])
+    more_third, more_second = unpack(received, group_third.shape[0], group_second.shape[0])
     total, doubled = group_third[...] + more_third, group_second[...] + more_second
     pack(sent, total, doubled)
     earlier_third = jnp.where(is_later(distance), more_third, 0.0)
@@ -253,56 +288,48 @@
         refs[7][...] = doubled
 
 
-def return_kernel(distance, third, received, kept, earlier, sent):
+def return_kernel(distance, third, received, own, other, earlier, sent):
     count = third.shape[0]
     total = third[...] + jnp.where(is_later(distance), received[:count, :].astype(F32), 0.0)
     earlier[...] = total
-    sent[...] = jnp.where(parity() == 0, total + kept[...], total).astype(BF16)
-
-
-def products(result, half, factor, x_twice, total):
+    sent[...] = (total + other[...] + jnp.where(parity() == 0, own[...], 0.0)).astype(BF16)
+
+
+def products(result, half, factor, x_twice, total=None):
     row_count, width = factor.shape
     lane = lax.broadcasted_iota(jnp.int32, (row_count, LANES), 1)
     factor = jnp.where(half == 0, factor[:, : width // 2], factor[:, width // 2 :])
     for at in range(width // 4):
         low = jnp.broadcast_to(factor[:, 2 * at : 2 * at + 1], (row_count, LANES))
         high = jnp.broadcast_to(factor[:, 2 * at + 1 : 2 * at + 2], (row_count, LANES))
-        result[:, at * LANES : (at + 1) * LANES] = (
-            jnp.where(lane < width, low, high) * x_twice - total[at * row_count : (at + 1) * row_count, :]
-        )
+        value = jnp.where(lane < width, low, high) * x_twice
+        if total is not None:
+            value = value - total[at * row_count : (at + 1) * row_count, :]
+        result[:, at * LANES : (at + 1) * LANES] = value
 
 
 def levels_kernel(
-    scale, row_count, distance, second, received, own_second, pair_second, ends, earlier, kept, pair_third, given,
-    level_one, level_two, partly, rest, held, own_half, sem,
+    scale, row_count, distance, second, received, own_second, other_second, earlier, own, other, x_twice, pairs, factor,
+    level_two, partly, rest, held, own_half, sem,
 ):
-    width = ends.shape[0]
-    count = received.shape[0] - second.shape[0]
+    width = pairs.shape[0]
+    count, rows = own.shape[0], second.shape[0]
     is_first = parity() == 0
-    end_cols = ends[...]
-    end_rows = end_cols.T
-    x_col, a_col = end_cols[:, 0:1], end_cols[:, 1:2]
-    x_row, a_row = end_rows[0:1, :], end_rows[1:2, :]
-    xx = x_col * x_row
-    edge = a_col * x_row - a_col * a_row - 2.0 * x_col * a_row
-    coded = jnp.where(is_later(distance), received[count:, :].astype(F32), 0.0)
+    coded = jnp.where(is_later(distance), received[count : count + rows, :].astype(F32), 0.0)
     upper = second[...] + coded + pltpu.roll(coded, LANES // 2, 1)
-    upper = upper + jnp.where(is_first, own_second[...], pair_second[...])
-    pairs = 0.5 * xx + 0.5 * unfolded(upper)
-    factor = pairs - edge / 6.0 - xx / 3.0
-    level_one[...] = scale * x_row
-    held[:, :width] = scale**3 * factor
+    upper = upper + own_second[...] + jnp.where(is_first, 0.0, other_second[...])
+    turned = 0.5 * unfolded(upper)
+    held[:, :width] = scale**3 * (factor[:, :width] + turned)
     first_row = pl.multiple_of(lax.axis_index("narrow") * row_count, row_count)
-    own = held[pl.ds(first_row, row_count), :width]
-    twice = jnp.concatenate([x_row, x_row], axis=1)
-    total = (earlier[...] + jnp.where(is_first, kept[...], pair_third[...])) * (scale**3 / 6.0)
-    products(own_half, parity(), own, twice, total)
+    own_factor = held[pl.ds(first_row, row_count), :width]
+    total = earlier[...] + own[...] + jnp.where(is_first, 0.0, other[...])
+    products(own_half, parity(), own_factor, x_twice[...], total * (scale**3 / 6.0))
     size = own_half.shape[1]
     at = pl.multiple_of(parity() * size, size)
     copy = pltpu.make_async_copy(own_half, partly.at[:, pl.ds(at, size)], sem)
     copy.start()
-    products(rest, 1 - parity(), own, twice, given[...] * (scale**3 / 6.0))
-    held[:, :width] = scale**2 * pairs
+    products(rest, 1 - parity(), own_factor, x_twice[...])
+    held[:, :width] = scale**2 * (pairs[:, :width] + turned)
     level_two[:, :width] = held[pl.ds(0, width // 2, stride=2), :width]
     level_two[:, width:] = held[pl.ds(1, width // 2, stride=2), :width]
     copy.wait()
@@ -389,45 +416,48 @@
     piece = path_of(recording, conv_weight, conv_bias, projection)
 
     half, square, folds = ((count, LANES), F32), ((width, LANES), F32), ((width // 2, LANES), F32)
+    last = ((ENDS, LANES), F32)
     message = ((count + width // 2, LANES), BF16)
-
     scratch = [pltpu.VMEM((width, length), F32)] * 3 + [pltpu.VMEM((2, count, length), BF16)]
     share = 10**9 // 2
-    pieces = {0: piece, 1: exchanged(piece, "narrow", 1)}
-    distance = narrow_size // 2
-    arrived = {}
-    while distance > 1:
-        for mask, held in [(0, piece)] + sorted(arrived.items()):
-            arrived[mask ^ distance] = exchanged(held, "narrow", distance)
-        distance //= 2
-    *sums, points, kept = call(
-        functools.partial(given_kernel, (0, 1), False, False),
-        "given",
-        [half, folds, square, ((width, length), BF16), half],
+
+    mate = exchanged(piece, "narrow", 1)
+    targets = [(across, mask) for across in (1, 0) for mask in range(narrow_size - 2, -1, -2)][:-1]
+    points, chip_second, chip_ends, own, *sums = call(
+        functools.partial(own_kernel, [(0, 0)] + targets),
+        "own",
+        [((width, length), BF16), folds, last] + [half] * (1 + len(targets)),
         scratch=scratch,
-        flops=4 * share,
-    )(piece, pieces[1])
-    sums, arrived = lax.optimization_barrier((sums, arrived))
-    for mask, held in sorted(arrived.items()):
-        pieces[mask], pieces[mask ^ 1] = held, exchanged(held, "narrow", 1)
-    masks = sorted(arrived) + [mask ^ 1 for mask in sorted(arrived)]
-    for mask in masks:
-        *sums, sent = call(
-            functools.partial(given_kernel, (mask,), True, mask == masks[-1]),
-            "given",
-            [half, folds, square, message],
-            scratch=scratch,
-            flops=share,
-        )(*sums, pieces[mask])
-    given, second, ends = sums
-    received = exchanged(sent, "wide", 1)
-    (kept,) = call(kept_kernel, "kept", [half], scratch=scratch, flops=share * len(masks))(
-        kept, *[pieces[mask] for mask in masks]
-    )
-    pair_third, pair_second, sent = call(pair_kernel, "pair", [half, folds, message])(kept, second, received)
+        flops=share * (1 + len(targets)),
+    )(piece)
+    chip_second, chip_ends, *messages = call(
+        functools.partial(mate_kernel, targets),
+        "mate",
+        [folds, last] + [((count + width // 2 + ENDS, LANES), BF16)] * len(targets),
+        scratch=scratch,
+        flops=share * len(targets),
+    )(mate, chip_second, chip_ends, *sums)
+    size = wide_size * narrow_size
+    parts = []
+    for (across, mask), sent in zip(targets, messages):
+        flip = across * narrow_size + mask
+        parts.append(lax.ppermute(sent, WHOLE, [(i, i ^ flip) for i in range(size)]))
+    (kept,) = call(kept_kernel, "kept", [half], scratch=scratch, flops=share)(mate, own)
+    own, other, own_second, other_second, group_third, group_second, ends, sent = call(
+        functools.partial(reduce_kernel, targets),
+        "reduce",
+        [half, half, folds, folds, half, folds, last, message],
+    )(kept, chip_second, chip_ends, *parts)
+    level_one, x_twice, pairs, factor = call(
+        functools.partial(ends_kernel, scale),
+        "ends",
+        [((1, width), F32), ((1, LANES), F32), square, square],
+        flops=share,
+    )(ends)
+
+    earlier = ()
     distance = 2
     received = exchanged(sent, "wide", distance)
-    earlier, group_third, group_second = (), pair_third, pair_second
     while 2 * distance < wide_size:
         ended = 4 * distance >= wide_size
         *earlier, sent = call(
@@ -443,20 +473,20 @@
     if not earlier:
         earlier = [jnp.zeros(dims, dtype) for dims, dtype in (half, folds)]
     total, sent = call(functools.partial(return_kernel, distance), "back", [half, ((count, LANES), BF16)])(
-        earlier[0], received, kept
+        earlier[0], received, own, other
     )
     returned = exchanged(sent, "wide", 1)
     own_size = width * width // 2
     third_shape = ((row_count, 2 * own_size), F32)
     half_buffer = ((row_count, own_size), F32)
-    level_one, level_two, partly, rest = call(
+    level_two, partly, rest = call(
         functools.partial(levels_kernel, scale, row_count, distance),
         "levels",
-        [((1, width), F32), folds, third_shape, half_buffer],
+        [folds, third_shape, half_buffer],
         scratch=[pltpu.VMEM((width, LANES), F32), pltpu.VMEM(half_buffer[0], F32), pltpu.SemaphoreType.DMA],
-        out_specs=(VMEM, VMEM, HBM, VMEM),
+        out_specs=(VMEM, HBM, VMEM),
         flops=10**9,
-    )(earlier[1], received, second, pair_second, ends, total, kept, pair_third, given)
+    )(earlier[1], received, own_second, other_second, total, own, other, x_twice, pairs, factor)
     (level_three,) = call(
         functools.partial(finish_kernel, scale, row_count),
         "finish",

time: 43.3 us -> 41.1 us (0.949)
  waiting for transfers between devices: 11 us -> 8.84 us
  Pallas kernels: 16.8 us -> 16.1 us
  starting transfers between devices: 13.7 us -> 14.3 us
    ppermute x8 -> x5, waiting for transfers between devices: 10.2 us -> 5.03 us  [exchanged(): return lax.ppermute(array, axis, [(i, i ^ distance) for i in range(size)])]
    ppermute x0 -> x3, starting transfers between devices: none -> 4.03 us  [per_device(): lax.ppermute(sent, WHOLE, [(i, i ^ flip) for i in range(size)])]
    ppermute x8 -> x5, starting transfers between devices: 10.6 us -> 7.21 us  [exchanged(): return lax.ppermute(array, axis, [(i, i ^ distance) for i in range(size)])]
    ppermute x0 -> x3, waiting for transfers between devices: none -> 3.06 us  [per_device(): lax.ppermute(sent, WHOLE, [(i, i ^ flip) for i in range(size)])]
    pallas_call x11, Pallas kernels: 16.8 us -> 16.1 us  [run(): pl.pallas_call(kernel, out_shape=tuple(shapes), in_specs=in_specs or [VME...]
  transfers between devices with their start and end apart: 10 -> 10, of which waited for: 7 -> 6; matrix products, arithmetic and copies ran while one was open for 0% -> 0% of each run, Pallas kernels for 20% -> 18%
where the time goes in v5:
time: 41.1 us; the launch traced here: 40.8 us
  Pallas kernels  16.1 us (39%)
  starting transfers between devices  14.3 us (35%)
  waiting for transfers between devices  8.84 us (22%)
  local copies, waits for them, and re-layouts  0.74 us (2%)
  between operations  0.73 us (2%)
    pallas_call x11, Pallas kernels, run(): pl.pallas_call(kernel, out_shape=tuple(shapes), in_specs=in_specs or [VME...  16.1 us
    ppermute x5, starting transfers between devices, exchanged(): return lax.ppermute(array, axis, [(i, i ^ distance) for i in range(size)])  7.21 us
    ppermute x5, waiting for transfers between devices, exchanged(): return lax.ppermute(array, axis, [(i, i ^ distance) for i in range(size)])  5.03 us
    ppermute x3, starting transfers between devices, per_device(): lax.ppermute(sent, WHOLE, [(i, i ^ flip) for i in range(size)])  4.03 us
    ppermute x3, waiting for transfers between devices, per_device(): lax.ppermute(sent, WHOLE, [(i, i ^ flip) for i in range(size)])  3.06 us
    ppermute x1, starting transfers between devices, edges_exchanged(): inside = lax.ppermute(outer, 'narrow', list(inside.items()))  2.41 us
  transfers between devices with their start and end apart: 10, of which 6 were waited for; matrix products, arithmetic and copies ran while one was open for 0% of the time, Pallas kernels for 18%

profile of v5, /device:TPU:0, one launch (start us, length us, event | category | flops | bytes accessed | tf_op | source)
XLA Modules:
  0.0 40.8 jit_solution(6812916341618687574)
XLA Ops:
  0.7 0.7 %constant_dynamic-slice_fusion = (bf16[16,512]{1,0:T(8,128)(2,1)S(1)}, bf16[16,512]{1,0:T(8,128)(2,1)S(1)}) fusion(bf16[1024,512]{1,0:T(8,128)(2,1)} %rec_hbm.1, s32[]{:T(128)S(6)} %select_n.15, s32[]{:T(128)S(6)} %select_n.14), kind=kLoop, calls=%fused_computation | loop fusion | bytes 65544 | tf_op jit(solution)/shard_map/dynamic_slice | solution.py:28
  1.4 2.4 %collective-permute-start.1 = (bf16[16,512]{1,0:T(8,128)(2,1)S(1)}, bf16[16,512]{1,0:T(8,128)(2,1)S(1)}, u32[]{:S(2)}, u32[]{:S(2)}) collective-permute-start(bf16[16,512]{1,0:T(8,128)(2,1)S(1)} %get-tuple-element.79), channel_id=1, source_target_pairs={{0,3},{1,2},{2,1},{3,0},{4,7},{5,6},{6,5},{7,4},{8,11},{9,10},{10,... | collective-permute-start | bytes 49160 | tf_op jit(solution)/shard_map/ppermute | solution.py:37
  3.8 0.7 %collective-permute-start = (bf16[16,512]{1,0:T(8,128)(2,1)S(1)}, bf16[16,512]{1,0:T(8,128)(2,1)S(1)}, u32[]{:S(2)}, u32[]{:S(2)}) collective-permute-start(bf16[16,512]{1,0:T(8,128)(2,1)S(1)} %get-tuple-element.79), channel_id=1, source_target_pairs={{0,1},{1,2},{2,0},{3,4},{4,3},{5,6},{6,5},{7,8},{8,7},{9,10},{10,9... | collective-permute-start | bytes 49160 | tf_op jit(solution)/shard_map/ppermute | solution.py:38
  4.5 0.0 collective-permute-start.2
  4.5 2.3 %load.1 = (f32[1072,512]{1,0:T(8,128)S(1)}, bf16[2,3,512,512]{3,2,1,0:T(8,128)(2,1)S(1)}, f32[3,512]{1,0:T(4,128)S(1)}, bf16[64,512]{1,0:T(8,128)(2,1)S(1)}) custom-call(bf16[1024,512]{1,0:T(8,128)(2,1)} %rec_hbm.1, bf16[3,3,512,512]{3,2,1,0:T(8,128)(2,1)} %weights_hbm.3, f32[3,512]{1,0:T(4,128)} %bias_hbm.1, bf16[64,512]{1,0:T(8,128)(2,1)} %bitcast.5), custom_call_target="tpu_custom_call" | custom-call | flops 1000000000 | bytes 5835776 | tf_op jit(solution)/shard_map/load/pallas_call | solution.py:358
  6.8 0.0 collective-permute-done.2.inner
  6.8 0.0 collective-permute-done.1.inside
  6.8 0.7 %collective-permute-done.over = bf16[16,512]{1,0:T(8,128)(2,1)S(1)} collective-permute-done((bf16[16,512]{1,0:T(8,128)(2,1)S(1)}, bf16[16,512]{1,0:T(8,128)(2,1)S(1)}, u32[]{:S(2)}, u32[]{:S(2)}) %collective-permute-start) | collective-permute-done | bytes 16416 | tf_op jit(solution)/shard_map/ppermute | solution.py:38
  7.5 6.6 %conv.1 = (bf16[64,1152]{1,0:T(8,128)(2,1)S(1)}, f32[1072,512]{1,0:T(8,128)S(1)}) custom-call(f32[1072,512]{1,0:T(8,128)S(1)} %get-tuple-element.41._, bf16[16,512]{1,0:T(8,128)(2,1)S(1)} %collective-permute-done.over, bf16[16,512]{1,0:T(8,128)(2,1)S(1)} %collective-permute-done.1.inside, ...), custom_call_target="tpu_custom_call", output_to_operand_aliasing={{1}: (0, {})} | custom-call | flops 4831838208 | bytes 4718592 | tf_op jit(solution)/shard_map/conv/pallas_call | solution.py:358
  14.2 0.1 collective-permute-start.3
  14.3 2.0 %own.1 = (bf16[64,1024]{1,0:T(8,128)(2,1)}, f32[32,128]{1,0:T(8,128)S(1)}, f32[16,128]{1,0:T(8,128)S(1)}, f32[256,128]{1,0:T(8,128)S(1)}, f32[256,128]{1,0:T(8,1...) custom-call(bf16[64,1152]{1,0:T(8,128)(2,1)S(1)} %get-tuple-element.45.piece), custom_call_target="tpu_custom_call" | custom-call | flops 2000000000 | tf_op jit(solution)/shard_map/own/pallas_call | solution.py:358
  16.3 0.0 collective-permute-done.3.piece
  16.3 1.3 %mate.1 = (f32[32,128]{1,0:T(8,128)S(1)}, f32[16,128]{1,0:T(8,128)S(1)}, bf16[304,128]{1,0:T(8,128)(2,1)S(1)}, bf16[304,128]{1,0:T(8,128)(2,1)S(1)}, bf16[304,128]{1,0:T(8,128)(2,1)S(1)}) custom-call(bf16[64,1152]{1,0:T(8,128)(2,1)S(1)} %collective-permute-done.3.piece, f32[32,128]{1,0:T(8,128)S(1)} %get-tuple-element.48.second, ...), custom_call_target="tpu_custom_call" | custom-call | flops 1500000000 | tf_op jit(solution)/shard_map/mate/pallas_call | solution.py:358
  17.5 3.4 %collective-permute-start.4 = (bf16[304,128]{1,0:T(8,128)(2,1)S(1)}, bf16[304,128]{1,0:T(8,128)(2,1)S(1)}, u32[]{:S(2)}, u32[]{:S(2)}) collective-permute-start(bf16[304,128]{1,0:T(8,128)(2,1)S(1)} %get-tuple-element.55), channel_id=1, source_target_pairs={{0,6},{1,7},{2,4},{3,5},{4,2},{5,3},{6,0},{7,1},{8,14},{9,15},{10,... | collective-permute-start | bytes 233480 | tf_op jit(solution)/shard_map/ppermute | solution.py:444
  20.9 0.0 collective-permute-start.5
  20.9 0.6 %collective-permute-start.6 = (bf16[304,128]{1,0:T(8,128)(2,1)S(1)}, bf16[304,128]{1,0:T(8,128)(2,1)S(1)}, u32[]{:S(2)}, u32[]{:S(2)}) collective-permute-start(bf16[304,128]{1,0:T(8,128)(2,1)S(1)} %get-tuple-element.57), channel_id=1, source_target_pairs={{0,2},{1,3},{2,0},{3,1},{4,6},{5,7},{6,4},{7,5},{8,10},{9,11},{10,... | collective-permute-start | bytes 233480 | tf_op jit(solution)/shard_map/ppermute | solution.py:444
  21.6 0.7 %kept.1 = f32[256,128]{1,0:T(8,128)S(1)} custom-call(bf16[64,1152]{1,0:T(8,128)(2,1)S(1)} %collective-permute-done.3.piece, f32[256,128]{1,0:T(8,128)S(1)} %get-tuple-element.47.before), custom_call_target="tpu_custom_call" | custom-call | flops 500000000 | tf_op jit(solution)/shard_map/kept/pallas_call | solution.py:358
  22.3 1.5 %collective-permute-done.4.refs_0_ = bf16[304,128]{1,0:T(8,128)(2,1)S(1)} collective-permute-done((bf16[304,128]{1,0:T(8,128)(2,1)S(1)}, bf16[304,128]{1,0:T(8,128)(2,1)S(1)}, u32[]{:S(2)}, u32[]{:S(2)}) %collective-permute-start.4) | collective-permute-done | bytes 77856 | tf_op jit(solution)/shard_map/ppermute | solution.py:444
  23.8 1.6 %collective-permute-done.5.refs_1_ = bf16[304,128]{1,0:T(8,128)(2,1)S(1)} collective-permute-done((bf16[304,128]{1,0:T(8,128)(2,1)S(1)}, bf16[304,128]{1,0:T(8,128)(2,1)S(1)}, u32[]{:S(2)}, u32[]{:S(2)}) %collective-permute-start.5) | collective-permute-done | bytes 77856 | tf_op jit(solution)/shard_map/ppermute | solution.py:444
  25.3 0.0 collective-permute-done.6.refs_2_
  25.3 0.1 reduce.1
  25.4 2.4 %collective-permute-start.7 = (bf16[288,128]{1,0:T(8,128)(2,1)S(1)}, bf16[288,128]{1,0:T(8,128)(2,1)S(1)}, u32[]{:S(2)}, u32[]{:S(2)}) collective-permute-start(bf16[288,128]{1,0:T(8,128)(2,1)S(1)} %get-tuple-element.62), channel_id=1, source_target_pairs={{0,8},{4,12},{8,0},{12,4},{16,24},{20,28},{24,16},{28,20},{1,9},{5... | collective-permute-start | bytes 221192 | tf_op jit(solution)/shard_map/ppermute | solution.py:21
  27.9 2.3 %collective-permute-done.7.refs_2_ = bf16[288,128]{1,0:T(8,128)(2,1)S(1)} collective-permute-done((bf16[288,128]{1,0:T(8,128)(2,1)S(1)}, bf16[288,128]{1,0:T(8,128)(2,1)S(1)}, u32[]{:S(2)}, u32[]{:S(2)}) %collective-permute-start.7) | collective-permute-done | bytes 73760 | tf_op jit(solution)/shard_map/ppermute | solution.py:21
  30.2 0.1 scan.1
  30.3 3.1 %collective-permute-start.8 = (bf16[288,128]{1,0:T(8,128)(2,1)S(1)}, bf16[288,128]{1,0:T(8,128)(2,1)S(1)}, u32[]{:S(2)}, u32[]{:S(2)}) collective-permute-start(bf16[288,128]{1,0:T(8,128)(2,1)S(1)} %get-tuple-element.64), channel_id=1, source_target_pairs={{0,16},{4,20},{8,24},{12,28},{16,0},{20,4},{24,8},{28,12},{1,17},{... | collective-permute-start | bytes 221192 | tf_op jit(solution)/shard_map/ppermute | solution.py:21
  33.4 0.5 %ends.1 = (f32[1,64]{1,0:T(1,128)}, f32[1,128]{1,0:T(1,128)S(1)}, f32[64,128]{1,0:T(8,128)S(1)}, f32[64,128]{1,0:T(8,128)S(1)}) custom-call(f32[16,128]{1,0:T(8,128)S(1)} %get-tuple-element.58.ends), custom_call_target="tpu_custom_call" | custom-call | flops 500000000 | tf_op jit(solution)/shard_map/ends/pallas_call | solution.py:358
  33.9 1.8 %collective-permute-done.8.received = bf16[288,128]{1,0:T(8,128)(2,1)S(1)} collective-permute-done((bf16[288,128]{1,0:T(8,128)(2,1)S(1)}, bf16[288,128]{1,0:T(8,128)(2,1)S(1)}, u32[]{:S(2)}, u32[]{:S(2)}) %collective-permute-start.8) | collective-permute-done | bytes 73760 | tf_op jit(solution)/shard_map/ppermute | solution.py:21
  35.7 1.6 %collective-permute-start.9 = (bf16[256,128]{1,0:T(8,128)(2,1)S(1)}, bf16[256,128]{1,0:T(8,128)(2,1)S(1)}, u32[]{:S(2)}, u32[]{:S(2)}) collective-permute-start(bf16[256,128]{1,0:T(8,128)(2,1)S(1)} %get-tuple-element.75), channel_id=1, source_target_pairs={{0,4},{4,0},{8,12},{12,8},{16,20},{20,16},{24,28},{28,24},{1,5},{5... | collective-permute-start | bytes 196616 | tf_op jit(solution)/shard_map/ppermute | solution.py:21
  37.3 1.8 %levels.1 = (f32[32,128]{1,0:T(8,128)}, f32[16,4096]{1,0:T(8,128)}, f32[16,2048]{1,0:T(8,128)S(1)}) custom-call(f32[32,128]{1,0:T(8,128)S(1)} %get-tuple-element.63.second, bf16[288,128]{1,0:T(8,128)(2,1)S(1)} %collective-permute-done.8.received, f32[32,128]{1,0:T(8,128)S(1)} %get-tuple-element.65.own_second, f32[32,128]{1,0:T(8,128)S(1)} %get-tuple-element.66.other_second, ...), custom_call_target="tpu_custom_call" | custom-call | flops 1000000000 | tf_op jit(solution)/shard_map/levels/pallas_call | solution.py:358
  39.2 0.9 %collective-permute-done.9.received = bf16[256,128]{1,0:T(8,128)(2,1)S(1)} collective-permute-done((bf16[256,128]{1,0:T(8,128)(2,1)S(1)}, bf16[256,128]{1,0:T(8,128)(2,1)S(1)}, u32[]{:S(2)}, u32[]{:S(2)}) %collective-permute-start.9) | collective-permute-done | bytes 65568 | tf_op jit(solution)/shard_map/ppermute | solution.py:21
  40.1 0.7 %finish.1 = f32[16,4096]{1,0:T(8,128)} custom-call(bf16[256,128]{1,0:T(8,128)(2,1)S(1)} %collective-permute-done.9.received, f32[16,2048]{1,0:T(8,128)S(1)} %get-tuple-element.76.rest, f32[16,4096]{1,0:T(8,128)} %get-tuple-element.77.partly), custom_call_target="tpu_custom_call", output_to_operand_aliasing={{}: (2, {})} | custom-call | tf_op jit(solution)/shard_map/finish/pallas_call | solution.py:358
  (1 shorter events, 0.0 us)
Async XLA Ops:
  1.4 5.4 %collective-permute-start.1 = (bf16[16,512]{1,0:T(8,128)(2,1)S(1)}, bf16[16,512]{1,0:T(8,128)(2,1)S(1)}, u32[]{:S(2)}, u32[]{:S(2)}) collective-permute-start(bf16[16,512]{1,0:T(8,128)(2,1)S(1)} %get-tuple-element.79), channel_id=1, source_target_pairs={{0,3},{1,2},{2,1},{3,0},{4,7},{5,6},{6,5},{7,4},{8,11},{9,10},{10,... | collective-permute-start | bytes 49160 | tf_op jit(solution)/shard_map/ppermute | solution.py:37
  3.8 3.7 %collective-permute-start = (bf16[16,512]{1,0:T(8,128)(2,1)S(1)}, bf16[16,512]{1,0:T(8,128)(2,1)S(1)}, u32[]{:S(2)}, u32[]{:S(2)}) collective-permute-start(bf16[16,512]{1,0:T(8,128)(2,1)S(1)} %get-tuple-element.79), channel_id=1, source_target_pairs={{0,1},{1,2},{2,0},{3,4},{4,3},{5,6},{6,5},{7,8},{8,7},{9,10},{10,9... | collective-permute-start | bytes 49160 | tf_op jit(solution)/shard_map/ppermute | solution.py:38
  4.5 2.3 %collective-permute-start.2 = (bf16[16,512]{1,0:T(8,128)(2,1)S(1)}, bf16[16,512]{1,0:T(8,128)(2,1)S(1)}, u32[]{:S(2)}, u32[]{:S(2)}) collective-permute-start(bf16[16,512]{1,0:T(8,128)(2,1)S(1)} %get-tuple-element.78), channel_id=1, source_target_pairs={{0,1},{1,0},{2,3},{3,2},{4,5},{5,4},{6,7},{7,6},{8,9},{9,8},{10,11... | collective-permute-start | bytes 49160 | tf_op jit(solution)/shard_map/ppermute | solution.py:21
  14.2 2.1 %collective-permute-start.3 = (bf16[64,1152]{1,0:T(8,128)(2,1)S(1)}, bf16[64,1152]{1,0:T(8,128)(2,1)S(1)}, u32[]{:S(2)}, u32[]{:S(2)}) collective-permute-start(bf16[64,1152]{1,0:T(8,128)(2,1)S(1)} %get-tuple-element.45.piece), channel_id=1, source_target_pairs={{0,1},{1,0},{2,3},{3,2},{4,5},{5,4},{6,7},{7,6},{8,9},{9,8},{10,11... | collective-permute-start | bytes 442376 | tf_op jit(solution)/shard_map/ppermute | solution.py:21
  17.5 6.2 %collective-permute-start.4 = (bf16[304,128]{1,0:T(8,128)(2,1)S(1)}, bf16[304,128]{1,0:T(8,128)(2,1)S(1)}, u32[]{:S(2)}, u32[]{:S(2)}) collective-permute-start(bf16[304,128]{1,0:T(8,128)(2,1)S(1)} %get-tuple-element.55), channel_id=1, source_target_pairs={{0,6},{1,7},{2,4},{3,5},{4,2},{5,3},{6,0},{7,1},{8,14},{9,15},{10,... | collective-permute-start | bytes 233480 | tf_op jit(solution)/shard_map/ppermute | solution.py:444
  20.9 4.4 %collective-permute-start.5 = (bf16[304,128]{1,0:T(8,128)(2,1)S(1)}, bf16[304,128]{1,0:T(8,128)(2,1)S(1)}, u32[]{:S(2)}, u32[]{:S(2)}) collective-permute-start(bf16[304,128]{1,0:T(8,128)(2,1)S(1)} %get-tuple-element.56), channel_id=1, source_target_pairs={{0,4},{1,5},{2,6},{3,7},{4,0},{5,1},{6,2},{7,3},{8,12},{9,13},{10,... | collective-permute-start | bytes 233480 | tf_op jit(solution)/shard_map/ppermute | solution.py:444
  20.9 4.4 %collective-permute-start.6 = (bf16[304,128]{1,0:T(8,128)(2,1)S(1)}, bf16[304,128]{1,0:T(8,128)(2,1)S(1)}, u32[]{:S(2)}, u32[]{:S(2)}) collective-permute-start(bf16[304,128]{1,0:T(8,128)(2,1)S(1)} %get-tuple-element.57), channel_id=1, source_target_pairs={{0,2},{1,3},{2,0},{3,1},{4,6},{5,7},{6,4},{7,5},{8,10},{9,11},{10,... | collective-permute-start | bytes 233480 | tf_op jit(solution)/shard_map/ppermute | solution.py:444
  25.4 4.8 %collective-permute-start.7 = (bf16[288,128]{1,0:T(8,128)(2,1)S(1)}, bf16[288,128]{1,0:T(8,128)(2,1)S(1)}, u32[]{:S(2)}, u32[]{:S(2)}) collective-permute-start(bf16[288,128]{1,0:T(8,128)(2,1)S(1)} %get-tuple-element.62), channel_id=1, source_target_pairs={{0,8},{4,12},{8,0},{12,4},{16,24},{20,28},{24,16},{28,20},{1,9},{5... | collective-permute-start | bytes 221192 | tf_op jit(solution)/shard_map/ppermute | solution.py:21
  30.3 5.4 %collective-permute-start.8 = (bf16[288,128]{1,0:T(8,128)(2,1)S(1)}, bf16[288,128]{1,0:T(8,128)(2,1)S(1)}, u32[]{:S(2)}, u32[]{:S(2)}) collective-permute-start(bf16[288,128]{1,0:T(8,128)(2,1)S(1)} %get-tuple-element.64), channel_id=1, source_target_pairs={{0,16},{4,20},{8,24},{12,28},{16,0},{20,4},{24,8},{28,12},{1,17},{... | collective-permute-start | bytes 221192 | tf_op jit(solution)/shard_map/ppermute | solution.py:21
  35.7 4.3 %collective-permute-start.9 = (bf16[256,128]{1,0:T(8,128)(2,1)S(1)}, bf16[256,128]{1,0:T(8,128)(2,1)S(1)}, u32[]{:S(2)}, u32[]{:S(2)}) collective-permute-start(bf16[256,128]{1,0:T(8,128)(2,1)S(1)} %get-tuple-element.75), channel_id=1, source_target_pairs={{0,4},{4,0},{8,12},{12,8},{16,20},{20,16},{24,28},{28,24},{1,5},{5... | collective-permute-start | bytes 196616 | tf_op jit(solution)/shard_map/ppermute | solution.py:21

commit v6 on v5

--- a/solution.py
+++ b/solution.py
@@ -21,11 +21,31 @@
     return lax.ppermute(array, axis, [(i, i ^ distance) for i in range(size)])
 
 
+def edges_kernel(rec, outer, inner, sems):
+    far = rec.shape[0] - HALO
+    at = lax.rem(lax.axis_index("narrow"), 2) * far
+    copies = [
+        pltpu.make_async_copy(rec.at[pl.ds(pl.multiple_of(start, HALO), HALO), :], rows, sems.at[i])
+        for i, (start, rows) in enumerate(((at, outer), (far - at, inner)))
+    ]
+    for copy in copies:
+        copy.start()
+    for copy in copies:
+        copy.wait()
+
+
+def again_kernel(outer, inner, outer_again, inner_again):
+    outer_again[...] = outer[...]
+    inner_again[...] = inner[...]
+
+
 def edges_exchanged(recording):
-    length = recording.shape[0]
-    is_odd = lax.axis_index("narrow") % 2
-    outer = lax.dynamic_slice_in_dim(recording, is_odd * (length - HALO), HALO, 0)
-    inner = lax.dynamic_slice_in_dim(recording, (1 - is_odd) * (length - HALO), HALO, 0)
+    rows = ((HALO, recording.shape[1]), recording.dtype)
+    source = pltpu.with_memory_space_constraint(recording, pltpu.HBM)
+    outer, inner = call(
+        edges_kernel, "edges", [rows, rows], scratch=[pltpu.SemaphoreType.DMA((2,))], in_specs=[HBM]
+    )(source)
+    again, inner = call(again_kernel, "again", [rows, rows])(outer, inner)
     wide_size, narrow_size = lax.axis_size("wide"), lax.axis_size("narrow")
     size = wide_size * narrow_size
     inside = {i: (i - 1 + 2 * (i % 2)) % narrow_size for i in range(narrow_size)}
@@ -33,10 +53,9 @@
     if narrow_size > 2:
         end = size - 1
         over.update({0: 1, 1: 2, 2: 0, end: end - 1, end - 1: end - 2, end - 2: end})
-    inner = exchanged(inner, "narrow", 1)
-    inside = lax.ppermute(outer, "narrow", list(inside.items()))
     over = lax.ppermute(outer, WHOLE, list(over.items()))
-    return over, inside, inner
+    inside = lax.ppermute(again, "narrow", list(inside.items()))
+    return over, inside, exchanged(inner, "narrow", 1)
 
 
 def load_kernel(rec_hbm, weights_hbm, bias_hbm, proj_hbm, padded, weights, bias, proj, rec, sems):
@@ -165,10 +184,9 @@
     return folded(crossed), jnp.where(jnp.logical_and(is_last, first), row, 0.0)
 
 
-def own_kernel(targets, piece, path, second, ends, *refs):
+def own_kernel(targets, piece, second, ends, *refs):
     sums, (diff, lead, rest, lhs) = refs[: len(targets)], refs[len(targets) :]
     points, after = coefficients(piece, diff, lead, rest)
-    path[...] = after.astype(BF16)
     second[...], ends[...] = besides(0, piece, points, after)
     for target, total in zip(targets, sums):
         total[...] = target_sum(target, piece, diff, lead, rest, lhs)
@@ -187,9 +205,12 @@
         pack(message, before[...] + target_sum(target, piece, diff, lead, rest, lhs), both_second, both_ends)
 
 
-def kept_kernel(piece, before, total, diff, lead, rest, lhs):
-    coefficients(piece, diff, lead, rest)
-    total[...] = before[...] + target_sum((0, 0), piece, diff, lead, rest, lhs)
+def kept_kernel(piece, mate, total, path, diff, lead, rest, lhs):
+    _, after = coefficients(piece, diff, lead, rest)
+    path[...] = after.astype(BF16)
+    first = target_sum((0, 0), piece, diff, lead, rest, lhs)
+    coefficients(mate, diff, lead, rest)
+    total[...] = first + target_sum((0, 0), mate, diff, lead, rest, lhs)
 
 
 def folded(crossed):
@@ -235,7 +256,7 @@
 
 def reduce_kernel(targets, kept, chip_second, chip_ends, *refs):
     parts, refs = refs[: len(targets)], refs[len(targets) :]
-    own, other, own_second, other_second, pair, pair_second, ends, sent = refs
+    own, other, own_second, other_second, ends, sent = refs
     count, rows = kept.shape[0], chip_second.shape[0]
     sums = [[kept[...], chip_second[...]], None]
     last = chip_ends[...]
@@ -247,8 +268,6 @@
     own[...], own_second[...] = sums[0]
     other[...], other_second[...] = sums[1]
     total, doubled = sums[0][0] + sums[1][0], sums[0][1] + sums[1][1]
-    pair[...] = total
-    pair_second[...] = doubled
     ends[...] = last
     pack(sent, total, doubled)
 
@@ -267,30 +286,18 @@
     factor[:, :width] = 0.5 * xx - edge / 6.0 - xx / 3.0
 
 
-def is_later(distance):
-    return jnp.bitwise_and(lax.axis_index("wide"), distance) != 0
-
-
-def scan_kernel(distance, started, ended, *refs):
-    before, refs = refs[: 2 * started], refs[2 * started :]
-    group_third, group_second, received, third, second, sent = refs[:6]
-    more_third, more_second = unpack(received, group_third.shape[0], group_second.shape[0])
-    total, doubled = group_third[...] + more_third, group_second[...] + more_second
-    pack(sent, total, doubled)
-    earlier_third = jnp.where(is_later(distance), more_third, 0.0)
-    earlier_second = jnp.where(is_later(distance), more_second, 0.0)
-    if started:
-        earlier_third, earlier_second = earlier_third + before[0][...], earlier_second + before[1][...]
-    third[...] = earlier_third
-    second[...] = earlier_second
-    if not ended:
-        refs[6][...] = total
-        refs[7][...] = doubled
-
-
-def return_kernel(distance, third, received, own, other, earlier, sent):
-    count = third.shape[0]
-    total = third[...] + jnp.where(is_later(distance), received[:count, :].astype(F32), 0.0)
+def earlier_sum(flips, refs, start, size):
+    me = lax.axis_index("wide")
+    total = jnp.zeros((size, LANES), F32)
+    for flip, ref in zip(flips, refs):
+        come = ref[start : start + size, :].astype(F32)
+        total = total + jnp.where(jnp.bitwise_xor(me, flip) < me, come, 0.0)
+    return total
+
+
+def return_kernel(flips, own, other, *refs):
+    received, (earlier, sent) = refs[:-2], refs[-2:]
+    total = earlier_sum(flips, received, 0, own.shape[0])
     earlier[...] = total
     sent[...] = (total + other[...] + jnp.where(parity() == 0, own[...], 0.0)).astype(BF16)
 
@@ -308,15 +315,12 @@
         result[:, at * LANES : (at + 1) * LANES] = value
 
 
-def levels_kernel(
-    scale, row_count, distance, second, received, own_second, other_second, earlier, own, other, x_twice, pairs, factor,
-    level_two, partly, rest, held, own_half, sem,
-):
+def levels_kernel(scale, row_count, flips, own_second, other_second, earlier, own, other, x_twice, pairs, factor, *refs):
+    received, (level_two, partly, rest, held, own_half, sem) = refs[: len(flips)], refs[len(flips) :]
     width = pairs.shape[0]
-    count, rows = own.shape[0], second.shape[0]
     is_first = parity() == 0
-    coded = jnp.where(is_later(distance), received[count : count + rows, :].astype(F32), 0.0)
-    upper = second[...] + coded + pltpu.roll(coded, LANES // 2, 1)
+    coded = earlier_sum(flips, received, own.shape[0], own_second.shape[0])
+    upper = coded + pltpu.roll(coded, LANES // 2, 1)
     upper = upper + own_second[...] + jnp.where(is_first, 0.0, other_second[...])
     turned = 0.5 * unfolded(upper)
     held[:, :width] = scale**3 * (factor[:, :width] + turned)
@@ -423,12 +427,12 @@
 
     mate = exchanged(piece, "narrow", 1)
     targets = [(across, mask) for across in (1, 0) for mask in range(narrow_size - 2, -1, -2)][:-1]
-    points, chip_second, chip_ends, own, *sums = call(
-        functools.partial(own_kernel, [(0, 0)] + targets),
+    second, ends, *sums = call(
+        functools.partial(own_kernel, targets),
         "own",
-        [((width, length), BF16), folds, last] + [half] * (1 + len(targets)),
+        [folds, last] + [half] * len(targets),
         scratch=scratch,
-        flops=share * (1 + len(targets)),
+        flops=share * len(targets),
     )(piece)
     chip_second, chip_ends, *messages = call(
         functools.partial(mate_kernel, targets),
@@ -436,17 +440,19 @@
         [folds, last] + [((count + width // 2 + ENDS, LANES), BF16)] * len(targets),
         scratch=scratch,
         flops=share * len(targets),
-    )(mate, chip_second, chip_ends, *sums)
+    )(mate, second, ends, *sums)
     size = wide_size * narrow_size
     parts = []
     for (across, mask), sent in zip(targets, messages):
         flip = across * narrow_size + mask
         parts.append(lax.ppermute(sent, WHOLE, [(i, i ^ flip) for i in range(size)]))
-    (kept,) = call(kept_kernel, "kept", [half], scratch=scratch, flops=share)(mate, own)
-    own, other, own_second, other_second, group_third, group_second, ends, sent = call(
+    kept, points = call(
+        kept_kernel, "kept", [half, ((width, length), BF16)], scratch=scratch, flops=2 * share
+    )(piece, mate)
+    own, other, own_second, other_second, ends, sent = call(
         functools.partial(reduce_kernel, targets),
         "reduce",
-        [half, half, folds, folds, half, folds, last, message],
+        [half, half, folds, folds, last, message],
     )(kept, chip_second, chip_ends, *parts)
     level_one, x_twice, pairs, factor = call(
         functools.partial(ends_kernel, scale),
@@ -455,38 +461,23 @@
         flops=share,
     )(ends)
 
-    earlier = ()
-    distance = 2
-    received = exchanged(sent, "wide", distance)
-    while 2 * distance < wide_size:
-        ended = 4 * distance >= wide_size
-        *earlier, sent = call(
-            functools.partial(scan_kernel, distance, len(earlier) > 0, ended),
-            "scan",
-            [half, folds, message] + ([] if ended else [half, folds]),
-        )(*earlier, group_third, group_second, received)
-        if not ended:
-            sent, group_third, group_second = earlier[2], earlier[3], sent
-            earlier = earlier[:2]
-        distance *= 2
-        received = exchanged(sent, "wide", distance)
-    if not earlier:
-        earlier = [jnp.zeros(dims, dtype) for dims, dtype in (half, folds)]
-    total, sent = call(functools.partial(return_kernel, distance), "back", [half, ((count, LANES), BF16)])(
-        earlier[0], received, own, other
+    flips = [flip for flip in range(2, wide_size, 2) if flip != wide_size // 2] + [wide_size // 2]
+    received = [exchanged(sent, "wide", flip) for flip in flips]
+    total, sent = call(functools.partial(return_kernel, flips), "back", [half, ((count, LANES), BF16)])(
+        own, other, *received
     )
     returned = exchanged(sent, "wide", 1)
     own_size = width * width // 2
     third_shape = ((row_count, 2 * own_size), F32)
     half_buffer = ((row_count, own_size), F32)
     level_two, partly, rest = call(
-        functools.partial(levels_kernel, scale, row_count, distance),
+        functools.partial(levels_kernel, scale, row_count, flips),
         "levels",
         [folds, third_shape, half_buffer],
         scratch=[pltpu.VMEM((width, LANES), F32), pltpu.VMEM(half_buffer[0], F32), pltpu.SemaphoreType.DMA],
         out_specs=(VMEM, HBM, VMEM),
         flops=10**9,
-    )(earlier[1], received, own_second, other_second, total, own, other, x_twice, pairs, factor)
+    )(own_second, other_second, total, own, other, x_twice, pairs, factor, *received)
     (level_three,) = call(
         functools.partial(finish_kernel, scale, row_count),
         "finish",

time: 41.1 us -> 39.5 us (0.961)
  waiting for transfers between devices: 8.84 us -> 7.12 us
  Pallas kernels: 16.1 us -> 17 us
  local copies, waits for them, and re-layouts: 0.74 us -> 0 us
    ppermute x1, starting transfers between devices: 2.41 us -> 3.67 us  [edges_exchanged(): inside = lax.ppermute(again, 'narrow', list(inside.items()))]
    ppermute x3, waiting for transfers between devices: 3.06 us -> 1.85 us  [per_device(): lax.ppermute(sent, WHOLE, [(i, i ^ flip) for i in range(size)])]
    pallas_call x11 -> x12, Pallas kernels: 16.1 us -> 17 us  [run(): pl.pallas_call(kernel, out_shape=tuple(shapes), in_specs=in_specs or [VME...]
    ppermute x1, waiting for transfers between devices: 0.75 us -> 0.01 us  [edges_exchanged(): over = lax.ppermute(outer, WHOLE, list(over.items()))]
    dynamic_slice x1 -> x0, local copies, waits for them, and re-layouts: 0.74 us -> none  [edges_exchanged(): lax.dynamic_slice_in_dim(recording, (1 - is_odd) * (length - HALO), HALO, 0)]
    ppermute x5 -> x6, starting transfers between devices: 7.21 us -> 6.62 us  [exchanged(): return lax.ppermute(array, axis, [(i, i ^ distance) for i in range(size)])]
    ppermute x3, starting transfers between devices: 4.03 us -> 3.55 us  [per_device(): lax.ppermute(sent, WHOLE, [(i, i ^ flip) for i in range(size)])]
    ppermute x5 -> x6, waiting for transfers between devices: 5.03 us -> 5.27 us  [exchanged(): return lax.ppermute(array, axis, [(i, i ^ distance) for i in range(size)])]
  transfers between devices with their start and end apart: 10 -> 11, of which waited for: 6 -> 7; matrix products, arithmetic and copies ran while one was open for 0% -> 0% of each run, Pallas kernels for 18% -> 19%
where the time goes in v6:
time: 39.5 us; the launch traced here: 39.1 us
  Pallas kernels  17 us (43%)
  starting transfers between devices  14.3 us (36%)
  waiting for transfers between devices  7.12 us (18%)
  between operations  0.72 us (2%)
    pallas_call x12, Pallas kernels, run(): pl.pallas_call(kernel, out_shape=tuple(shapes), in_specs=in_specs or [VME...  17 us
    ppermute x6, starting transfers between devices, exchanged(): return lax.ppermute(array, axis, [(i, i ^ distance) for i in range(size)])  6.62 us
    ppermute x6, waiting for transfers between devices, exchanged(): return lax.ppermute(array, axis, [(i, i ^ distance) for i in range(size)])  5.27 us
    ppermute x1, starting transfers between devices, edges_exchanged(): inside = lax.ppermute(again, 'narrow', list(inside.items()))  3.67 us
    ppermute x3, starting transfers between devices, per_device(): lax.ppermute(sent, WHOLE, [(i, i ^ flip) for i in range(size)])  3.55 us
    ppermute x3, waiting for transfers between devices, per_device(): lax.ppermute(sent, WHOLE, [(i, i ^ flip) for i in range(size)])  1.85 us
  transfers between devices with their start and end apart: 11, of which 7 were waited for; matrix products, arithmetic and copies ran while one was open for 0% of the time, Pallas kernels for 19%

profile of v6, /device:TPU:0, one launch (start us, length us, event | category | flops | bytes accessed | tf_op | source)
XLA Modules:
  0.0 39.1 jit_solution(3021434093840940848)
XLA Ops:
  0.6 0.8 %edges.1 = (bf16[16,512]{1,0:T(8,128)(2,1)S(1)}, bf16[16,512]{1,0:T(8,128)(2,1)S(1)}) custom-call(bf16[1024,512]{1,0:T(8,128)(2,1)} %rec.1), custom_call_target="tpu_custom_call" | custom-call | tf_op jit(solution)/shard_map/edges/pallas_call | solution.py:362
  1.4 0.5 %collective-permute-start = (bf16[16,512]{1,0:T(8,128)(2,1)S(1)}, bf16[16,512]{1,0:T(8,128)(2,1)S(1)}, u32[]{:S(2)}, u32[]{:S(2)}) collective-permute-start(bf16[16,512]{1,0:T(8,128)(2,1)S(1)} %get-tuple-element.41.outer), channel_id=1, source_target_pairs={{0,1},{1,2},{2,0},{3,4},{4,3},{5,6},{6,5},{7,8},{8,7},{9,10},{10,9... | collective-permute-start | bytes 49160 | tf_op jit(solution)/shard_map/ppermute | solution.py:56
  1.9 3.7 %collective-permute-start.1 = (bf16[16,512]{1,0:T(8,128)(2,1)S(1)}, bf16[16,512]{1,0:T(8,128)(2,1)S(1)}, u32[]{:S(2)}, u32[]{:S(2)}) collective-permute-start(bf16[16,512]{1,0:T(8,128)(2,1)S(1)} %get-tuple-element.43), channel_id=1, source_target_pairs={{0,3},{1,2},{2,1},{3,0},{4,7},{5,6},{6,5},{7,4},{8,11},{9,10},{10,... | collective-permute-start | bytes 49160 | tf_op jit(solution)/shard_map/ppermute | solution.py:57
  5.6 0.0 collective-permute-start.2
  5.6 2.3 %load.1 = (f32[1072,512]{1,0:T(8,128)S(1)}, bf16[2,3,512,512]{3,2,1,0:T(8,128)(2,1)S(1)}, f32[3,512]{1,0:T(4,128)S(1)}, bf16[64,512]{1,0:T(8,128)(2,1)S(1)}) custom-call(bf16[1024,512]{1,0:T(8,128)(2,1)} %rec.1, bf16[3,3,512,512]{3,2,1,0:T(8,128)(2,1)} %weights_hbm.3, f32[3,512]{1,0:T(4,128)} %bias_hbm.1, bf16[64,512]{1,0:T(8,128)(2,1)} %bitcast.5), custom_call_target="tpu_custom_call" | custom-call | flops 1000000000 | bytes 5835776 | tf_op jit(solution)/shard_map/load/pallas_call | solution.py:362
  7.8 0.0 collective-permute-done.1.inside
  7.9 0.0 collective-permute-done.2.inner
  7.9 0.0 collective-permute-done.over
  7.9 6.6 %conv.1 = (bf16[64,1152]{1,0:T(8,128)(2,1)S(1)}, f32[1072,512]{1,0:T(8,128)S(1)}) custom-call(f32[1072,512]{1,0:T(8,128)S(1)} %get-tuple-element.40._, bf16[16,512]{1,0:T(8,128)(2,1)S(1)} %collective-permute-done.over, bf16[16,512]{1,0:T(8,128)(2,1)S(1)} %collective-permute-done.1.inside, ...), custom_call_target="tpu_custom_call", output_to_operand_aliasing={{1}: (0, {})} | custom-call | flops 4831838208 | bytes 4718592 | tf_op jit(solution)/shard_map/conv/pallas_call | solution.py:362
  14.5 0.6 %collective-permute-start.3 = (bf16[64,1152]{1,0:T(8,128)(2,1)S(1)}, bf16[64,1152]{1,0:T(8,128)(2,1)S(1)}, u32[]{:S(2)}, u32[]{:S(2)}) collective-permute-start(bf16[64,1152]{1,0:T(8,128)(2,1)S(1)} %get-tuple-element.48.piece), channel_id=1, source_target_pairs={{0,1},{1,0},{2,3},{3,2},{4,5},{5,4},{6,7},{7,6},{8,9},{9,8},{10,11... | collective-permute-start | bytes 442376 | tf_op jit(solution)/shard_map/ppermute | solution.py:21
  15.1 1.2 %own.1 = (f32[32,128]{1,0:T(8,128)S(1)}, f32[16,128]{1,0:T(8,128)S(1)}, f32[256,128]{1,0:T(8,128)S(1)}, f32[256,128]{1,0:T(8,128)S(1)}, f32[256,128]{1,0:T(8,128)S(1)}) custom-call(bf16[64,1152]{1,0:T(8,128)(2,1)S(1)} %get-tuple-element.48.piece), custom_call_target="tpu_custom_call" | custom-call | flops 1500000000 | tf_op jit(solution)/shard_map/own/pallas_call | solution.py:362
  16.3 0.0 collective-permute-done.3.mate.piece
  16.3 1.3 %mate.1 = (f32[32,128]{1,0:T(8,128)S(1)}, f32[16,128]{1,0:T(8,128)S(1)}, bf16[304,128]{1,0:T(8,128)(2,1)S(1)}, bf16[304,128]{1,0:T(8,128)(2,1)S(1)}, bf16[304,128]{1,0:T(8,128)(2,1)S(1)}) custom-call(bf16[64,1152]{1,0:T(8,128)(2,1)S(1)} %collective-permute-done.3.mate.piece, f32[32,128]{1,0:T(8,128)S(1)} %get-tuple-element.51.second, ...), custom_call_target="tpu_custom_call" | custom-call | flops 1500000000 | tf_op jit(solution)/shard_map/mate/pallas_call | solution.py:362
  17.6 2.0 %collective-permute-start.4 = (bf16[304,128]{1,0:T(8,128)(2,1)S(1)}, bf16[304,128]{1,0:T(8,128)(2,1)S(1)}, u32[]{:S(2)}, u32[]{:S(2)}) collective-permute-start(bf16[304,128]{1,0:T(8,128)(2,1)S(1)} %get-tuple-element.58), channel_id=1, source_target_pairs={{0,6},{1,7},{2,4},{3,5},{4,2},{5,3},{6,0},{7,1},{8,14},{9,15},{10,... | collective-permute-start | bytes 233480 | tf_op jit(solution)/shard_map/ppermute | solution.py:448
  19.6 0.3 collective-permute-start.5
  19.9 1.2 %collective-permute-start.6 = (bf16[304,128]{1,0:T(8,128)(2,1)S(1)}, bf16[304,128]{1,0:T(8,128)(2,1)S(1)}, u32[]{:S(2)}, u32[]{:S(2)}) collective-permute-start(bf16[304,128]{1,0:T(8,128)(2,1)S(1)} %get-tuple-element.60), channel_id=1, source_target_pairs={{0,2},{1,3},{2,0},{3,1},{4,6},{5,7},{6,4},{7,5},{8,10},{9,11},{10,... | collective-permute-start | bytes 233480 | tf_op jit(solution)/shard_map/ppermute | solution.py:448
  21.2 1.6 %kept.1 = (f32[256,128]{1,0:T(8,128)S(1)}, bf16[64,1024]{1,0:T(8,128)(2,1)}) custom-call(bf16[64,1152]{1,0:T(8,128)(2,1)S(1)} %get-tuple-element.48.piece, bf16[64,1152]{1,0:T(8,128)(2,1)S(1)} %collective-permute-done.3.mate.piece), custom_call_target="tpu_custom_call" | custom-call | flops 1000000000 | tf_op jit(solution)/shard_map/kept/pallas_call | solution.py:362
  22.8 0.7 %collective-permute-done.4.refs_0_ = bf16[304,128]{1,0:T(8,128)(2,1)S(1)} collective-permute-done((bf16[304,128]{1,0:T(8,128)(2,1)S(1)}, bf16[304,128]{1,0:T(8,128)(2,1)S(1)}, u32[]{:S(2)}, u32[]{:S(2)}) %collective-permute-start.4) | collective-permute-done | bytes 77856 | tf_op jit(solution)/shard_map/ppermute | solution.py:448
  23.5 0.6 %collective-permute-done.5.refs_1_ = bf16[304,128]{1,0:T(8,128)(2,1)S(1)} collective-permute-done((bf16[304,128]{1,0:T(8,128)(2,1)S(1)}, bf16[304,128]{1,0:T(8,128)(2,1)S(1)}, u32[]{:S(2)}, u32[]{:S(2)}) %collective-permute-start.5) | collective-permute-done | bytes 77856 | tf_op jit(solution)/shard_map/ppermute | solution.py:448
  24.0 0.6 %collective-permute-done.6.refs_2_ = bf16[304,128]{1,0:T(8,128)(2,1)S(1)} collective-permute-done((bf16[304,128]{1,0:T(8,128)(2,1)S(1)}, bf16[304,128]{1,0:T(8,128)(2,1)S(1)}, u32[]{:S(2)}, u32[]{:S(2)}) %collective-permute-start.6) | collective-permute-done | bytes 77856 | tf_op jit(solution)/shard_map/ppermute | solution.py:448
  24.6 0.1 reduce.1
  24.7 2.8 %collective-permute-start.9 = (bf16[288,128]{1,0:T(8,128)(2,1)S(1)}, bf16[288,128]{1,0:T(8,128)(2,1)S(1)}, u32[]{:S(2)}, u32[]{:S(2)}) collective-permute-start(bf16[288,128]{1,0:T(8,128)(2,1)S(1)} %get-tuple-element.67), channel_id=1, source_target_pairs={{0,16},{4,20},{8,24},{12,28},{16,0},{20,4},{24,8},{28,12},{1,17},{... | collective-permute-start | bytes 221192 | tf_op jit(solution)/shard_map/ppermute | solution.py:21
  27.5 1.4 %collective-permute-start.8 = (bf16[288,128]{1,0:T(8,128)(2,1)S(1)}, bf16[288,128]{1,0:T(8,128)(2,1)S(1)}, u32[]{:S(2)}, u32[]{:S(2)}) collective-permute-start(bf16[288,128]{1,0:T(8,128)(2,1)S(1)} %get-tuple-element.67), channel_id=1, source_target_pairs={{0,24},{4,28},{8,16},{12,20},{16,8},{20,12},{24,0},{28,4},{1,25},{... | collective-permute-start | bytes 221192 | tf_op jit(solution)/shard_map/ppermute | solution.py:21
  28.9 0.2 collective-permute-start.7
  29.2 0.5 %ends.1 = (f32[1,64]{1,0:T(1,128)}, f32[1,128]{1,0:T(1,128)S(1)}, f32[64,128]{1,0:T(8,128)S(1)}, f32[64,128]{1,0:T(8,128)S(1)}) custom-call(f32[16,128]{1,0:T(8,128)S(1)} %get-tuple-element.61.ends), custom_call_target="tpu_custom_call" | custom-call | flops 500000000 | tf_op jit(solution)/shard_map/ends/pallas_call | solution.py:362
  29.7 2.7 %collective-permute-done.9.refs_2_ = bf16[288,128]{1,0:T(8,128)(2,1)S(1)} collective-permute-done((bf16[288,128]{1,0:T(8,128)(2,1)S(1)}, bf16[288,128]{1,0:T(8,128)(2,1)S(1)}, u32[]{:S(2)}, u32[]{:S(2)}) %collective-permute-start.9) | collective-permute-done | bytes 73760 | tf_op jit(solution)/shard_map/ppermute | solution.py:21
  32.4 1.5 %collective-permute-done.8.refs_1_ = bf16[288,128]{1,0:T(8,128)(2,1)S(1)} collective-permute-done((bf16[288,128]{1,0:T(8,128)(2,1)S(1)}, bf16[288,128]{1,0:T(8,128)(2,1)S(1)}, u32[]{:S(2)}, u32[]{:S(2)}) %collective-permute-start.8) | collective-permute-done | bytes 73760 | tf_op jit(solution)/shard_map/ppermute | solution.py:21
  33.9 0.2 collective-permute-done.7.refs_0_
  34.1 0.1 back.1
  34.1 1.6 %collective-permute-start.10 = (bf16[256,128]{1,0:T(8,128)(2,1)S(1)}, bf16[256,128]{1,0:T(8,128)(2,1)S(1)}, u32[]{:S(2)}, u32[]{:S(2)}) collective-permute-start(bf16[256,128]{1,0:T(8,128)(2,1)S(1)} %get-tuple-element.73), channel_id=1, source_target_pairs={{0,4},{4,0},{8,12},{12,8},{16,20},{20,16},{24,28},{28,24},{1,5},{5... | collective-permute-start | bytes 196616 | tf_op jit(solution)/shard_map/ppermute | solution.py:21
  35.8 1.8 %levels.1 = (f32[32,128]{1,0:T(8,128)}, f32[16,4096]{1,0:T(8,128)}, f32[16,2048]{1,0:T(8,128)S(1)}) custom-call(f32[32,128]{1,0:T(8,128)S(1)} %get-tuple-element.63.own_second, f32[32,128]{1,0:T(8,128)S(1)} %get-tuple-element.64.other_second, f32[256,128]{1,0:T(8,128)S(1)} %get-tuple-element.68.earlier, f32[256,128]{1,0:T(8,128)S(1)} %get-tuple-element.65.own, ...), custom_call_target="tpu_custom_call" | custom-call | flops 1000000000 | tf_op jit(solution)/shard_map/levels/pallas_call | solution.py:362
  37.6 0.9 %collective-permute-done.10.received = bf16[256,128]{1,0:T(8,128)(2,1)S(1)} collective-permute-done((bf16[256,128]{1,0:T(8,128)(2,1)S(1)}, bf16[256,128]{1,0:T(8,128)(2,1)S(1)}, u32[]{:S(2)}, u32[]{:S(2)}) %collective-permute-start.10) | collective-permute-done | bytes 65568 | tf_op jit(solution)/shard_map/ppermute | solution.py:21
  38.5 0.7 %finish.1 = f32[16,4096]{1,0:T(8,128)} custom-call(bf16[256,128]{1,0:T(8,128)(2,1)S(1)} %collective-permute-done.10.received, f32[16,2048]{1,0:T(8,128)S(1)} %get-tuple-element.74.rest, f32[16,4096]{1,0:T(8,128)} %get-tuple-element.75.partly), custom_call_target="tpu_custom_call", output_to_operand_aliasing={{}: (2, {})} | custom-call | tf_op jit(solution)/shard_map/finish/pallas_call | solution.py:362
  (1 shorter events, 0.0 us)
Async XLA Ops:
  1.4 6.5 %collective-permute-start = (bf16[16,512]{1,0:T(8,128)(2,1)S(1)}, bf16[16,512]{1,0:T(8,128)(2,1)S(1)}, u32[]{:S(2)}, u32[]{:S(2)}) collective-permute-start(bf16[16,512]{1,0:T(8,128)(2,1)S(1)} %get-tuple-element.41.outer), channel_id=1, source_target_pairs={{0,1},{1,2},{2,0},{3,4},{4,3},{5,6},{6,5},{7,8},{8,7},{9,10},{10,9... | collective-permute-start | bytes 49160 | tf_op jit(solution)/shard_map/ppermute | solution.py:56
  1.9 5.9 %collective-permute-start.1 = (bf16[16,512]{1,0:T(8,128)(2,1)S(1)}, bf16[16,512]{1,0:T(8,128)(2,1)S(1)}, u32[]{:S(2)}, u32[]{:S(2)}) collective-permute-start(bf16[16,512]{1,0:T(8,128)(2,1)S(1)} %get-tuple-element.43), channel_id=1, source_target_pairs={{0,3},{1,2},{2,1},{3,0},{4,7},{5,6},{6,5},{7,4},{8,11},{9,10},{10,... | collective-permute-start | bytes 49160 | tf_op jit(solution)/shard_map/ppermute | solution.py:57
  5.6 2.3 %collective-permute-start.2 = (bf16[16,512]{1,0:T(8,128)(2,1)S(1)}, bf16[16,512]{1,0:T(8,128)(2,1)S(1)}, u32[]{:S(2)}, u32[]{:S(2)}) collective-permute-start(bf16[16,512]{1,0:T(8,128)(2,1)S(1)} %get-tuple-element.44), channel_id=1, source_target_pairs={{0,1},{1,0},{2,3},{3,2},{4,5},{5,4},{6,7},{7,6},{8,9},{9,8},{10,11... | collective-permute-start | bytes 49160 | tf_op jit(solution)/shard_map/ppermute | solution.py:21
  14.5 1.8 %collective-permute-start.3 = (bf16[64,1152]{1,0:T(8,128)(2,1)S(1)}, bf16[64,1152]{1,0:T(8,128)(2,1)S(1)}, u32[]{:S(2)}, u32[]{:S(2)}) collective-permute-start(bf16[64,1152]{1,0:T(8,128)(2,1)S(1)} %get-tuple-element.48.piece), channel_id=1, source_target_pairs={{0,1},{1,0},{2,3},{3,2},{4,5},{5,4},{6,7},{7,6},{8,9},{9,8},{10,11... | collective-permute-start | bytes 442376 | tf_op jit(solution)/shard_map/ppermute | solution.py:21
  17.6 5.9 %collective-permute-start.4 = (bf16[304,128]{1,0:T(8,128)(2,1)S(1)}, bf16[304,128]{1,0:T(8,128)(2,1)S(1)}, u32[]{:S(2)}, u32[]{:S(2)}) collective-permute-start(bf16[304,128]{1,0:T(8,128)(2,1)S(1)} %get-tuple-element.58), channel_id=1, source_target_pairs={{0,6},{1,7},{2,4},{3,5},{4,2},{5,3},{6,0},{7,1},{8,14},{9,15},{10,... | collective-permute-start | bytes 233480 | tf_op jit(solution)/shard_map/ppermute | solution.py:448
  19.6 4.4 %collective-permute-start.5 = (bf16[304,128]{1,0:T(8,128)(2,1)S(1)}, bf16[304,128]{1,0:T(8,128)(2,1)S(1)}, u32[]{:S(2)}, u32[]{:S(2)}) collective-permute-start(bf16[304,128]{1,0:T(8,128)(2,1)S(1)} %get-tuple-element.59), channel_id=1, source_target_pairs={{0,4},{1,5},{2,6},{3,7},{4,0},{5,1},{6,2},{7,3},{8,12},{9,13},{10,... | collective-permute-start | bytes 233480 | tf_op jit(solution)/shard_map/ppermute | solution.py:448
  19.9 4.7 %collective-permute-start.6 = (bf16[304,128]{1,0:T(8,128)(2,1)S(1)}, bf16[304,128]{1,0:T(8,128)(2,1)S(1)}, u32[]{:S(2)}, u32[]{:S(2)}) collective-permute-start(bf16[304,128]{1,0:T(8,128)(2,1)S(1)} %get-tuple-element.60), channel_id=1, source_target_pairs={{0,2},{1,3},{2,0},{3,1},{4,6},{5,7},{6,4},{7,5},{8,10},{9,11},{10,... | collective-permute-start | bytes 233480 | tf_op jit(solution)/shard_map/ppermute | solution.py:448
  24.7 7.7 %collective-permute-start.9 = (bf16[288,128]{1,0:T(8,128)(2,1)S(1)}, bf16[288,128]{1,0:T(8,128)(2,1)S(1)}, u32[]{:S(2)}, u32[]{:S(2)}) collective-permute-start(bf16[288,128]{1,0:T(8,128)(2,1)S(1)} %get-tuple-element.67), channel_id=1, source_target_pairs={{0,16},{4,20},{8,24},{12,28},{16,0},{20,4},{24,8},{28,12},{1,17},{... | collective-permute-start | bytes 221192 | tf_op jit(solution)/shard_map/ppermute | solution.py:21
  27.5 6.3 %collective-permute-start.8 = (bf16[288,128]{1,0:T(8,128)(2,1)S(1)}, bf16[288,128]{1,0:T(8,128)(2,1)S(1)}, u32[]{:S(2)}, u32[]{:S(2)}) collective-permute-start(bf16[288,128]{1,0:T(8,128)(2,1)S(1)} %get-tuple-element.67), channel_id=1, source_target_pairs={{0,24},{4,28},{8,16},{12,20},{16,8},{20,12},{24,0},{28,4},{1,25},{... | collective-permute-start | bytes 221192 | tf_op jit(solution)/shard_map/ppermute | solution.py:21
  28.9 5.1 %collective-permute-start.7 = (bf16[288,128]{1,0:T(8,128)(2,1)S(1)}, bf16[288,128]{1,0:T(8,128)(2,1)S(1)}, u32[]{:S(2)}, u32[]{:S(2)}) collective-permute-start(bf16[288,128]{1,0:T(8,128)(2,1)S(1)} %get-tuple-element.67), channel_id=1, source_target_pairs={{0,8},{4,12},{8,0},{12,4},{16,24},{20,28},{24,16},{28,20},{1,9},{5... | collective-permute-start | bytes 221192 | tf_op jit(solution)/shard_map/ppermute | solution.py:21
  34.1 4.3 %collective-permute-start.10 = (bf16[256,128]{1,0:T(8,128)(2,1)S(1)}, bf16[256,128]{1,0:T(8,128)(2,1)S(1)}, u32[]{:S(2)}, u32[]{:S(2)}) collective-permute-start(bf16[256,128]{1,0:T(8,128)(2,1)S(1)} %get-tuple-element.73), channel_id=1, source_target_pairs={{0,4},{4,0},{8,12},{12,8},{16,20},{20,16},{24,28},{28,24},{1,5},{5... | collective-permute-start | bytes 196616 | tf_op jit(solution)/shard_map/ppermute | solution.py:21

commit v7 on v6

--- a/solution.py
+++ b/solution.py
@@ -58,21 +58,39 @@
     return over, inside, exchanged(inner, "narrow", 1)
 
 
-def load_kernel(rec_hbm, weights_hbm, bias_hbm, proj_hbm, padded, weights, bias, proj, rec, sems):
-    early = weights.shape[0]
-    pairs = ((rec_hbm, rec), (weights_hbm.at[:early], weights), (bias_hbm, bias), (proj_hbm, proj))
+def layer_rows(source, weights, bias, reach, start, size):
+    windows = [source[8 + start + k * reach : 8 + start + k * reach + size, :] for k in (-1, 0, 1)]
+    conv = bias
+    for tap, window in enumerate(windows):
+        conv = conv + jnp.dot(window.astype(BF16), weights[tap], preferred_element_type=F32)
+    half = 0.5 * conv
+    return (windows[1] + (half + half * jnp.tanh(half))).astype(BF16)
+
+
+def load_kernel(middle, rec_hbm, weights_hbm, bias_hbm, proj_hbm, padded, hidden, weights, bias, proj, rec, sems):
+    pairs = [(rec_hbm, rec), (bias_hbm, bias), (proj_hbm, proj)]
+    pairs += [(weights_hbm.at[layer], weights.at[layer]) for layer in range(weights.shape[0])]
     copies = [pltpu.make_async_copy(*pair, sems.at[i]) for i, pair in enumerate(pairs)]
-    for copy in copies:
+    for copy in copies[:4]:
         copy.start()
     copies[0].wait()
+    for copy in copies[4:]:
+        copy.start()
     padded[: 8 + HALO, :] = jnp.zeros((8 + HALO, rec.shape[1]), F32)
     padded[8 + HALO : 8 + HALO + rec.shape[0], :] = rec[...].astype(F32)
     padded[8 + HALO + rec.shape[0] :, :] = jnp.zeros((8 + HALO, rec.shape[1]), F32)
-    for copy in copies[1:]:
+    for copy in copies[1:4]:
         copy.wait()
-
-
-def conv_kernel(chunk, _, over, inside, inner, weights, weights_hbm, bias, proj, piece, padded, even, last_weights, path, sem):
+    for start, size in middle:
+        rows = layer_rows(padded, weights.at[0], bias[0:1, :], 1, start, size)
+        hidden[8 + start : 8 + start + size, :] = rows.astype(F32)
+    for copy in copies[4:]:
+        copy.wait()
+
+
+def conv_kernel(
+    chunks, _, __, over, inside, inner, weights, weights_hbm, bias, proj, piece, padded, even, last_weights, path, sem
+):
     layers = 1 + weights.shape[0]
     rows = padded.shape[0] - 16
     length = rows - 2 * HALO
@@ -98,17 +116,9 @@
         if layer == layers - 1:
             copy.wait()
         reach = 2**layer
-        for start in range(0, rows, chunk):
-            size = min(chunk, rows - start)
-            windows = [
-                source[8 + start + k * reach : 8 + start + k * reach + size, :] for k in (-1, 0, 1)
-            ]
-            conv = bias[layer : layer + 1, :]
-            for tap, window in enumerate(windows):
-                tap_weights = last_weights[tap] if layer == layers - 1 else weights[layer, tap]
-                conv = conv + jnp.dot(window.astype(BF16), tap_weights, preferred_element_type=F32)
-            half = 0.5 * conv
-            hidden = (windows[1] + (half + half * jnp.tanh(half))).astype(BF16)
+        for start, size in chunks[layer]:
+            layer_weights = last_weights if layer == layers - 1 else weights.at[layer]
+            hidden = layer_rows(source, layer_weights, bias[layer : layer + 1, :], reach, start, size)
             if layer < layers - 1:
                 target[8 + start : 8 + start + size, :] = hidden.astype(F32)
             else:
@@ -383,30 +393,35 @@
     buffer = ((rows + 16, channels), F32)
     far = (recording, conv_weight, conv_bias, projection.T)
     far = [pltpu.with_memory_space_constraint(held, pltpu.HBM) for held in far]
-    padded, *near = call(
-        load_kernel,
+    edge = rows // 4 // HALO * HALO
+    middle = [(edge, rows - 2 * edge - 2 * HALO)]
+    after = sum(middle[0])
+    chunk = 3 * LANES
+    chunks = [[(start, min(chunk, rows - start)) for start in range(0, rows, chunk)]] * layers
+    chunks[0] = [(0, edge), (after, rows - after)]
+    padded, hidden, *near = call(
+        functools.partial(load_kernel, middle),
         "load",
-        [buffer, ((layers - 1,) + conv_weight.shape[1:], BF16), (conv_bias.shape, F32), ((width, channels), BF16)],
-        scratch=[pltpu.VMEM(recording.shape, BF16), pltpu.SemaphoreType.DMA((4,))],
+        [buffer, buffer, ((layers - 1,) + conv_weight.shape[1:], BF16), (conv_bias.shape, F32), ((width, channels), BF16)],
+        scratch=[pltpu.VMEM(recording.shape, BF16), pltpu.SemaphoreType.DMA((2 + layers,))],
         in_specs=[HBM] * len(far),
         flops=10**9,
         moved=2 * sum(held.size for held in far),
     )(*far)
-    piece, _ = call(
-        functools.partial(conv_kernel, 3 * LANES),
+    piece, *_ = call(
+        functools.partial(conv_kernel, chunks),
         "conv",
-        [((width, length + LANES), BF16), buffer],
+        [((width, length + LANES), BF16), buffer, buffer],
         scratch=[
-            pltpu.VMEM(buffer[0], F32),
             pltpu.VMEM(conv_weight.shape[1:], BF16),
             pltpu.VMEM((width, length + LANES), F32),
             pltpu.SemaphoreType.DMA,
         ],
-        in_specs=[VMEM] * 5 + [HBM] + [VMEM] * 2,
-        aliases={0: 1},
+        in_specs=[VMEM] * 6 + [HBM] + [VMEM] * 2,
+        aliases={0: 1, 1: 2},
         flops=2 * layers * taps * length * channels**2,
         moved=2 * conv_weight.size,
-    )(padded, *edges, near[0], far[1], near[1], near[2])
+    )(padded, hidden, *edges, near[0], far[1], near[1], near[2])
     return piece
 
 

time: 39.5 us -> 39 us (0.987)
  Pallas kernels: 17 us -> 16.6 us
  transfers between devices with their start and end apart: 11 -> 11, of which waited for: 7 -> 7; matrix products, arithmetic and copies ran while one was open for 0% -> 0% of each run, Pallas kernels for 19% -> 21%
where the time goes in v7:
time: 39 us; the launch traced here: 38.6 us
  Pallas kernels  16.6 us (43%)
  starting transfers between devices  14.5 us (37%)
  waiting for transfers between devices  6.79 us (17%)
  between operations  0.72 us (2%)
    pallas_call x12, Pallas kernels, run(): pl.pallas_call(kernel, out_shape=tuple(shapes), in_specs=in_specs or [VME...  16.6 us
    ppermute x6, starting transfers between devices, exchanged(): return lax.ppermute(array, axis, [(i, i ^ distance) for i in range(size)])  6.77 us
    ppermute x6, waiting for transfers between devices, exchanged(): return lax.ppermute(array, axis, [(i, i ^ distance) for i in range(size)])  4.93 us
    ppermute x1, starting transfers between devices, edges_exchanged(): inside = lax.ppermute(again, 'narrow', list(inside.items()))  3.67 us
    ppermute x3, starting transfers between devices, per_device(): lax.ppermute(sent, WHOLE, [(i, i ^ flip) for i in range(size)])  3.55 us
    ppermute x3, waiting for transfers between devices, per_device(): lax.ppermute(sent, WHOLE, [(i, i ^ flip) for i in range(size)])  1.85 us
  transfers between devices with their start and end apart: 11, of which 7 were waited for; matrix products, arithmetic and copies ran while one was open for 0% of the time, Pallas kernels for 21%

profile of v7, /device:TPU:0, one launch (start us, length us, event | category | flops | bytes accessed | tf_op | source)
XLA Modules:
  0.0 38.6 jit_solution(11190733177923128072)
XLA Ops:
  0.6 0.8 %edges.1 = (bf16[16,512]{1,0:T(8,128)(2,1)S(1)}, bf16[16,512]{1,0:T(8,128)(2,1)S(1)}) custom-call(bf16[1024,512]{1,0:T(8,128)(2,1)} %rec.1), custom_call_target="tpu_custom_call" | custom-call | tf_op jit(solution)/shard_map/edges/pallas_call | solution.py:372
  1.4 0.5 %collective-permute-start = (bf16[16,512]{1,0:T(8,128)(2,1)S(1)}, bf16[16,512]{1,0:T(8,128)(2,1)S(1)}, u32[]{:S(2)}, u32[]{:S(2)}) collective-permute-start(bf16[16,512]{1,0:T(8,128)(2,1)S(1)} %get-tuple-element.43.outer), channel_id=1, source_target_pairs={{0,1},{1,2},{2,0},{3,4},{4,3},{5,6},{6,5},{7,8},{8,7},{9,10},{10,9... | collective-permute-start | bytes 49160 | tf_op jit(solution)/shard_map/ppermute | solution.py:56
  1.9 3.7 %collective-permute-start.1 = (bf16[16,512]{1,0:T(8,128)(2,1)S(1)}, bf16[16,512]{1,0:T(8,128)(2,1)S(1)}, u32[]{:S(2)}, u32[]{:S(2)}) collective-permute-start(bf16[16,512]{1,0:T(8,128)(2,1)S(1)} %get-tuple-element.45), channel_id=1, source_target_pairs={{0,3},{1,2},{2,1},{3,0},{4,7},{5,6},{6,5},{7,4},{8,11},{9,10},{10,... | collective-permute-start | bytes 49160 | tf_op jit(solution)/shard_map/ppermute | solution.py:57
  5.6 0.0 collective-permute-start.2
  5.6 3.0 %load.1 = (f32[1072,512]{1,0:T(8,128)S(1)}, f32[1072,512]{1,0:T(8,128)S(1)}, bf16[2,3,512,512]{3,2,1,0:T(8,128)(2,1)S(1)}, f32[3,512]{1,0:T(4,128)S(1)}, bf16[64,512]{1,0:T(8,128)(2,1)S(1)}) custom-call(bf16[1024,512]{1,0:T(8,128)(2,1)} %rec.1, bf16[3,3,512,512]{3,2,1,0:T(8,128)(2,1)} %weights_hbm.3, f32[3,512]{1,0:T(4,128)} %bias_hbm.1, bf16[64,512]{1,0:T(8,128)(2,1)} %bitcast.5), custom_call_target="tpu_custom_call" | custom-call | flops 1000000000 | bytes 5835776 | tf_op jit(solution)/shard_map/load/pallas_call | solution.py:372
  8.6 0.0 collective-permute-done.1.inside
  8.6 0.0 collective-permute-done.2.inner
  8.6 0.0 collective-permute-done.over
  8.6 5.6 %conv.1 = (bf16[64,1152]{1,0:T(8,128)(2,1)S(1)}, f32[1072,512]{1,0:T(8,128)S(1)}, f32[1072,512]{1,0:T(8,128)S(1)}) custom-call(f32[1072,512]{1,0:T(8,128)S(1)} %get-tuple-element.41._, f32[1072,512]{1,0:T(8,128)S(1)} %get-tuple-element.42.__, bf16[16,512]{1,0:T(8,128)(2,1)S(1)} %collective-permute-done.over, ...), custom_call_target="tpu_custom_call", output_to_operand_aliasing={{1}: (0, {}), {2}: (1, {})} | custom-call | flops 4831838208 | bytes 4718592 | tf_op jit(solution)/shard_map/conv/pallas_call | solution.py:372
  14.2 0.6 %collective-permute-start.3 = (bf16[64,1152]{1,0:T(8,128)(2,1)S(1)}, bf16[64,1152]{1,0:T(8,128)(2,1)S(1)}, u32[]{:S(2)}, u32[]{:S(2)}) collective-permute-start(bf16[64,1152]{1,0:T(8,128)(2,1)S(1)} %get-tuple-element.50.piece), channel_id=1, source_target_pairs={{0,1},{1,0},{2,3},{3,2},{4,5},{5,4},{6,7},{7,6},{8,9},{9,8},{10,11... | collective-permute-start | bytes 442376 | tf_op jit(solution)/shard_map/ppermute | solution.py:21
  14.7 1.2 %own.1 = (f32[32,128]{1,0:T(8,128)S(1)}, f32[16,128]{1,0:T(8,128)S(1)}, f32[256,128]{1,0:T(8,128)S(1)}, f32[256,128]{1,0:T(8,128)S(1)}, f32[256,128]{1,0:T(8,128)S(1)}) custom-call(bf16[64,1152]{1,0:T(8,128)(2,1)S(1)} %get-tuple-element.50.piece), custom_call_target="tpu_custom_call" | custom-call | flops 1500000000 | tf_op jit(solution)/shard_map/own/pallas_call | solution.py:372
  16.0 0.0 collective-permute-done.3.mate.piece
  16.0 1.3 %mate.1 = (f32[32,128]{1,0:T(8,128)S(1)}, f32[16,128]{1,0:T(8,128)S(1)}, bf16[304,128]{1,0:T(8,128)(2,1)S(1)}, bf16[304,128]{1,0:T(8,128)(2,1)S(1)}, bf16[304,128]{1,0:T(8,128)(2,1)S(1)}) custom-call(bf16[64,1152]{1,0:T(8,128)(2,1)S(1)} %collective-permute-done.3.mate.piece, f32[32,128]{1,0:T(8,128)S(1)} %get-tuple-element.53.second, ...), custom_call_target="tpu_custom_call" | custom-call | flops 1500000000 | tf_op jit(solution)/shard_map/mate/pallas_call | solution.py:372
  17.2 1.6 %collective-permute-start.4 = (bf16[304,128]{1,0:T(8,128)(2,1)S(1)}, bf16[304,128]{1,0:T(8,128)(2,1)S(1)}, u32[]{:S(2)}, u32[]{:S(2)}) collective-permute-start(bf16[304,128]{1,0:T(8,128)(2,1)S(1)} %get-tuple-element.60), channel_id=1, source_target_pairs={{0,6},{1,7},{2,4},{3,5},{4,2},{5,3},{6,0},{7,1},{8,14},{9,15},{10,... | collective-permute-start | bytes 233480 | tf_op jit(solution)/shard_map/ppermute | solution.py:463
  18.8 0.5 %collective-permute-start.5 = (bf16[304,128]{1,0:T(8,128)(2,1)S(1)}, bf16[304,128]{1,0:T(8,128)(2,1)S(1)}, u32[]{:S(2)}, u32[]{:S(2)}) collective-permute-start(bf16[304,128]{1,0:T(8,128)(2,1)S(1)} %get-tuple-element.61), channel_id=1, source_target_pairs={{0,4},{1,5},{2,6},{3,7},{4,0},{5,1},{6,2},{7,3},{8,12},{9,13},{10,... | collective-permute-start | bytes 233480 | tf_op jit(solution)/shard_map/ppermute | solution.py:463
  19.4 1.4 %collective-permute-start.6 = (bf16[304,128]{1,0:T(8,128)(2,1)S(1)}, bf16[304,128]{1,0:T(8,128)(2,1)S(1)}, u32[]{:S(2)}, u32[]{:S(2)}) collective-permute-start(bf16[304,128]{1,0:T(8,128)(2,1)S(1)} %get-tuple-element.62), channel_id=1, source_target_pairs={{0,2},{1,3},{2,0},{3,1},{4,6},{5,7},{6,4},{7,5},{8,10},{9,11},{10,... | collective-permute-start | bytes 233480 | tf_op jit(solution)/shard_map/ppermute | solution.py:463
  20.8 1.6 %kept.1 = (f32[256,128]{1,0:T(8,128)S(1)}, bf16[64,1024]{1,0:T(8,128)(2,1)}) custom-call(bf16[64,1152]{1,0:T(8,128)(2,1)S(1)} %get-tuple-element.50.piece, bf16[64,1152]{1,0:T(8,128)(2,1)S(1)} %collective-permute-done.3.mate.piece), custom_call_target="tpu_custom_call" | custom-call | flops 1000000000 | tf_op jit(solution)/shard_map/kept/pallas_call | solution.py:372
  22.4 0.7 %collective-permute-done.4.refs_0_ = bf16[304,128]{1,0:T(8,128)(2,1)S(1)} collective-permute-done((bf16[304,128]{1,0:T(8,128)(2,1)S(1)}, bf16[304,128]{1,0:T(8,128)(2,1)S(1)}, u32[]{:S(2)}, u32[]{:S(2)}) %collective-permute-start.4) | collective-permute-done | bytes 77856 | tf_op jit(solution)/shard_map/ppermute | solution.py:463
  23.1 0.3 collective-permute-done.5.refs_1_
  23.4 0.9 %collective-permute-done.6.refs_2_ = bf16[304,128]{1,0:T(8,128)(2,1)S(1)} collective-permute-done((bf16[304,128]{1,0:T(8,128)(2,1)S(1)}, bf16[304,128]{1,0:T(8,128)(2,1)S(1)}, u32[]{:S(2)}, u32[]{:S(2)}) %collective-permute-start.6) | collective-permute-done | bytes 77856 | tf_op jit(solution)/shard_map/ppermute | solution.py:463
  24.3 0.1 reduce.1
  24.4 2.7 %collective-permute-start.9 = (bf16[288,128]{1,0:T(8,128)(2,1)S(1)}, bf16[288,128]{1,0:T(8,128)(2,1)S(1)}, u32[]{:S(2)}, u32[]{:S(2)}) collective-permute-start(bf16[288,128]{1,0:T(8,128)(2,1)S(1)} %get-tuple-element.69), channel_id=1, source_target_pairs={{0,16},{4,20},{8,24},{12,28},{16,0},{20,4},{24,8},{28,12},{1,17},{... | collective-permute-start | bytes 221192 | tf_op jit(solution)/shard_map/ppermute | solution.py:21
  27.0 1.4 %collective-permute-start.8 = (bf16[288,128]{1,0:T(8,128)(2,1)S(1)}, bf16[288,128]{1,0:T(8,128)(2,1)S(1)}, u32[]{:S(2)}, u32[]{:S(2)}) collective-permute-start(bf16[288,128]{1,0:T(8,128)(2,1)S(1)} %get-tuple-element.69), channel_id=1, source_target_pairs={{0,24},{4,28},{8,16},{12,20},{16,8},{20,12},{24,0},{28,4},{1,25},{... | collective-permute-start | bytes 221192 | tf_op jit(solution)/shard_map/ppermute | solution.py:21
  28.4 0.4 collective-permute-start.7
  28.8 0.5 %ends.1 = (f32[1,64]{1,0:T(1,128)}, f32[1,128]{1,0:T(1,128)S(1)}, f32[64,128]{1,0:T(8,128)S(1)}, f32[64,128]{1,0:T(8,128)S(1)}) custom-call(f32[16,128]{1,0:T(8,128)S(1)} %get-tuple-element.63.ends), custom_call_target="tpu_custom_call" | custom-call | flops 500000000 | tf_op jit(solution)/shard_map/ends/pallas_call | solution.py:372
  29.3 2.6 %collective-permute-done.9.refs_2_ = bf16[288,128]{1,0:T(8,128)(2,1)S(1)} collective-permute-done((bf16[288,128]{1,0:T(8,128)(2,1)S(1)}, bf16[288,128]{1,0:T(8,128)(2,1)S(1)}, u32[]{:S(2)}, u32[]{:S(2)}) %collective-permute-start.9) | collective-permute-done | bytes 73760 | tf_op jit(solution)/shard_map/ppermute | solution.py:21
  31.9 1.5 %collective-permute-done.8.refs_1_ = bf16[288,128]{1,0:T(8,128)(2,1)S(1)} collective-permute-done((bf16[288,128]{1,0:T(8,128)(2,1)S(1)}, bf16[288,128]{1,0:T(8,128)(2,1)S(1)}, u32[]{:S(2)}, u32[]{:S(2)}) %collective-permute-start.8) | collective-permute-done | bytes 73760 | tf_op jit(solution)/shard_map/ppermute | solution.py:21
  33.3 0.2 collective-permute-done.7.refs_0_
  33.5 0.1 back.1
  33.6 1.8 %collective-permute-start.10 = (bf16[256,128]{1,0:T(8,128)(2,1)S(1)}, bf16[256,128]{1,0:T(8,128)(2,1)S(1)}, u32[]{:S(2)}, u32[]{:S(2)}) collective-permute-start(bf16[256,128]{1,0:T(8,128)(2,1)S(1)} %get-tuple-element.75), channel_id=1, source_target_pairs={{0,4},{4,0},{8,12},{12,8},{16,20},{20,16},{24,28},{28,24},{1,5},{5... | collective-permute-start | bytes 196616 | tf_op jit(solution)/shard_map/ppermute | solution.py:21
  35.4 1.8 %levels.1 = (f32[32,128]{1,0:T(8,128)}, f32[16,4096]{1,0:T(8,128)}, f32[16,2048]{1,0:T(8,128)S(1)}) custom-call(f32[32,128]{1,0:T(8,128)S(1)} %get-tuple-element.65.own_second, f32[32,128]{1,0:T(8,128)S(1)} %get-tuple-element.66.other_second, f32[256,128]{1,0:T(8,128)S(1)} %get-tuple-element.70.earlier, f32[256,128]{1,0:T(8,128)S(1)} %get-tuple-element.67.own, ...), custom_call_target="tpu_custom_call" | custom-call | flops 1000000000 | tf_op jit(solution)/shard_map/levels/pallas_call | solution.py:372
  37.2 0.7 %collective-permute-done.10.received = bf16[256,128]{1,0:T(8,128)(2,1)S(1)} collective-permute-done((bf16[256,128]{1,0:T(8,128)(2,1)S(1)}, bf16[256,128]{1,0:T(8,128)(2,1)S(1)}, u32[]{:S(2)}, u32[]{:S(2)}) %collective-permute-start.10) | collective-permute-done | bytes 65568 | tf_op jit(solution)/shard_map/ppermute | solution.py:21
  37.9 0.7 %finish.1 = f32[16,4096]{1,0:T(8,128)} custom-call(bf16[256,128]{1,0:T(8,128)(2,1)S(1)} %collective-permute-done.10.received, f32[16,2048]{1,0:T(8,128)S(1)} %get-tuple-element.76.rest, f32[16,4096]{1,0:T(8,128)} %get-tuple-element.77.partly), custom_call_target="tpu_custom_call", output_to_operand_aliasing={{}: (2, {})} | custom-call | tf_op jit(solution)/shard_map/finish/pallas_call | solution.py:372
  (1 shorter events, 0.0 us)
Async XLA Ops:
  1.4 7.2 %collective-permute-start = (bf16[16,512]{1,0:T(8,128)(2,1)S(1)}, bf16[16,512]{1,0:T(8,128)(2,1)S(1)}, u32[]{:S(2)}, u32[]{:S(2)}) collective-permute-start(bf16[16,512]{1,0:T(8,128)(2,1)S(1)} %get-tuple-element.43.outer), channel_id=1, source_target_pairs={{0,1},{1,2},{2,0},{3,4},{4,3},{5,6},{6,5},{7,8},{8,7},{9,10},{10,9... | collective-permute-start | bytes 49160 | tf_op jit(solution)/shard_map/ppermute | solution.py:56
  1.9 6.6 %collective-permute-start.1 = (bf16[16,512]{1,0:T(8,128)(2,1)S(1)}, bf16[16,512]{1,0:T(8,128)(2,1)S(1)}, u32[]{:S(2)}, u32[]{:S(2)}) collective-permute-start(bf16[16,512]{1,0:T(8,128)(2,1)S(1)} %get-tuple-element.45), channel_id=1, source_target_pairs={{0,3},{1,2},{2,1},{3,0},{4,7},{5,6},{6,5},{7,4},{8,11},{9,10},{10,... | collective-permute-start | bytes 49160 | tf_op jit(solution)/shard_map/ppermute | solution.py:57
  5.6 3.0 %collective-permute-start.2 = (bf16[16,512]{1,0:T(8,128)(2,1)S(1)}, bf16[16,512]{1,0:T(8,128)(2,1)S(1)}, u32[]{:S(2)}, u32[]{:S(2)}) collective-permute-start(bf16[16,512]{1,0:T(8,128)(2,1)S(1)} %get-tuple-element.46), channel_id=1, source_target_pairs={{0,1},{1,0},{2,3},{3,2},{4,5},{5,4},{6,7},{7,6},{8,9},{9,8},{10,11... | collective-permute-start | bytes 49160 | tf_op jit(solution)/shard_map/ppermute | solution.py:21
  14.2 1.8 %collective-permute-start.3 = (bf16[64,1152]{1,0:T(8,128)(2,1)S(1)}, bf16[64,1152]{1,0:T(8,128)(2,1)S(1)}, u32[]{:S(2)}, u32[]{:S(2)}) collective-permute-start(bf16[64,1152]{1,0:T(8,128)(2,1)S(1)} %get-tuple-element.50.piece), channel_id=1, source_target_pairs={{0,1},{1,0},{2,3},{3,2},{4,5},{5,4},{6,7},{7,6},{8,9},{9,8},{10,11... | collective-permute-start | bytes 442376 | tf_op jit(solution)/shard_map/ppermute | solution.py:21
  17.2 5.9 %collective-permute-start.4 = (bf16[304,128]{1,0:T(8,128)(2,1)S(1)}, bf16[304,128]{1,0:T(8,128)(2,1)S(1)}, u32[]{:S(2)}, u32[]{:S(2)}) collective-permute-start(bf16[304,128]{1,0:T(8,128)(2,1)S(1)} %get-tuple-element.60), channel_id=1, source_target_pairs={{0,6},{1,7},{2,4},{3,5},{4,2},{5,3},{6,0},{7,1},{8,14},{9,15},{10,... | collective-permute-start | bytes 233480 | tf_op jit(solution)/shard_map/ppermute | solution.py:463
  18.8 4.6 %collective-permute-start.5 = (bf16[304,128]{1,0:T(8,128)(2,1)S(1)}, bf16[304,128]{1,0:T(8,128)(2,1)S(1)}, u32[]{:S(2)}, u32[]{:S(2)}) collective-permute-start(bf16[304,128]{1,0:T(8,128)(2,1)S(1)} %get-tuple-element.61), channel_id=1, source_target_pairs={{0,4},{1,5},{2,6},{3,7},{4,0},{5,1},{6,2},{7,3},{8,12},{9,13},{10,... | collective-permute-start | bytes 233480 | tf_op jit(solution)/shard_map/ppermute | solution.py:463
  19.4 4.9 %collective-permute-start.6 = (bf16[304,128]{1,0:T(8,128)(2,1)S(1)}, bf16[304,128]{1,0:T(8,128)(2,1)S(1)}, u32[]{:S(2)}, u32[]{:S(2)}) collective-permute-start(bf16[304,128]{1,0:T(8,128)(2,1)S(1)} %get-tuple-element.62), channel_id=1, source_target_pairs={{0,2},{1,3},{2,0},{3,1},{4,6},{5,7},{6,4},{7,5},{8,10},{9,11},{10,... | collective-permute-start | bytes 233480 | tf_op jit(solution)/shard_map/ppermute | solution.py:463
  24.4 7.5 %collective-permute-start.9 = (bf16[288,128]{1,0:T(8,128)(2,1)S(1)}, bf16[288,128]{1,0:T(8,128)(2,1)S(1)}, u32[]{:S(2)}, u32[]{:S(2)}) collective-permute-start(bf16[288,128]{1,0:T(8,128)(2,1)S(1)} %get-tuple-element.69), channel_id=1, source_target_pairs={{0,16},{4,20},{8,24},{12,28},{16,0},{20,4},{24,8},{28,12},{1,17},{... | collective-permute-start | bytes 221192 | tf_op jit(solution)/shard_map/ppermute | solution.py:21
  27.0 6.3 %collective-permute-start.8 = (bf16[288,128]{1,0:T(8,128)(2,1)S(1)}, bf16[288,128]{1,0:T(8,128)(2,1)S(1)}, u32[]{:S(2)}, u32[]{:S(2)}) collective-permute-start(bf16[288,128]{1,0:T(8,128)(2,1)S(1)} %get-tuple-element.69), channel_id=1, source_target_pairs={{0,24},{4,28},{8,16},{12,20},{16,8},{20,12},{24,0},{28,4},{1,25},{... | collective-permute-start | bytes 221192 | tf_op jit(solution)/shard_map/ppermute | solution.py:21
  28.4 5.1 %collective-permute-start.7 = (bf16[288,128]{1,0:T(8,128)(2,1)S(1)}, bf16[288,128]{1,0:T(8,128)(2,1)S(1)}, u32[]{:S(2)}, u32[]{:S(2)}) collective-permute-start(bf16[288,128]{1,0:T(8,128)(2,1)S(1)} %get-tuple-element.69), channel_id=1, source_target_pairs={{0,8},{4,12},{8,0},{12,4},{16,24},{20,28},{24,16},{28,20},{1,9},{5... | collective-permute-start | bytes 221192 | tf_op jit(solution)/shard_map/ppermute | solution.py:21
  33.6 4.3 %collective-permute-start.10 = (bf16[256,128]{1,0:T(8,128)(2,1)S(1)}, bf16[256,128]{1,0:T(8,128)(2,1)S(1)}, u32[]{:S(2)}, u32[]{:S(2)}) collective-permute-start(bf16[256,128]{1,0:T(8,128)(2,1)S(1)} %get-tuple-element.75), channel_id=1, source_target_pairs={{0,4},{4,0},{8,12},{12,8},{16,20},{20,16},{24,28},{28,24},{1,5},{5... | collective-permute-start | bytes 196616 | tf_op jit(solution)/shard_map/ppermute | solution.py:21

commit v8 on v7

--- a/solution.py
+++ b/solution.py
@@ -68,24 +68,36 @@
 
 
 def load_kernel(middle, rec_hbm, weights_hbm, bias_hbm, proj_hbm, padded, hidden, weights, bias, proj, rec, sems):
-    pairs = [(rec_hbm, rec), (bias_hbm, bias), (proj_hbm, proj)]
-    pairs += [(weights_hbm.at[layer], weights.at[layer]) for layer in range(weights.shape[0])]
+    length, channels = rec.shape
+    low = middle[0][0] - 2 * HALO
+    high = sum(middle[-1])
+    parts = [slice(low, high), slice(0, low), slice(high, length)]
+    pairs = [(rec_hbm.at[parts[0]], rec.at[parts[0]]), (weights_hbm.at[0], weights.at[0]), (bias_hbm, bias)]
+    pairs += [(rec_hbm.at[part], rec.at[part]) for part in parts[1:]]
+    pairs += [(weights_hbm.at[layer], weights.at[layer]) for layer in range(1, weights.shape[0])]
+    pairs += [(proj_hbm, proj)]
     copies = [pltpu.make_async_copy(*pair, sems.at[i]) for i, pair in enumerate(pairs)]
-    for copy in copies[:4]:
+
+    def widen(part):
+        padded[8 + HALO + part.start : 8 + HALO + part.stop, :] = rec[part, :].astype(F32)
+
+    for copy in copies[:3]:
         copy.start()
     copies[0].wait()
-    for copy in copies[4:]:
+    for copy in copies[3:]:
         copy.start()
-    padded[: 8 + HALO, :] = jnp.zeros((8 + HALO, rec.shape[1]), F32)
-    padded[8 + HALO : 8 + HALO + rec.shape[0], :] = rec[...].astype(F32)
-    padded[8 + HALO + rec.shape[0] :, :] = jnp.zeros((8 + HALO, rec.shape[1]), F32)
-    for copy in copies[1:4]:
+    widen(parts[0])
+    padded[: 8 + HALO, :] = jnp.zeros((8 + HALO, channels), F32)
+    padded[8 + HALO + length :, :] = jnp.zeros((8 + HALO, channels), F32)
+    for copy in copies[1:3]:
         copy.wait()
     for start, size in middle:
         rows = layer_rows(padded, weights.at[0], bias[0:1, :], 1, start, size)
         hidden[8 + start : 8 + start + size, :] = rows.astype(F32)
-    for copy in copies[4:]:
+    for copy in copies[3:]:
         copy.wait()
+    for part in parts[1:]:
+        widen(part)
 
 
 def conv_kernel(
@@ -403,7 +415,7 @@
         functools.partial(load_kernel, middle),
         "load",
         [buffer, buffer, ((layers - 1,) + conv_weight.shape[1:], BF16), (conv_bias.shape, F32), ((width, channels), BF16)],
-        scratch=[pltpu.VMEM(recording.shape, BF16), pltpu.SemaphoreType.DMA((2 + layers,))],
+        scratch=[pltpu.VMEM(recording.shape, BF16), pltpu.SemaphoreType.DMA((5 + layers,))],
         in_specs=[HBM] * len(far),
         flops=10**9,
         moved=2 * sum(held.size for held in far),

time: 39 us -> 38.9 us (level)
  no operation moved by 1% of the time
where the time goes in v8:
time: 38.9 us; the launch traced here: 38.5 us
  Pallas kernels  16.5 us (42%)
  starting transfers between devices  14.5 us (37%)
  waiting for transfers between devices  6.76 us (17%)
  between operations  0.72 us (2%)
    pallas_call x12, Pallas kernels, run(): pl.pallas_call(kernel, out_shape=tuple(shapes), in_specs=in_specs or [VME...  16.5 us
    ppermute x6, starting transfers between devices, exchanged(): return lax.ppermute(array, axis, [(i, i ^ distance) for i in range(size)])  6.79 us
    ppermute x6, waiting for transfers between devices, exchanged(): return lax.ppermute(array, axis, [(i, i ^ distance) for i in range(size)])  4.91 us
    ppermute x1, starting transfers between devices, edges_exchanged(): inside = lax.ppermute(again, 'narrow', list(inside.items()))  3.67 us
    ppermute x3, starting transfers between devices, per_device(): lax.ppermute(sent, WHOLE, [(i, i ^ flip) for i in range(size)])  3.55 us
    ppermute x3, waiting for transfers between devices, per_device(): lax.ppermute(sent, WHOLE, [(i, i ^ flip) for i in range(size)])  1.85 us
  transfers between devices with their start and end apart: 11, of which 7 were waited for; matrix products, arithmetic and copies ran while one was open for 0% of the time, Pallas kernels for 21%

profile of v8, /device:TPU:0, one launch (start us, length us, event | category | flops | bytes accessed | tf_op | source)
XLA Modules:
  0.0 38.5 jit_solution(5347887520247488681)
XLA Ops:
  0.6 0.8 %edges.1 = (bf16[16,512]{1,0:T(8,128)(2,1)S(1)}, bf16[16,512]{1,0:T(8,128)(2,1)S(1)}) custom-call(bf16[1024,512]{1,0:T(8,128)(2,1)} %rec.1), custom_call_target="tpu_custom_call" | custom-call | tf_op jit(solution)/shard_map/edges/pallas_call | solution.py:384
  1.4 0.5 %collective-permute-start = (bf16[16,512]{1,0:T(8,128)(2,1)S(1)}, bf16[16,512]{1,0:T(8,128)(2,1)S(1)}, u32[]{:S(2)}, u32[]{:S(2)}) collective-permute-start(bf16[16,512]{1,0:T(8,128)(2,1)S(1)} %get-tuple-element.43.outer), channel_id=1, source_target_pairs={{0,1},{1,2},{2,0},{3,4},{4,3},{5,6},{6,5},{7,8},{8,7},{9,10},{10,9... | collective-permute-start | bytes 49160 | tf_op jit(solution)/shard_map/ppermute | solution.py:56
  1.9 3.7 %collective-permute-start.1 = (bf16[16,512]{1,0:T(8,128)(2,1)S(1)}, bf16[16,512]{1,0:T(8,128)(2,1)S(1)}, u32[]{:S(2)}, u32[]{:S(2)}) collective-permute-start(bf16[16,512]{1,0:T(8,128)(2,1)S(1)} %get-tuple-element.45), channel_id=1, source_target_pairs={{0,3},{1,2},{2,1},{3,0},{4,7},{5,6},{6,5},{7,4},{8,11},{9,10},{10,... | collective-permute-start | bytes 49160 | tf_op jit(solution)/shard_map/ppermute | solution.py:57
  5.6 0.0 collective-permute-start.2
  5.6 2.9 %load.1 = (f32[1072,512]{1,0:T(8,128)S(1)}, f32[1072,512]{1,0:T(8,128)S(1)}, bf16[2,3,512,512]{3,2,1,0:T(8,128)(2,1)S(1)}, f32[3,512]{1,0:T(4,128)S(1)}, bf16[64,512]{1,0:T(8,128)(2,1)S(1)}) custom-call(bf16[1024,512]{1,0:T(8,128)(2,1)} %rec.1, bf16[3,3,512,512]{3,2,1,0:T(8,128)(2,1)} %weights_hbm.3, f32[3,512]{1,0:T(4,128)} %bias_hbm.1, bf16[64,512]{1,0:T(8,128)(2,1)} %bitcast.5), custom_call_target="tpu_custom_call" | custom-call | flops 1000000000 | bytes 5835776 | tf_op jit(solution)/shard_map/load/pallas_call | solution.py:384
  8.5 0.0 collective-permute-done.1.inside
  8.5 0.0 collective-permute-done.2.inner
  8.5 0.0 collective-permute-done.over
  8.5 5.6 %conv.1 = (bf16[64,1152]{1,0:T(8,128)(2,1)S(1)}, f32[1072,512]{1,0:T(8,128)S(1)}, f32[1072,512]{1,0:T(8,128)S(1)}) custom-call(f32[1072,512]{1,0:T(8,128)S(1)} %get-tuple-element.41._, f32[1072,512]{1,0:T(8,128)S(1)} %get-tuple-element.42.__, bf16[16,512]{1,0:T(8,128)(2,1)S(1)} %collective-permute-done.over, ...), custom_call_target="tpu_custom_call", output_to_operand_aliasing={{1}: (0, {}), {2}: (1, {})} | custom-call | flops 4831838208 | bytes 4718592 | tf_op jit(solution)/shard_map/conv/pallas_call | solution.py:384
  14.1 0.6 %collective-permute-start.3 = (bf16[64,1152]{1,0:T(8,128)(2,1)S(1)}, bf16[64,1152]{1,0:T(8,128)(2,1)S(1)}, u32[]{:S(2)}, u32[]{:S(2)}) collective-permute-start(bf16[64,1152]{1,0:T(8,128)(2,1)S(1)} %get-tuple-element.50.piece), channel_id=1, source_target_pairs={{0,1},{1,0},{2,3},{3,2},{4,5},{5,4},{6,7},{7,6},{8,9},{9,8},{10,11... | collective-permute-start | bytes 442376 | tf_op jit(solution)/shard_map/ppermute | solution.py:21
  14.6 1.2 %own.1 = (f32[32,128]{1,0:T(8,128)S(1)}, f32[16,128]{1,0:T(8,128)S(1)}, f32[256,128]{1,0:T(8,128)S(1)}, f32[256,128]{1,0:T(8,128)S(1)}, f32[256,128]{1,0:T(8,128)S(1)}) custom-call(bf16[64,1152]{1,0:T(8,128)(2,1)S(1)} %get-tuple-element.50.piece), custom_call_target="tpu_custom_call" | custom-call | flops 1500000000 | tf_op jit(solution)/shard_map/own/pallas_call | solution.py:384
  15.9 0.0 collective-permute-done.3.mate.piece
  15.9 1.3 %mate.1 = (f32[32,128]{1,0:T(8,128)S(1)}, f32[16,128]{1,0:T(8,128)S(1)}, bf16[304,128]{1,0:T(8,128)(2,1)S(1)}, bf16[304,128]{1,0:T(8,128)(2,1)S(1)}, bf16[304,128]{1,0:T(8,128)(2,1)S(1)}) custom-call(bf16[64,1152]{1,0:T(8,128)(2,1)S(1)} %collective-permute-done.3.mate.piece, f32[32,128]{1,0:T(8,128)S(1)} %get-tuple-element.53.second, ...), custom_call_target="tpu_custom_call" | custom-call | flops 1500000000 | tf_op jit(solution)/shard_map/mate/pallas_call | solution.py:384
  17.1 1.6 %collective-permute-start.4 = (bf16[304,128]{1,0:T(8,128)(2,1)S(1)}, bf16[304,128]{1,0:T(8,128)(2,1)S(1)}, u32[]{:S(2)}, u32[]{:S(2)}) collective-permute-start(bf16[304,128]{1,0:T(8,128)(2,1)S(1)} %get-tuple-element.60), channel_id=1, source_target_pairs={{0,6},{1,7},{2,4},{3,5},{4,2},{5,3},{6,0},{7,1},{8,14},{9,15},{10,... | collective-permute-start | bytes 233480 | tf_op jit(solution)/shard_map/ppermute | solution.py:475
  18.7 0.5 %collective-permute-start.5 = (bf16[304,128]{1,0:T(8,128)(2,1)S(1)}, bf16[304,128]{1,0:T(8,128)(2,1)S(1)}, u32[]{:S(2)}, u32[]{:S(2)}) collective-permute-start(bf16[304,128]{1,0:T(8,128)(2,1)S(1)} %get-tuple-element.61), channel_id=1, source_target_pairs={{0,4},{1,5},{2,6},{3,7},{4,0},{5,1},{6,2},{7,3},{8,12},{9,13},{10,... | collective-permute-start | bytes 233480 | tf_op jit(solution)/shard_map/ppermute | solution.py:475
  19.3 1.4 %collective-permute-start.6 = (bf16[304,128]{1,0:T(8,128)(2,1)S(1)}, bf16[304,128]{1,0:T(8,128)(2,1)S(1)}, u32[]{:S(2)}, u32[]{:S(2)}) collective-permute-start(bf16[304,128]{1,0:T(8,128)(2,1)S(1)} %get-tuple-element.62), channel_id=1, source_target_pairs={{0,2},{1,3},{2,0},{3,1},{4,6},{5,7},{6,4},{7,5},{8,10},{9,11},{10,... | collective-permute-start | bytes 233480 | tf_op jit(solution)/shard_map/ppermute | solution.py:475
  20.7 1.6 %kept.1 = (f32[256,128]{1,0:T(8,128)S(1)}, bf16[64,1024]{1,0:T(8,128)(2,1)}) custom-call(bf16[64,1152]{1,0:T(8,128)(2,1)S(1)} %get-tuple-element.50.piece, bf16[64,1152]{1,0:T(8,128)(2,1)S(1)} %collective-permute-done.3.mate.piece), custom_call_target="tpu_custom_call" | custom-call | flops 1000000000 | tf_op jit(solution)/shard_map/kept/pallas_call | solution.py:384
  22.3 0.7 %collective-permute-done.4.refs_0_ = bf16[304,128]{1,0:T(8,128)(2,1)S(1)} collective-permute-done((bf16[304,128]{1,0:T(8,128)(2,1)S(1)}, bf16[304,128]{1,0:T(8,128)(2,1)S(1)}, u32[]{:S(2)}, u32[]{:S(2)}) %collective-permute-start.4) | collective-permute-done | bytes 77856 | tf_op jit(solution)/shard_map/ppermute | solution.py:475
  23.0 0.3 collective-permute-done.5.refs_1_
  23.3 0.9 %collective-permute-done.6.refs_2_ = bf16[304,128]{1,0:T(8,128)(2,1)S(1)} collective-permute-done((bf16[304,128]{1,0:T(8,128)(2,1)S(1)}, bf16[304,128]{1,0:T(8,128)(2,1)S(1)}, u32[]{:S(2)}, u32[]{:S(2)}) %collective-permute-start.6) | collective-permute-done | bytes 77856 | tf_op jit(solution)/shard_map/ppermute | solution.py:475
  24.2 0.1 reduce.1
  24.3 2.7 %collective-permute-start.9 = (bf16[288,128]{1,0:T(8,128)(2,1)S(1)}, bf16[288,128]{1,0:T(8,128)(2,1)S(1)}, u32[]{:S(2)}, u32[]{:S(2)}) collective-permute-start(bf16[288,128]{1,0:T(8,128)(2,1)S(1)} %get-tuple-element.69), channel_id=1, source_target_pairs={{0,16},{4,20},{8,24},{12,28},{16,0},{20,4},{24,8},{28,12},{1,17},{... | collective-permute-start | bytes 221192 | tf_op jit(solution)/shard_map/ppermute | solution.py:21
  26.9 1.3 %collective-permute-start.8 = (bf16[288,128]{1,0:T(8,128)(2,1)S(1)}, bf16[288,128]{1,0:T(8,128)(2,1)S(1)}, u32[]{:S(2)}, u32[]{:S(2)}) collective-permute-start(bf16[288,128]{1,0:T(8,128)(2,1)S(1)} %get-tuple-element.69), channel_id=1, source_target_pairs={{0,24},{4,28},{8,16},{12,20},{16,8},{20,12},{24,0},{28,4},{1,25},{... | collective-permute-start | bytes 221192 | tf_op jit(solution)/shard_map/ppermute | solution.py:21
  28.3 0.4 collective-permute-start.7
  28.7 0.5 %ends.1 = (f32[1,64]{1,0:T(1,128)}, f32[1,128]{1,0:T(1,128)S(1)}, f32[64,128]{1,0:T(8,128)S(1)}, f32[64,128]{1,0:T(8,128)S(1)}) custom-call(f32[16,128]{1,0:T(8,128)S(1)} %get-tuple-element.63.ends), custom_call_target="tpu_custom_call" | custom-call | flops 500000000 | tf_op jit(solution)/shard_map/ends/pallas_call | solution.py:384
  29.2 2.6 %collective-permute-done.9.refs_2_ = bf16[288,128]{1,0:T(8,128)(2,1)S(1)} collective-permute-done((bf16[288,128]{1,0:T(8,128)(2,1)S(1)}, bf16[288,128]{1,0:T(8,128)(2,1)S(1)}, u32[]{:S(2)}, u32[]{:S(2)}) %collective-permute-start.9) | collective-permute-done | bytes 73760 | tf_op jit(solution)/shard_map/ppermute | solution.py:21
  31.8 1.4 %collective-permute-done.8.refs_1_ = bf16[288,128]{1,0:T(8,128)(2,1)S(1)} collective-permute-done((bf16[288,128]{1,0:T(8,128)(2,1)S(1)}, bf16[288,128]{1,0:T(8,128)(2,1)S(1)}, u32[]{:S(2)}, u32[]{:S(2)}) %collective-permute-start.8) | collective-permute-done | bytes 73760 | tf_op jit(solution)/shard_map/ppermute | solution.py:21
  33.3 0.2 collective-permute-done.7.refs_0_
  33.4 0.1 back.1
  33.5 1.8 %collective-permute-start.10 = (bf16[256,128]{1,0:T(8,128)(2,1)S(1)}, bf16[256,128]{1,0:T(8,128)(2,1)S(1)}, u32[]{:S(2)}, u32[]{:S(2)}) collective-permute-start(bf16[256,128]{1,0:T(8,128)(2,1)S(1)} %get-tuple-element.75), channel_id=1, source_target_pairs={{0,4},{4,0},{8,12},{12,8},{16,20},{20,16},{24,28},{28,24},{1,5},{5... | collective-permute-start | bytes 196616 | tf_op jit(solution)/shard_map/ppermute | solution.py:21
  35.3 1.8 %levels.1 = (f32[32,128]{1,0:T(8,128)}, f32[16,4096]{1,0:T(8,128)}, f32[16,2048]{1,0:T(8,128)S(1)}) custom-call(f32[32,128]{1,0:T(8,128)S(1)} %get-tuple-element.65.own_second, f32[32,128]{1,0:T(8,128)S(1)} %get-tuple-element.66.other_second, f32[256,128]{1,0:T(8,128)S(1)} %get-tuple-element.70.earlier, f32[256,128]{1,0:T(8,128)S(1)} %get-tuple-element.67.own, ...), custom_call_target="tpu_custom_call" | custom-call | flops 1000000000 | tf_op jit(solution)/shard_map/levels/pallas_call | solution.py:384
  37.2 0.7 %collective-permute-done.10.received = bf16[256,128]{1,0:T(8,128)(2,1)S(1)} collective-permute-done((bf16[256,128]{1,0:T(8,128)(2,1)S(1)}, bf16[256,128]{1,0:T(8,128)(2,1)S(1)}, u32[]{:S(2)}, u32[]{:S(2)}) %collective-permute-start.10) | collective-permute-done | bytes 65568 | tf_op jit(solution)/shard_map/ppermute | solution.py:21
  37.8 0.7 %finish.1 = f32[16,4096]{1,0:T(8,128)} custom-call(bf16[256,128]{1,0:T(8,128)(2,1)S(1)} %collective-permute-done.10.received, f32[16,2048]{1,0:T(8,128)S(1)} %get-tuple-element.76.rest, f32[16,4096]{1,0:T(8,128)} %get-tuple-element.77.partly), custom_call_target="tpu_custom_call", output_to_operand_aliasing={{}: (2, {})} | custom-call | tf_op jit(solution)/shard_map/finish/pallas_call | solution.py:384
  (1 shorter events, 0.0 us)
Async XLA Ops:
  1.4 7.1 %collective-permute-start = (bf16[16,512]{1,0:T(8,128)(2,1)S(1)}, bf16[16,512]{1,0:T(8,128)(2,1)S(1)}, u32[]{:S(2)}, u32[]{:S(2)}) collective-permute-start(bf16[16,512]{1,0:T(8,128)(2,1)S(1)} %get-tuple-element.43.outer), channel_id=1, source_target_pairs={{0,1},{1,2},{2,0},{3,4},{4,3},{5,6},{6,5},{7,8},{8,7},{9,10},{10,9... | collective-permute-start | bytes 49160 | tf_op jit(solution)/shard_map/ppermute | solution.py:56
  1.9 6.6 %collective-permute-start.1 = (bf16[16,512]{1,0:T(8,128)(2,1)S(1)}, bf16[16,512]{1,0:T(8,128)(2,1)S(1)}, u32[]{:S(2)}, u32[]{:S(2)}) collective-permute-start(bf16[16,512]{1,0:T(8,128)(2,1)S(1)} %get-tuple-element.45), channel_id=1, source_target_pairs={{0,3},{1,2},{2,1},{3,0},{4,7},{5,6},{6,5},{7,4},{8,11},{9,10},{10,... | collective-permute-start | bytes 49160 | tf_op jit(solution)/shard_map/ppermute | solution.py:57
  5.6 2.9 %collective-permute-start.2 = (bf16[16,512]{1,0:T(8,128)(2,1)S(1)}, bf16[16,512]{1,0:T(8,128)(2,1)S(1)}, u32[]{:S(2)}, u32[]{:S(2)}) collective-permute-start(bf16[16,512]{1,0:T(8,128)(2,1)S(1)} %get-tuple-element.46), channel_id=1, source_target_pairs={{0,1},{1,0},{2,3},{3,2},{4,5},{5,4},{6,7},{7,6},{8,9},{9,8},{10,11... | collective-permute-start | bytes 49160 | tf_op jit(solution)/shard_map/ppermute | solution.py:21
  14.1 1.8 %collective-permute-start.3 = (bf16[64,1152]{1,0:T(8,128)(2,1)S(1)}, bf16[64,1152]{1,0:T(8,128)(2,1)S(1)}, u32[]{:S(2)}, u32[]{:S(2)}) collective-permute-start(bf16[64,1152]{1,0:T(8,128)(2,1)S(1)} %get-tuple-element.50.piece), channel_id=1, source_target_pairs={{0,1},{1,0},{2,3},{3,2},{4,5},{5,4},{6,7},{7,6},{8,9},{9,8},{10,11... | collective-permute-start | bytes 442376 | tf_op jit(solution)/shard_map/ppermute | solution.py:21
  17.1 5.9 %collective-permute-start.4 = (bf16[304,128]{1,0:T(8,128)(2,1)S(1)}, bf16[304,128]{1,0:T(8,128)(2,1)S(1)}, u32[]{:S(2)}, u32[]{:S(2)}) collective-permute-start(bf16[304,128]{1,0:T(8,128)(2,1)S(1)} %get-tuple-element.60), channel_id=1, source_target_pairs={{0,6},{1,7},{2,4},{3,5},{4,2},{5,3},{6,0},{7,1},{8,14},{9,15},{10,... | collective-permute-start | bytes 233480 | tf_op jit(solution)/shard_map/ppermute | solution.py:475
  18.7 4.6 %collective-permute-start.5 = (bf16[304,128]{1,0:T(8,128)(2,1)S(1)}, bf16[304,128]{1,0:T(8,128)(2,1)S(1)}, u32[]{:S(2)}, u32[]{:S(2)}) collective-permute-start(bf16[304,128]{1,0:T(8,128)(2,1)S(1)} %get-tuple-element.61), channel_id=1, source_target_pairs={{0,4},{1,5},{2,6},{3,7},{4,0},{5,1},{6,2},{7,3},{8,12},{9,13},{10,... | collective-permute-start | bytes 233480 | tf_op jit(solution)/shard_map/ppermute | solution.py:475
  19.3 4.9 %collective-permute-start.6 = (bf16[304,128]{1,0:T(8,128)(2,1)S(1)}, bf16[304,128]{1,0:T(8,128)(2,1)S(1)}, u32[]{:S(2)}, u32[]{:S(2)}) collective-permute-start(bf16[304,128]{1,0:T(8,128)(2,1)S(1)} %get-tuple-element.62), channel_id=1, source_target_pairs={{0,2},{1,3},{2,0},{3,1},{4,6},{5,7},{6,4},{7,5},{8,10},{9,11},{10,... | collective-permute-start | bytes 233480 | tf_op jit(solution)/shard_map/ppermute | solution.py:475
  24.3 7.5 %collective-permute-start.9 = (bf16[288,128]{1,0:T(8,128)(2,1)S(1)}, bf16[288,128]{1,0:T(8,128)(2,1)S(1)}, u32[]{:S(2)}, u32[]{:S(2)}) collective-permute-start(bf16[288,128]{1,0:T(8,128)(2,1)S(1)} %get-tuple-element.69), channel_id=1, source_target_pairs={{0,16},{4,20},{8,24},{12,28},{16,0},{20,4},{24,8},{28,12},{1,17},{... | collective-permute-start | bytes 221192 | tf_op jit(solution)/shard_map/ppermute | solution.py:21
  26.9 6.3 %collective-permute-start.8 = (bf16[288,128]{1,0:T(8,128)(2,1)S(1)}, bf16[288,128]{1,0:T(8,128)(2,1)S(1)}, u32[]{:S(2)}, u32[]{:S(2)}) collective-permute-start(bf16[288,128]{1,0:T(8,128)(2,1)S(1)} %get-tuple-element.69), channel_id=1, source_target_pairs={{0,24},{4,28},{8,16},{12,20},{16,8},{20,12},{24,0},{28,4},{1,25},{... | collective-permute-start | bytes 221192 | tf_op jit(solution)/shard_map/ppermute | solution.py:21
  28.3 5.1 %collective-permute-start.7 = (bf16[288,128]{1,0:T(8,128)(2,1)S(1)}, bf16[288,128]{1,0:T(8,128)(2,1)S(1)}, u32[]{:S(2)}, u32[]{:S(2)}) collective-permute-start(bf16[288,128]{1,0:T(8,128)(2,1)S(1)} %get-tuple-element.69), channel_id=1, source_target_pairs={{0,8},{4,12},{8,0},{12,4},{16,24},{20,28},{24,16},{28,20},{1,9},{5... | collective-permute-start | bytes 221192 | tf_op jit(solution)/shard_map/ppermute | solution.py:21
  33.5 4.3 %collective-permute-start.10 = (bf16[256,128]{1,0:T(8,128)(2,1)S(1)}, bf16[256,128]{1,0:T(8,128)(2,1)S(1)}, u32[]{:S(2)}, u32[]{:S(2)}) collective-permute-start(bf16[256,128]{1,0:T(8,128)(2,1)S(1)} %get-tuple-element.75), channel_id=1, source_target_pairs={{0,4},{4,0},{8,12},{12,8},{16,20},{20,16},{24,28},{28,24},{1,5},{5... | collective-permute-start | bytes 196616 | tf_op jit(solution)/shard_map/ppermute | solution.py:21

commit v9 on v8

--- a/solution.py
+++ b/solution.py
@@ -58,10 +58,12 @@
     return over, inside, exchanged(inner, "narrow", 1)
 
 
-def layer_rows(source, weights, bias, reach, start, size):
+def layer_rows(source, weights, bias, reach, start, size, arriving=None):
     windows = [source[8 + start + k * reach : 8 + start + k * reach + size, :] for k in (-1, 0, 1)]
     conv = bias
     for tap, window in enumerate(windows):
+        if arriving:
+            arriving[tap].wait()
         conv = conv + jnp.dot(window.astype(BF16), weights[tap], preferred_element_type=F32)
     half = 0.5 * conv
     return (windows[1] + (half + half * jnp.tanh(half))).astype(BF16)
@@ -72,7 +74,10 @@
     low = middle[0][0] - 2 * HALO
     high = sum(middle[-1])
     parts = [slice(low, high), slice(0, low), slice(high, length)]
-    pairs = [(rec_hbm.at[parts[0]], rec.at[parts[0]]), (weights_hbm.at[0], weights.at[0]), (bias_hbm, bias)]
+    taps = weights.shape[1]
+    pairs = [(rec_hbm.at[parts[0]], rec.at[parts[0]]), (bias_hbm, bias)]
+    pairs += [(weights_hbm.at[0, tap], weights.at[0, tap]) for tap in range(taps)]
+    early = len(pairs)
     pairs += [(rec_hbm.at[part], rec.at[part]) for part in parts[1:]]
     pairs += [(weights_hbm.at[layer], weights.at[layer]) for layer in range(1, weights.shape[0])]
     pairs += [(proj_hbm, proj)]
@@ -81,23 +86,24 @@
     def widen(part):
         padded[8 + HALO + part.start : 8 + HALO + part.stop, :] = rec[part, :].astype(F32)
 
-    for copy in copies[:3]:
+    for copy in copies[:early]:
         copy.start()
     copies[0].wait()
-    for copy in copies[3:]:
+    for copy in copies[early:]:
         copy.start()
     widen(parts[0])
     padded[: 8 + HALO, :] = jnp.zeros((8 + HALO, channels), F32)
     padded[8 + HALO + length :, :] = jnp.zeros((8 + HALO, channels), F32)
-    for copy in copies[1:3]:
+    copies[1].wait()
+    for at, (start, size) in enumerate(middle):
+        arriving = None if at else copies[2:early]
+        rows = layer_rows(padded, weights.at[0], bias[0:1, :], 1, start, size, arriving)
+        hidden[8 + start : 8 + start + size, :] = rows.astype(F32)
+    for copy, part in zip(copies[early:], parts[1:]):
         copy.wait()
-    for start, size in middle:
-        rows = layer_rows(padded, weights.at[0], bias[0:1, :], 1, start, size)
-        hidden[8 + start : 8 + start + size, :] = rows.astype(F32)
-    for copy in copies[3:]:
+        widen(part)
+    for copy in copies[early + 2 :]:
         copy.wait()
-    for part in parts[1:]:
-        widen(part)
 
 
 def conv_kernel(
@@ -165,12 +171,12 @@
     row_count = 4 * lhs.shape[1] // width
     first_row = pl.multiple_of(owner * row_count, row_count)
     group = max(1, 16 // row_count)
-    span = 2 * LANES
-    sums = []
-    for h in range(2):
-        for lanes in [slice(at, at + span) for at in range(0, length, span)]:
-            own_lead = lead[pl.ds(first_row, row_count), lanes]
-            own_diff = diff[pl.ds(first_row, row_count), lanes]
+    span = 4 * LANES
+    sums = [None, None]
+    for lanes in [slice(at, at + span) for at in range(0, length, span)]:
+        own_lead = lead[pl.ds(first_row, row_count), lanes]
+        own_diff = diff[pl.ds(first_row, row_count), lanes]
+        for h in range(2):
             for at in range(0, width // 4, group):
                 terms = []
                 for g in range(group):
@@ -178,7 +184,8 @@
                     terms.append(diff[row, lanes] * own_lead + rest[row, lanes] * own_diff)
                 term = terms[0] if group == 1 else jnp.concatenate(terms, axis=0)
                 lhs[h, at * row_count : (at + group) * row_count, lanes] = term.astype(BF16)
-        sums.append(lax.dot_general(lhs[h], piece[:, :length], NT, preferred_element_type=F32))
+            part = lax.dot_general(lhs[h, :, lanes], piece[:, lanes], NT, preferred_element_type=F32)
+            sums[h] = part if sums[h] is None else sums[h] + part
     return jnp.concatenate(sums, axis=1)
 
 
@@ -224,7 +231,8 @@
     chip_second[...] = both_second
     chip_ends[...] = both_ends
     for target, before, message in zip(targets, sums, messages):
-        pack(message, before[...] + target_sum(target, piece, diff, lead, rest, lhs), both_second, both_ends)
+        total = before[...] + target_sum(target, piece, diff, lead, rest, lhs)
+        pack(message, total, both_second, None if target[0] else both_ends)
 
 
 def kept_kernel(piece, mate, total, path, diff, lead, rest, lhs):
@@ -415,7 +423,7 @@
         functools.partial(load_kernel, middle),
         "load",
         [buffer, buffer, ((layers - 1,) + conv_weight.shape[1:], BF16), (conv_bias.shape, F32), ((width, channels), BF16)],
-        scratch=[pltpu.VMEM(recording.shape, BF16), pltpu.SemaphoreType.DMA((5 + layers,))],
+        scratch=[pltpu.VMEM(recording.shape, BF16), pltpu.SemaphoreType.DMA((4 + taps + layers,))],
         in_specs=[HBM] * len(far),
         flops=10**9,
         moved=2 * sum(held.size for held in far),
@@ -464,7 +472,7 @@
     chip_second, chip_ends, *messages = call(
         functools.partial(mate_kernel, targets),
         "mate",
-        [folds, last] + [((count + width // 2 + ENDS, LANES), BF16)] * len(targets),
+        [folds, last] + [((count + width // 2 + (0 if across else ENDS), LANES), BF16) for across, _ in targets],
         scratch=scratch,
         flops=share * len(targets),
     )(mate, second, ends, *sums)

time: 38.9 us -> 38.7 us (level)
  no operation moved by 1% of the time
where the time goes in v9:
time: 38.7 us; the launch traced here: 38.4 us
  Pallas kernels  16.4 us (42%)
  starting transfers between devices  14.5 us (37%)
  waiting for transfers between devices  6.78 us (18%)
  between operations  0.73 us (2%)
    pallas_call x12, Pallas kernels, run(): pl.pallas_call(kernel, out_shape=tuple(shapes), in_specs=in_specs or [VME...  16.4 us
    ppermute x6, starting transfers between devices, exchanged(): return lax.ppermute(array, axis, [(i, i ^ distance) for i in range(size)])  6.75 us
    ppermute x6, waiting for transfers between devices, exchanged(): return lax.ppermute(array, axis, [(i, i ^ distance) for i in range(size)])  4.97 us
    ppermute x1, starting transfers between devices, edges_exchanged(): inside = lax.ppermute(again, 'narrow', list(inside.items()))  3.67 us
    ppermute x3, starting transfers between devices, per_device(): lax.ppermute(sent, WHOLE, [(i, i ^ flip) for i in range(size)])  3.55 us
    ppermute x3, waiting for transfers between devices, per_device(): lax.ppermute(sent, WHOLE, [(i, i ^ flip) for i in range(size)])  1.81 us
  transfers between devices with their start and end apart: 11, of which 7 were waited for; matrix products, arithmetic and copies ran while one was open for 0% of the time, Pallas kernels for 21%

profile of v9, /device:TPU:0, one launch (start us, length us, event | category | flops | bytes accessed | tf_op | source)
XLA Modules:
  0.0 38.4 jit_solution(9835933450917393476)
XLA Ops:
  0.6 0.8 %edges.1 = (bf16[16,512]{1,0:T(8,128)(2,1)S(1)}, bf16[16,512]{1,0:T(8,128)(2,1)S(1)}) custom-call(bf16[1024,512]{1,0:T(8,128)(2,1)} %rec.1), custom_call_target="tpu_custom_call" | custom-call | tf_op jit(solution)/shard_map/edges/pallas_call | solution.py:392
  1.4 0.5 %collective-permute-start = (bf16[16,512]{1,0:T(8,128)(2,1)S(1)}, bf16[16,512]{1,0:T(8,128)(2,1)S(1)}, u32[]{:S(2)}, u32[]{:S(2)}) collective-permute-start(bf16[16,512]{1,0:T(8,128)(2,1)S(1)} %get-tuple-element.43.outer), channel_id=1, source_target_pairs={{0,1},{1,2},{2,0},{3,4},{4,3},{5,6},{6,5},{7,8},{8,7},{9,10},{10,9... | collective-permute-start | bytes 49160 | tf_op jit(solution)/shard_map/ppermute | solution.py:56
  1.9 3.7 %collective-permute-start.1 = (bf16[16,512]{1,0:T(8,128)(2,1)S(1)}, bf16[16,512]{1,0:T(8,128)(2,1)S(1)}, u32[]{:S(2)}, u32[]{:S(2)}) collective-permute-start(bf16[16,512]{1,0:T(8,128)(2,1)S(1)} %get-tuple-element.45), channel_id=1, source_target_pairs={{0,3},{1,2},{2,1},{3,0},{4,7},{5,6},{6,5},{7,4},{8,11},{9,10},{10,... | collective-permute-start | bytes 49160 | tf_op jit(solution)/shard_map/ppermute | solution.py:57
  5.6 0.0 collective-permute-start.2
  5.6 2.8 %load.1 = (f32[1072,512]{1,0:T(8,128)S(1)}, f32[1072,512]{1,0:T(8,128)S(1)}, bf16[2,3,512,512]{3,2,1,0:T(8,128)(2,1)S(1)}, f32[3,512]{1,0:T(4,128)S(1)}, bf16[64,512]{1,0:T(8,128)(2,1)S(1)}) custom-call(bf16[1024,512]{1,0:T(8,128)(2,1)} %rec.1, bf16[3,3,512,512]{3,2,1,0:T(8,128)(2,1)} %weights_hbm.3, f32[3,512]{1,0:T(4,128)} %bias_hbm.1, bf16[64,512]{1,0:T(8,128)(2,1)} %bitcast.5), custom_call_target="tpu_custom_call" | custom-call | flops 1000000000 | bytes 5835776 | tf_op jit(solution)/shard_map/load/pallas_call | solution.py:392
  8.4 0.0 collective-permute-done.1.inside
  8.4 0.0 collective-permute-done.2.inner
  8.4 0.0 collective-permute-done.over
  8.4 5.6 %conv.1 = (bf16[64,1152]{1,0:T(8,128)(2,1)S(1)}, f32[1072,512]{1,0:T(8,128)S(1)}, f32[1072,512]{1,0:T(8,128)S(1)}) custom-call(f32[1072,512]{1,0:T(8,128)S(1)} %get-tuple-element.41._, f32[1072,512]{1,0:T(8,128)S(1)} %get-tuple-element.42.__, bf16[16,512]{1,0:T(8,128)(2,1)S(1)} %collective-permute-done.over, ...), custom_call_target="tpu_custom_call", output_to_operand_aliasing={{1}: (0, {}), {2}: (1, {})} | custom-call | flops 4831838208 | bytes 4718592 | tf_op jit(solution)/shard_map/conv/pallas_call | solution.py:392
  14.0 0.6 %collective-permute-start.3 = (bf16[64,1152]{1,0:T(8,128)(2,1)S(1)}, bf16[64,1152]{1,0:T(8,128)(2,1)S(1)}, u32[]{:S(2)}, u32[]{:S(2)}) collective-permute-start(bf16[64,1152]{1,0:T(8,128)(2,1)S(1)} %get-tuple-element.50.piece), channel_id=1, source_target_pairs={{0,1},{1,0},{2,3},{3,2},{4,5},{5,4},{6,7},{7,6},{8,9},{9,8},{10,11... | collective-permute-start | bytes 442376 | tf_op jit(solution)/shard_map/ppermute | solution.py:21
  14.6 1.2 %own.1 = (f32[32,128]{1,0:T(8,128)S(1)}, f32[16,128]{1,0:T(8,128)S(1)}, f32[256,128]{1,0:T(8,128)S(1)}, f32[256,128]{1,0:T(8,128)S(1)}, f32[256,128]{1,0:T(8,128)S(1)}) custom-call(bf16[64,1152]{1,0:T(8,128)(2,1)S(1)} %get-tuple-element.50.piece), custom_call_target="tpu_custom_call" | custom-call | flops 1500000000 | tf_op jit(solution)/shard_map/own/pallas_call | solution.py:392
  15.8 0.0 collective-permute-done.3.mate.piece
  15.8 1.2 %mate.1 = (f32[32,128]{1,0:T(8,128)S(1)}, f32[16,128]{1,0:T(8,128)S(1)}, bf16[288,128]{1,0:T(8,128)(2,1)S(1)}, bf16[288,128]{1,0:T(8,128)(2,1)S(1)}, bf16[304,128]{1,0:T(8,128)(2,1)S(1)}) custom-call(bf16[64,1152]{1,0:T(8,128)(2,1)S(1)} %collective-permute-done.3.mate.piece, f32[32,128]{1,0:T(8,128)S(1)} %get-tuple-element.53.second, ...), custom_call_target="tpu_custom_call" | custom-call | flops 1500000000 | tf_op jit(solution)/shard_map/mate/pallas_call | solution.py:392
  17.1 1.6 %collective-permute-start.4 = (bf16[288,128]{1,0:T(8,128)(2,1)S(1)}, bf16[288,128]{1,0:T(8,128)(2,1)S(1)}, u32[]{:S(2)}, u32[]{:S(2)}) collective-permute-start(bf16[288,128]{1,0:T(8,128)(2,1)S(1)} %get-tuple-element.60), channel_id=1, source_target_pairs={{0,6},{1,7},{2,4},{3,5},{4,2},{5,3},{6,0},{7,1},{8,14},{9,15},{10,... | collective-permute-start | bytes 221192 | tf_op jit(solution)/shard_map/ppermute | solution.py:483
  18.6 0.5 %collective-permute-start.5 = (bf16[288,128]{1,0:T(8,128)(2,1)S(1)}, bf16[288,128]{1,0:T(8,128)(2,1)S(1)}, u32[]{:S(2)}, u32[]{:S(2)}) collective-permute-start(bf16[288,128]{1,0:T(8,128)(2,1)S(1)} %get-tuple-element.61), channel_id=1, source_target_pairs={{0,4},{1,5},{2,6},{3,7},{4,0},{5,1},{6,2},{7,3},{8,12},{9,13},{10,... | collective-permute-start | bytes 221192 | tf_op jit(solution)/shard_map/ppermute | solution.py:483
  19.2 1.4 %collective-permute-start.6 = (bf16[304,128]{1,0:T(8,128)(2,1)S(1)}, bf16[304,128]{1,0:T(8,128)(2,1)S(1)}, u32[]{:S(2)}, u32[]{:S(2)}) collective-permute-start(bf16[304,128]{1,0:T(8,128)(2,1)S(1)} %get-tuple-element.62), channel_id=1, source_target_pairs={{0,2},{1,3},{2,0},{3,1},{4,6},{5,7},{6,4},{7,5},{8,10},{9,11},{10,... | collective-permute-start | bytes 233480 | tf_op jit(solution)/shard_map/ppermute | solution.py:483
  20.6 1.6 %kept.1 = (f32[256,128]{1,0:T(8,128)S(1)}, bf16[64,1024]{1,0:T(8,128)(2,1)}) custom-call(bf16[64,1152]{1,0:T(8,128)(2,1)S(1)} %get-tuple-element.50.piece, bf16[64,1152]{1,0:T(8,128)(2,1)S(1)} %collective-permute-done.3.mate.piece), custom_call_target="tpu_custom_call" | custom-call | flops 1000000000 | tf_op jit(solution)/shard_map/kept/pallas_call | solution.py:392
  22.2 0.6 %collective-permute-done.4.refs_0_ = bf16[288,128]{1,0:T(8,128)(2,1)S(1)} collective-permute-done((bf16[288,128]{1,0:T(8,128)(2,1)S(1)}, bf16[288,128]{1,0:T(8,128)(2,1)S(1)}, u32[]{:S(2)}, u32[]{:S(2)}) %collective-permute-start.4) | collective-permute-done | bytes 73760 | tf_op jit(solution)/shard_map/ppermute | solution.py:483
  22.8 0.3 collective-permute-done.5.refs_1_
  23.1 0.9 %collective-permute-done.6.refs_2_ = bf16[304,128]{1,0:T(8,128)(2,1)S(1)} collective-permute-done((bf16[304,128]{1,0:T(8,128)(2,1)S(1)}, bf16[304,128]{1,0:T(8,128)(2,1)S(1)}, u32[]{:S(2)}, u32[]{:S(2)}) %collective-permute-start.6) | collective-permute-done | bytes 77856 | tf_op jit(solution)/shard_map/ppermute | solution.py:483
  24.0 0.1 reduce.1
  24.1 2.7 %collective-permute-start.9 = (bf16[288,128]{1,0:T(8,128)(2,1)S(1)}, bf16[288,128]{1,0:T(8,128)(2,1)S(1)}, u32[]{:S(2)}, u32[]{:S(2)}) collective-permute-start(bf16[288,128]{1,0:T(8,128)(2,1)S(1)} %get-tuple-element.69), channel_id=1, source_target_pairs={{0,16},{4,20},{8,24},{12,28},{16,0},{20,4},{24,8},{28,12},{1,17},{... | collective-permute-start | bytes 221192 | tf_op jit(solution)/shard_map/ppermute | solution.py:21
  26.8 1.3 %collective-permute-start.8 = (bf16[288,128]{1,0:T(8,128)(2,1)S(1)}, bf16[288,128]{1,0:T(8,128)(2,1)S(1)}, u32[]{:S(2)}, u32[]{:S(2)}) collective-permute-start(bf16[288,128]{1,0:T(8,128)(2,1)S(1)} %get-tuple-element.69), channel_id=1, source_target_pairs={{0,24},{4,28},{8,16},{12,20},{16,8},{20,12},{24,0},{28,4},{1,25},{... | collective-permute-start | bytes 221192 | tf_op jit(solution)/shard_map/ppermute | solution.py:21
  28.2 0.4 collective-permute-start.7
  28.5 0.5 %ends.1 = (f32[1,64]{1,0:T(1,128)}, f32[1,128]{1,0:T(1,128)S(1)}, f32[64,128]{1,0:T(8,128)S(1)}, f32[64,128]{1,0:T(8,128)S(1)}) custom-call(f32[16,128]{1,0:T(8,128)S(1)} %get-tuple-element.63.ends), custom_call_target="tpu_custom_call" | custom-call | flops 500000000 | tf_op jit(solution)/shard_map/ends/pallas_call | solution.py:392
  29.0 2.5 %collective-permute-done.9.refs_2_ = bf16[288,128]{1,0:T(8,128)(2,1)S(1)} collective-permute-done((bf16[288,128]{1,0:T(8,128)(2,1)S(1)}, bf16[288,128]{1,0:T(8,128)(2,1)S(1)}, u32[]{:S(2)}, u32[]{:S(2)}) %collective-permute-start.9) | collective-permute-done | bytes 73760 | tf_op jit(solution)/shard_map/ppermute | solution.py:21
  31.6 1.6 %collective-permute-done.8.refs_1_ = bf16[288,128]{1,0:T(8,128)(2,1)S(1)} collective-permute-done((bf16[288,128]{1,0:T(8,128)(2,1)S(1)}, bf16[288,128]{1,0:T(8,128)(2,1)S(1)}, u32[]{:S(2)}, u32[]{:S(2)}) %collective-permute-start.8) | collective-permute-done | bytes 73760 | tf_op jit(solution)/shard_map/ppermute | solution.py:21
  33.1 0.2 collective-permute-done.7.refs_0_
  33.3 0.1 back.1
  33.4 1.8 %collective-permute-start.10 = (bf16[256,128]{1,0:T(8,128)(2,1)S(1)}, bf16[256,128]{1,0:T(8,128)(2,1)S(1)}, u32[]{:S(2)}, u32[]{:S(2)}) collective-permute-start(bf16[256,128]{1,0:T(8,128)(2,1)S(1)} %get-tuple-element.75), channel_id=1, source_target_pairs={{0,4},{4,0},{8,12},{12,8},{16,20},{20,16},{24,28},{28,24},{1,5},{5... | collective-permute-start | bytes 196616 | tf_op jit(solution)/shard_map/ppermute | solution.py:21
  35.2 1.8 %levels.1 = (f32[32,128]{1,0:T(8,128)}, f32[16,4096]{1,0:T(8,128)}, f32[16,2048]{1,0:T(8,128)S(1)}) custom-call(f32[32,128]{1,0:T(8,128)S(1)} %get-tuple-element.65.own_second, f32[32,128]{1,0:T(8,128)S(1)} %get-tuple-element.66.other_second, f32[256,128]{1,0:T(8,128)S(1)} %get-tuple-element.70.earlier, f32[256,128]{1,0:T(8,128)S(1)} %get-tuple-element.67.own, ...), custom_call_target="tpu_custom_call" | custom-call | flops 1000000000 | tf_op jit(solution)/shard_map/levels/pallas_call | solution.py:392
  37.0 0.7 %collective-permute-done.10.received = bf16[256,128]{1,0:T(8,128)(2,1)S(1)} collective-permute-done((bf16[256,128]{1,0:T(8,128)(2,1)S(1)}, bf16[256,128]{1,0:T(8,128)(2,1)S(1)}, u32[]{:S(2)}, u32[]{:S(2)}) %collective-permute-start.10) | collective-permute-done | bytes 65568 | tf_op jit(solution)/shard_map/ppermute | solution.py:21
  37.7 0.7 %finish.1 = f32[16,4096]{1,0:T(8,128)} custom-call(bf16[256,128]{1,0:T(8,128)(2,1)S(1)} %collective-permute-done.10.received, f32[16,2048]{1,0:T(8,128)S(1)} %get-tuple-element.76.rest, f32[16,4096]{1,0:T(8,128)} %get-tuple-element.77.partly), custom_call_target="tpu_custom_call", output_to_operand_aliasing={{}: (2, {})} | custom-call | tf_op jit(solution)/shard_map/finish/pallas_call | solution.py:392
  (1 shorter events, 0.0 us)
Async XLA Ops:
  1.4 7.0 %collective-permute-start = (bf16[16,512]{1,0:T(8,128)(2,1)S(1)}, bf16[16,512]{1,0:T(8,128)(2,1)S(1)}, u32[]{:S(2)}, u32[]{:S(2)}) collective-permute-start(bf16[16,512]{1,0:T(8,128)(2,1)S(1)} %get-tuple-element.43.outer), channel_id=1, source_target_pairs={{0,1},{1,2},{2,0},{3,4},{4,3},{5,6},{6,5},{7,8},{8,7},{9,10},{10,9... | collective-permute-start | bytes 49160 | tf_op jit(solution)/shard_map/ppermute | solution.py:56
  1.9 6.5 %collective-permute-start.1 = (bf16[16,512]{1,0:T(8,128)(2,1)S(1)}, bf16[16,512]{1,0:T(8,128)(2,1)S(1)}, u32[]{:S(2)}, u32[]{:S(2)}) collective-permute-start(bf16[16,512]{1,0:T(8,128)(2,1)S(1)} %get-tuple-element.45), channel_id=1, source_target_pairs={{0,3},{1,2},{2,1},{3,0},{4,7},{5,6},{6,5},{7,4},{8,11},{9,10},{10,... | collective-permute-start | bytes 49160 | tf_op jit(solution)/shard_map/ppermute | solution.py:57
  5.6 2.8 %collective-permute-start.2 = (bf16[16,512]{1,0:T(8,128)(2,1)S(1)}, bf16[16,512]{1,0:T(8,128)(2,1)S(1)}, u32[]{:S(2)}, u32[]{:S(2)}) collective-permute-start(bf16[16,512]{1,0:T(8,128)(2,1)S(1)} %get-tuple-element.46), channel_id=1, source_target_pairs={{0,1},{1,0},{2,3},{3,2},{4,5},{5,4},{6,7},{7,6},{8,9},{9,8},{10,11... | collective-permute-start | bytes 49160 | tf_op jit(solution)/shard_map/ppermute | solution.py:21
  14.0 1.8 %collective-permute-start.3 = (bf16[64,1152]{1,0:T(8,128)(2,1)S(1)}, bf16[64,1152]{1,0:T(8,128)(2,1)S(1)}, u32[]{:S(2)}, u32[]{:S(2)}) collective-permute-start(bf16[64,1152]{1,0:T(8,128)(2,1)S(1)} %get-tuple-element.50.piece), channel_id=1, source_target_pairs={{0,1},{1,0},{2,3},{3,2},{4,5},{5,4},{6,7},{7,6},{8,9},{9,8},{10,11... | collective-permute-start | bytes 442376 | tf_op jit(solution)/shard_map/ppermute | solution.py:21
  17.1 5.7 %collective-permute-start.4 = (bf16[288,128]{1,0:T(8,128)(2,1)S(1)}, bf16[288,128]{1,0:T(8,128)(2,1)S(1)}, u32[]{:S(2)}, u32[]{:S(2)}) collective-permute-start(bf16[288,128]{1,0:T(8,128)(2,1)S(1)} %get-tuple-element.60), channel_id=1, source_target_pairs={{0,6},{1,7},{2,4},{3,5},{4,2},{5,3},{6,0},{7,1},{8,14},{9,15},{10,... | collective-permute-start | bytes 221192 | tf_op jit(solution)/shard_map/ppermute | solution.py:483
  18.6 4.4 %collective-permute-start.5 = (bf16[288,128]{1,0:T(8,128)(2,1)S(1)}, bf16[288,128]{1,0:T(8,128)(2,1)S(1)}, u32[]{:S(2)}, u32[]{:S(2)}) collective-permute-start(bf16[288,128]{1,0:T(8,128)(2,1)S(1)} %get-tuple-element.61), channel_id=1, source_target_pairs={{0,4},{1,5},{2,6},{3,7},{4,0},{5,1},{6,2},{7,3},{8,12},{9,13},{10,... | collective-permute-start | bytes 221192 | tf_op jit(solution)/shard_map/ppermute | solution.py:483
  19.2 4.8 %collective-permute-start.6 = (bf16[304,128]{1,0:T(8,128)(2,1)S(1)}, bf16[304,128]{1,0:T(8,128)(2,1)S(1)}, u32[]{:S(2)}, u32[]{:S(2)}) collective-permute-start(bf16[304,128]{1,0:T(8,128)(2,1)S(1)} %get-tuple-element.62), channel_id=1, source_target_pairs={{0,2},{1,3},{2,0},{3,1},{4,6},{5,7},{6,4},{7,5},{8,10},{9,11},{10,... | collective-permute-start | bytes 233480 | tf_op jit(solution)/shard_map/ppermute | solution.py:483
  24.1 7.4 %collective-permute-start.9 = (bf16[288,128]{1,0:T(8,128)(2,1)S(1)}, bf16[288,128]{1,0:T(8,128)(2,1)S(1)}, u32[]{:S(2)}, u32[]{:S(2)}) collective-permute-start(bf16[288,128]{1,0:T(8,128)(2,1)S(1)} %get-tuple-element.69), channel_id=1, source_target_pairs={{0,16},{4,20},{8,24},{12,28},{16,0},{20,4},{24,8},{28,12},{1,17},{... | collective-permute-start | bytes 221192 | tf_op jit(solution)/shard_map/ppermute | solution.py:21
  26.8 6.3 %collective-permute-start.8 = (bf16[288,128]{1,0:T(8,128)(2,1)S(1)}, bf16[288,128]{1,0:T(8,128)(2,1)S(1)}, u32[]{:S(2)}, u32[]{:S(2)}) collective-permute-start(bf16[288,128]{1,0:T(8,128)(2,1)S(1)} %get-tuple-element.69), channel_id=1, source_target_pairs={{0,24},{4,28},{8,16},{12,20},{16,8},{20,12},{24,0},{28,4},{1,25},{... | collective-permute-start | bytes 221192 | tf_op jit(solution)/shard_map/ppermute | solution.py:21
  28.2 5.1 %collective-permute-start.7 = (bf16[288,128]{1,0:T(8,128)(2,1)S(1)}, bf16[288,128]{1,0:T(8,128)(2,1)S(1)}, u32[]{:S(2)}, u32[]{:S(2)}) collective-permute-start(bf16[288,128]{1,0:T(8,128)(2,1)S(1)} %get-tuple-element.69), channel_id=1, source_target_pairs={{0,8},{4,12},{8,0},{12,4},{16,24},{20,28},{24,16},{28,20},{1,9},{5... | collective-permute-start | bytes 221192 | tf_op jit(solution)/shard_map/ppermute | solution.py:21
  33.4 4.3 %collective-permute-start.10 = (bf16[256,128]{1,0:T(8,128)(2,1)S(1)}, bf16[256,128]{1,0:T(8,128)(2,1)S(1)}, u32[]{:S(2)}, u32[]{:S(2)}) collective-permute-start(bf16[256,128]{1,0:T(8,128)(2,1)S(1)} %get-tuple-element.75), channel_id=1, source_target_pairs={{0,4},{4,0},{8,12},{12,8},{16,20},{20,16},{24,28},{28,24},{1,5},{5... | collective-permute-start | bytes 196616 | tf_op jit(solution)/shard_map/ppermute | solution.py:21

commit v10 on v9

--- a/solution.py
+++ b/solution.py
@@ -62,8 +62,8 @@
     windows = [source[8 + start + k * reach : 8 + start + k * reach + size, :] for k in (-1, 0, 1)]
     conv = bias
     for tap, window in enumerate(windows):
-        if arriving:
-            arriving[tap].wait()
+        if arriving and tap:
+            arriving[tap - 1].wait()
         conv = conv + jnp.dot(window.astype(BF16), weights[tap], preferred_element_type=F32)
     half = 0.5 * conv
     return (windows[1] + (half + half * jnp.tanh(half))).astype(BF16)
@@ -89,14 +89,17 @@
     for copy in copies[:early]:
         copy.start()
     copies[0].wait()
-    for copy in copies[early:]:
+    for copy in copies[early : early + 2]:
         copy.start()
     widen(parts[0])
     padded[: 8 + HALO, :] = jnp.zeros((8 + HALO, channels), F32)
     padded[8 + HALO + length :, :] = jnp.zeros((8 + HALO, channels), F32)
     copies[1].wait()
+    copies[2].wait()
+    for copy in copies[early + 2 :]:
+        copy.start()
     for at, (start, size) in enumerate(middle):
-        arriving = None if at else copies[2:early]
+        arriving = None if at else copies[3:early]
         rows = layer_rows(padded, weights.at[0], bias[0:1, :], 1, start, size, arriving)
         hidden[8 + start : 8 + start + size, :] = rows.astype(F32)
     for copy, part in zip(copies[early:], parts[1:]):

time: 38.7 us -> 38.7 us (level)
  no operation moved by 1% of the time
where the time goes in v10:
time: 38.7 us; the launch traced here: 38.4 us
  Pallas kernels  16.4 us (42%)
  starting transfers between devices  14.5 us (37%)
  waiting for transfers between devices  6.83 us (18%)
  between operations  0.73 us (2%)
    pallas_call x12, Pallas kernels, run(): pl.pallas_call(kernel, out_shape=tuple(shapes), in_specs=in_specs or [VME...  16.4 us
    ppermute x6, starting transfers between devices, exchanged(): return lax.ppermute(array, axis, [(i, i ^ distance) for i in range(size)])  6.73 us
    ppermute x6, waiting for transfers between devices, exchanged(): return lax.ppermute(array, axis, [(i, i ^ distance) for i in range(size)])  5.01 us
    ppermute x1, starting transfers between devices, edges_exchanged(): inside = lax.ppermute(again, 'narrow', list(inside.items()))  3.67 us
    ppermute x3, starting transfers between devices, per_device(): lax.ppermute(sent, WHOLE, [(i, i ^ flip) for i in range(size)])  3.55 us
    ppermute x3, waiting for transfers between devices, per_device(): lax.ppermute(sent, WHOLE, [(i, i ^ flip) for i in range(size)])  1.82 us
  transfers between devices with their start and end apart: 11, of which 7 were waited for; matrix products, arithmetic and copies ran while one was open for 0% of the time, Pallas kernels for 21%

profile of v10, /device:TPU:0, one launch (start us, length us, event | category | flops | bytes accessed | tf_op | source)
XLA Modules:
  0.0 38.4 jit_solution(9363869822572708824)
XLA Ops:
  0.6 0.8 %edges.1 = (bf16[16,512]{1,0:T(8,128)(2,1)S(1)}, bf16[16,512]{1,0:T(8,128)(2,1)S(1)}) custom-call(bf16[1024,512]{1,0:T(8,128)(2,1)} %rec.1), custom_call_target="tpu_custom_call" | custom-call | tf_op jit(solution)/shard_map/edges/pallas_call | solution.py:395
  1.4 0.5 %collective-permute-start = (bf16[16,512]{1,0:T(8,128)(2,1)S(1)}, bf16[16,512]{1,0:T(8,128)(2,1)S(1)}, u32[]{:S(2)}, u32[]{:S(2)}) collective-permute-start(bf16[16,512]{1,0:T(8,128)(2,1)S(1)} %get-tuple-element.43.outer), channel_id=1, source_target_pairs={{0,1},{1,2},{2,0},{3,4},{4,3},{5,6},{6,5},{7,8},{8,7},{9,10},{10,9... | collective-permute-start | bytes 49160 | tf_op jit(solution)/shard_map/ppermute | solution.py:56
  1.9 3.7 %collective-permute-start.1 = (bf16[16,512]{1,0:T(8,128)(2,1)S(1)}, bf16[16,512]{1,0:T(8,128)(2,1)S(1)}, u32[]{:S(2)}, u32[]{:S(2)}) collective-permute-start(bf16[16,512]{1,0:T(8,128)(2,1)S(1)} %get-tuple-element.45), channel_id=1, source_target_pairs={{0,3},{1,2},{2,1},{3,0},{4,7},{5,6},{6,5},{7,4},{8,11},{9,10},{10,... | collective-permute-start | bytes 49160 | tf_op jit(solution)/shard_map/ppermute | solution.py:57
  5.6 0.0 collective-permute-start.2
  5.6 2.8 %load.1 = (f32[1072,512]{1,0:T(8,128)S(1)}, f32[1072,512]{1,0:T(8,128)S(1)}, bf16[2,3,512,512]{3,2,1,0:T(8,128)(2,1)S(1)}, f32[3,512]{1,0:T(4,128)S(1)}, bf16[64,512]{1,0:T(8,128)(2,1)S(1)}) custom-call(bf16[1024,512]{1,0:T(8,128)(2,1)} %rec.1, bf16[3,3,512,512]{3,2,1,0:T(8,128)(2,1)} %weights_hbm.3, f32[3,512]{1,0:T(4,128)} %bias_hbm.1, bf16[64,512]{1,0:T(8,128)(2,1)} %bitcast.5), custom_call_target="tpu_custom_call" | custom-call | flops 1000000000 | bytes 5835776 | tf_op jit(solution)/shard_map/load/pallas_call | solution.py:395
  8.4 0.0 collective-permute-done.1.inside
  8.4 0.0 collective-permute-done.2.inner
  8.4 0.0 collective-permute-done.over
  8.4 5.6 %conv.1 = (bf16[64,1152]{1,0:T(8,128)(2,1)S(1)}, f32[1072,512]{1,0:T(8,128)S(1)}, f32[1072,512]{1,0:T(8,128)S(1)}) custom-call(f32[1072,512]{1,0:T(8,128)S(1)} %get-tuple-element.41._, f32[1072,512]{1,0:T(8,128)S(1)} %get-tuple-element.42.__, bf16[16,512]{1,0:T(8,128)(2,1)S(1)} %collective-permute-done.over, ...), custom_call_target="tpu_custom_call", output_to_operand_aliasing={{1}: (0, {}), {2}: (1, {})} | custom-call | flops 4831838208 | bytes 4718592 | tf_op jit(solution)/shard_map/conv/pallas_call | solution.py:395
  14.0 0.6 %collective-permute-start.3 = (bf16[64,1152]{1,0:T(8,128)(2,1)S(1)}, bf16[64,1152]{1,0:T(8,128)(2,1)S(1)}, u32[]{:S(2)}, u32[]{:S(2)}) collective-permute-start(bf16[64,1152]{1,0:T(8,128)(2,1)S(1)} %get-tuple-element.50.piece), channel_id=1, source_target_pairs={{0,1},{1,0},{2,3},{3,2},{4,5},{5,4},{6,7},{7,6},{8,9},{9,8},{10,11... | collective-permute-start | bytes 442376 | tf_op jit(solution)/shard_map/ppermute | solution.py:21
  14.6 1.2 %own.1 = (f32[32,128]{1,0:T(8,128)S(1)}, f32[16,128]{1,0:T(8,128)S(1)}, f32[256,128]{1,0:T(8,128)S(1)}, f32[256,128]{1,0:T(8,128)S(1)}, f32[256,128]{1,0:T(8,128)S(1)}) custom-call(bf16[64,1152]{1,0:T(8,128)(2,1)S(1)} %get-tuple-element.50.piece), custom_call_target="tpu_custom_call" | custom-call | flops 1500000000 | tf_op jit(solution)/shard_map/own/pallas_call | solution.py:395
  15.8 0.0 collective-permute-done.3.mate.piece
  15.8 1.2 %mate.1 = (f32[32,128]{1,0:T(8,128)S(1)}, f32[16,128]{1,0:T(8,128)S(1)}, bf16[288,128]{1,0:T(8,128)(2,1)S(1)}, bf16[288,128]{1,0:T(8,128)(2,1)S(1)}, bf16[304,128]{1,0:T(8,128)(2,1)S(1)}) custom-call(bf16[64,1152]{1,0:T(8,128)(2,1)S(1)} %collective-permute-done.3.mate.piece, f32[32,128]{1,0:T(8,128)S(1)} %get-tuple-element.53.second, ...), custom_call_target="tpu_custom_call" | custom-call | flops 1500000000 | tf_op jit(solution)/shard_map/mate/pallas_call | solution.py:395
  17.1 1.6 %collective-permute-start.4 = (bf16[288,128]{1,0:T(8,128)(2,1)S(1)}, bf16[288,128]{1,0:T(8,128)(2,1)S(1)}, u32[]{:S(2)}, u32[]{:S(2)}) collective-permute-start(bf16[288,128]{1,0:T(8,128)(2,1)S(1)} %get-tuple-element.60), channel_id=1, source_target_pairs={{0,6},{1,7},{2,4},{3,5},{4,2},{5,3},{6,0},{7,1},{8,14},{9,15},{10,... | collective-permute-start | bytes 221192 | tf_op jit(solution)/shard_map/ppermute | solution.py:486
  18.7 0.5 %collective-permute-start.5 = (bf16[288,128]{1,0:T(8,128)(2,1)S(1)}, bf16[288,128]{1,0:T(8,128)(2,1)S(1)}, u32[]{:S(2)}, u32[]{:S(2)}) collective-permute-start(bf16[288,128]{1,0:T(8,128)(2,1)S(1)} %get-tuple-element.61), channel_id=1, source_target_pairs={{0,4},{1,5},{2,6},{3,7},{4,0},{5,1},{6,2},{7,3},{8,12},{9,13},{10,... | collective-permute-start | bytes 221192 | tf_op jit(solution)/shard_map/ppermute | solution.py:486
  19.2 1.4 %collective-permute-start.6 = (bf16[304,128]{1,0:T(8,128)(2,1)S(1)}, bf16[304,128]{1,0:T(8,128)(2,1)S(1)}, u32[]{:S(2)}, u32[]{:S(2)}) collective-permute-start(bf16[304,128]{1,0:T(8,128)(2,1)S(1)} %get-tuple-element.62), channel_id=1, source_target_pairs={{0,2},{1,3},{2,0},{3,1},{4,6},{5,7},{6,4},{7,5},{8,10},{9,11},{10,... | collective-permute-start | bytes 233480 | tf_op jit(solution)/shard_map/ppermute | solution.py:486
  20.6 1.6 %kept.1 = (f32[256,128]{1,0:T(8,128)S(1)}, bf16[64,1024]{1,0:T(8,128)(2,1)}) custom-call(bf16[64,1152]{1,0:T(8,128)(2,1)S(1)} %get-tuple-element.50.piece, bf16[64,1152]{1,0:T(8,128)(2,1)S(1)} %collective-permute-done.3.mate.piece), custom_call_target="tpu_custom_call" | custom-call | flops 1000000000 | tf_op jit(solution)/shard_map/kept/pallas_call | solution.py:395
  22.2 0.6 %collective-permute-done.4.refs_0_ = bf16[288,128]{1,0:T(8,128)(2,1)S(1)} collective-permute-done((bf16[288,128]{1,0:T(8,128)(2,1)S(1)}, bf16[288,128]{1,0:T(8,128)(2,1)S(1)}, u32[]{:S(2)}, u32[]{:S(2)}) %collective-permute-start.4) | collective-permute-done | bytes 73760 | tf_op jit(solution)/shard_map/ppermute | solution.py:486
  22.8 0.3 collective-permute-done.5.refs_1_
  23.1 0.9 %collective-permute-done.6.refs_2_ = bf16[304,128]{1,0:T(8,128)(2,1)S(1)} collective-permute-done((bf16[304,128]{1,0:T(8,128)(2,1)S(1)}, bf16[304,128]{1,0:T(8,128)(2,1)S(1)}, u32[]{:S(2)}, u32[]{:S(2)}) %collective-permute-start.6) | collective-permute-done | bytes 77856 | tf_op jit(solution)/shard_map/ppermute | solution.py:486
  24.0 0.1 reduce.1
  24.1 2.7 %collective-permute-start.9 = (bf16[288,128]{1,0:T(8,128)(2,1)S(1)}, bf16[288,128]{1,0:T(8,128)(2,1)S(1)}, u32[]{:S(2)}, u32[]{:S(2)}) collective-permute-start(bf16[288,128]{1,0:T(8,128)(2,1)S(1)} %get-tuple-element.69), channel_id=1, source_target_pairs={{0,16},{4,20},{8,24},{12,28},{16,0},{20,4},{24,8},{28,12},{1,17},{... | collective-permute-start | bytes 221192 | tf_op jit(solution)/shard_map/ppermute | solution.py:21
  26.8 1.4 %collective-permute-start.8 = (bf16[288,128]{1,0:T(8,128)(2,1)S(1)}, bf16[288,128]{1,0:T(8,128)(2,1)S(1)}, u32[]{:S(2)}, u32[]{:S(2)}) collective-permute-start(bf16[288,128]{1,0:T(8,128)(2,1)S(1)} %get-tuple-element.69), channel_id=1, source_target_pairs={{0,24},{4,28},{8,16},{12,20},{16,8},{20,12},{24,0},{28,4},{1,25},{... | collective-permute-start | bytes 221192 | tf_op jit(solution)/shard_map/ppermute | solution.py:21
  28.2 0.3 collective-permute-start.7
  28.5 0.5 %ends.1 = (f32[1,64]{1,0:T(1,128)}, f32[1,128]{1,0:T(1,128)S(1)}, f32[64,128]{1,0:T(8,128)S(1)}, f32[64,128]{1,0:T(8,128)S(1)}) custom-call(f32[16,128]{1,0:T(8,128)S(1)} %get-tuple-element.63.ends), custom_call_target="tpu_custom_call" | custom-call | flops 500000000 | tf_op jit(solution)/shard_map/ends/pallas_call | solution.py:395
  29.0 2.5 %collective-permute-done.9.refs_2_ = bf16[288,128]{1,0:T(8,128)(2,1)S(1)} collective-permute-done((bf16[288,128]{1,0:T(8,128)(2,1)S(1)}, bf16[288,128]{1,0:T(8,128)(2,1)S(1)}, u32[]{:S(2)}, u32[]{:S(2)}) %collective-permute-start.9) | collective-permute-done | bytes 73760 | tf_op jit(solution)/shard_map/ppermute | solution.py:21
  31.6 1.6 %collective-permute-done.8.refs_1_ = bf16[288,128]{1,0:T(8,128)(2,1)S(1)} collective-permute-done((bf16[288,128]{1,0:T(8,128)(2,1)S(1)}, bf16[288,128]{1,0:T(8,128)(2,1)S(1)}, u32[]{:S(2)}, u32[]{:S(2)}) %collective-permute-start.8) | collective-permute-done | bytes 73760 | tf_op jit(solution)/shard_map/ppermute | solution.py:21
  33.1 0.2 collective-permute-done.7.refs_0_
  33.3 0.1 back.1
  33.4 1.8 %collective-permute-start.10 = (bf16[256,128]{1,0:T(8,128)(2,1)S(1)}, bf16[256,128]{1,0:T(8,128)(2,1)S(1)}, u32[]{:S(2)}, u32[]{:S(2)}) collective-permute-start(bf16[256,128]{1,0:T(8,128)(2,1)S(1)} %get-tuple-element.75), channel_id=1, source_target_pairs={{0,4},{4,0},{8,12},{12,8},{16,20},{20,16},{24,28},{28,24},{1,5},{5... | collective-permute-start | bytes 196616 | tf_op jit(solution)/shard_map/ppermute | solution.py:21
  35.2 1.8 %levels.1 = (f32[32,128]{1,0:T(8,128)}, f32[16,4096]{1,0:T(8,128)}, f32[16,2048]{1,0:T(8,128)S(1)}) custom-call(f32[32,128]{1,0:T(8,128)S(1)} %get-tuple-element.65.own_second, f32[32,128]{1,0:T(8,128)S(1)} %get-tuple-element.66.other_second, f32[256,128]{1,0:T(8,128)S(1)} %get-tuple-element.70.earlier, f32[256,128]{1,0:T(8,128)S(1)} %get-tuple-element.67.own, ...), custom_call_target="tpu_custom_call" | custom-call | flops 1000000000 | tf_op jit(solution)/shard_map/levels/pallas_call | solution.py:395
  37.0 0.7 %collective-permute-done.10.received = bf16[256,128]{1,0:T(8,128)(2,1)S(1)} collective-permute-done((bf16[256,128]{1,0:T(8,128)(2,1)S(1)}, bf16[256,128]{1,0:T(8,128)(2,1)S(1)}, u32[]{:S(2)}, u32[]{:S(2)}) %collective-permute-start.10) | collective-permute-done | bytes 65568 | tf_op jit(solution)/shard_map/ppermute | solution.py:21
  37.7 0.7 %finish.1 = f32[16,4096]{1,0:T(8,128)} custom-call(bf16[256,128]{1,0:T(8,128)(2,1)S(1)} %collective-permute-done.10.received, f32[16,2048]{1,0:T(8,128)S(1)} %get-tuple-element.76.rest, f32[16,4096]{1,0:T(8,128)} %get-tuple-element.77.partly), custom_call_target="tpu_custom_call", output_to_operand_aliasing={{}: (2, {})} | custom-call | tf_op jit(solution)/shard_map/finish/pallas_call | solution.py:395
  (1 shorter events, 0.0 us)
Async XLA Ops:
  1.4 7.0 %collective-permute-start = (bf16[16,512]{1,0:T(8,128)(2,1)S(1)}, bf16[16,512]{1,0:T(8,128)(2,1)S(1)}, u32[]{:S(2)}, u32[]{:S(2)}) collective-permute-start(bf16[16,512]{1,0:T(8,128)(2,1)S(1)} %get-tuple-element.43.outer), channel_id=1, source_target_pairs={{0,1},{1,2},{2,0},{3,4},{4,3},{5,6},{6,5},{7,8},{8,7},{9,10},{10,9... | collective-permute-start | bytes 49160 | tf_op jit(solution)/shard_map/ppermute | solution.py:56
  1.9 6.5 %collective-permute-start.1 = (bf16[16,512]{1,0:T(8,128)(2,1)S(1)}, bf16[16,512]{1,0:T(8,128)(2,1)S(1)}, u32[]{:S(2)}, u32[]{:S(2)}) collective-permute-start(bf16[16,512]{1,0:T(8,128)(2,1)S(1)} %get-tuple-element.45), channel_id=1, source_target_pairs={{0,3},{1,2},{2,1},{3,0},{4,7},{5,6},{6,5},{7,4},{8,11},{9,10},{10,... | collective-permute-start | bytes 49160 | tf_op jit(solution)/shard_map/ppermute | solution.py:57
  5.6 2.9 %collective-permute-start.2 = (bf16[16,512]{1,0:T(8,128)(2,1)S(1)}, bf16[16,512]{1,0:T(8,128)(2,1)S(1)}, u32[]{:S(2)}, u32[]{:S(2)}) collective-permute-start(bf16[16,512]{1,0:T(8,128)(2,1)S(1)} %get-tuple-element.46), channel_id=1, source_target_pairs={{0,1},{1,0},{2,3},{3,2},{4,5},{5,4},{6,7},{7,6},{8,9},{9,8},{10,11... | collective-permute-start | bytes 49160 | tf_op jit(solution)/shard_map/ppermute | solution.py:21
  14.0 1.8 %collective-permute-start.3 = (bf16[64,1152]{1,0:T(8,128)(2,1)S(1)}, bf16[64,1152]{1,0:T(8,128)(2,1)S(1)}, u32[]{:S(2)}, u32[]{:S(2)}) collective-permute-start(bf16[64,1152]{1,0:T(8,128)(2,1)S(1)} %get-tuple-element.50.piece), channel_id=1, source_target_pairs={{0,1},{1,0},{2,3},{3,2},{4,5},{5,4},{6,7},{7,6},{8,9},{9,8},{10,11... | collective-permute-start | bytes 442376 | tf_op jit(solution)/shard_map/ppermute | solution.py:21
  17.1 5.8 %collective-permute-start.4 = (bf16[288,128]{1,0:T(8,128)(2,1)S(1)}, bf16[288,128]{1,0:T(8,128)(2,1)S(1)}, u32[]{:S(2)}, u32[]{:S(2)}) collective-permute-start(bf16[288,128]{1,0:T(8,128)(2,1)S(1)} %get-tuple-element.60), channel_id=1, source_target_pairs={{0,6},{1,7},{2,4},{3,5},{4,2},{5,3},{6,0},{7,1},{8,14},{9,15},{10,... | collective-permute-start | bytes 221192 | tf_op jit(solution)/shard_map/ppermute | solution.py:486
  18.7 4.4 %collective-permute-start.5 = (bf16[288,128]{1,0:T(8,128)(2,1)S(1)}, bf16[288,128]{1,0:T(8,128)(2,1)S(1)}, u32[]{:S(2)}, u32[]{:S(2)}) collective-permute-start(bf16[288,128]{1,0:T(8,128)(2,1)S(1)} %get-tuple-element.61), channel_id=1, source_target_pairs={{0,4},{1,5},{2,6},{3,7},{4,0},{5,1},{6,2},{7,3},{8,12},{9,13},{10,... | collective-permute-start | bytes 221192 | tf_op jit(solution)/shard_map/ppermute | solution.py:486
  19.2 4.8 %collective-permute-start.6 = (bf16[304,128]{1,0:T(8,128)(2,1)S(1)}, bf16[304,128]{1,0:T(8,128)(2,1)S(1)}, u32[]{:S(2)}, u32[]{:S(2)}) collective-permute-start(bf16[304,128]{1,0:T(8,128)(2,1)S(1)} %get-tuple-element.62), channel_id=1, source_target_pairs={{0,2},{1,3},{2,0},{3,1},{4,6},{5,7},{6,4},{7,5},{8,10},{9,11},{10,... | collective-permute-start | bytes 233480 | tf_op jit(solution)/shard_map/ppermute | solution.py:486
  24.1 7.4 %collective-permute-start.9 = (bf16[288,128]{1,0:T(8,128)(2,1)S(1)}, bf16[288,128]{1,0:T(8,128)(2,1)S(1)}, u32[]{:S(2)}, u32[]{:S(2)}) collective-permute-start(bf16[288,128]{1,0:T(8,128)(2,1)S(1)} %get-tuple-element.69), channel_id=1, source_target_pairs={{0,16},{4,20},{8,24},{12,28},{16,0},{20,4},{24,8},{28,12},{1,17},{... | collective-permute-start | bytes 221192 | tf_op jit(solution)/shard_map/ppermute | solution.py:21
  26.8 6.3 %collective-permute-start.8 = (bf16[288,128]{1,0:T(8,128)(2,1)S(1)}, bf16[288,128]{1,0:T(8,128)(2,1)S(1)}, u32[]{:S(2)}, u32[]{:S(2)}) collective-permute-start(bf16[288,128]{1,0:T(8,128)(2,1)S(1)} %get-tuple-element.69), channel_id=1, source_target_pairs={{0,24},{4,28},{8,16},{12,20},{16,8},{20,12},{24,0},{28,4},{1,25},{... | collective-permute-start | bytes 221192 | tf_op jit(solution)/shard_map/ppermute | solution.py:21
  28.2 5.1 %collective-permute-start.7 = (bf16[288,128]{1,0:T(8,128)(2,1)S(1)}, bf16[288,128]{1,0:T(8,128)(2,1)S(1)}, u32[]{:S(2)}, u32[]{:S(2)}) collective-permute-start(bf16[288,128]{1,0:T(8,128)(2,1)S(1)} %get-tuple-element.69), channel_id=1, source_target_pairs={{0,8},{4,12},{8,0},{12,4},{16,24},{20,28},{24,16},{28,20},{1,9},{5... | collective-permute-start | bytes 221192 | tf_op jit(solution)/shard_map/ppermute | solution.py:21
  33.4 4.3 %collective-permute-start.10 = (bf16[256,128]{1,0:T(8,128)(2,1)S(1)}, bf16[256,128]{1,0:T(8,128)(2,1)S(1)}, u32[]{:S(2)}, u32[]{:S(2)}) collective-permute-start(bf16[256,128]{1,0:T(8,128)(2,1)S(1)} %get-tuple-element.75), channel_id=1, source_target_pairs={{0,4},{4,0},{8,12},{12,8},{16,20},{20,16},{24,28},{28,24},{1,5},{5... | collective-permute-start | bytes 196616 | tf_op jit(solution)/shard_map/ppermute | solution.py:21
